TPU v7x, 32 devices: a whole 2x2x4 slice. The times are simulated.
32 devices in a mesh: crop: 4 (over y, x), slab: 8 (over z, core).
Axes of the slice: x: 2, y: 2, z: 4, core: 2. Of those that a mesh axis runs over, the one named last changes fastest.
Arguments:
- patches: bfloat16 [8, 8, 64, 16384], P('crop', 'slab'), may hold values from -6 to 6
- modality: int32 [8], P('crop'), may hold values from 0 to 1
- skip_feats: bfloat16 [8, 16, 16, 16, 128], P('crop', 'slab'), may hold values from -7.5 to 7.5
- cotangent: bfloat16 [8, 16, 16, 16, 128], P('crop', 'slab'), may hold values from -7.5 to 7.5
- embedding: float32 [20480, 768], P('slab', 'crop'), may hold values from -0.0625 to 0.0625
- attention_in: float32 [768, 2304], P('slab', 'crop'), may hold values from -0.3125 to 0.3125
- attention_out: float32 [768, 768], P('slab', 'crop'), may hold values from -0.625 to 0.625
- expand_up: float32 [768, 3072], P('slab', 'crop'), may hold values from -0.21875 to 0.21875
- expand_down: float32 [3072, 768], P('slab', 'crop'), may hold values from -0.109375 to 0.109375
- upsample: float32 [768, 1024], P('slab', 'crop'), may hold values from -0.3247595 to 0.3247595
- convolve_one: float32 [6912, 128], P('slab', 'crop'), may hold values from -0.078125 to 0.078125
- convolve_two: float32 [3456, 128], P('slab', 'crop'), may hold values from -0.109375 to 0.109375
- positions: float32 [512, 768], P('slab', 'crop'), may hold values from -0.48 to 0.48
- vectors: float32 [9216], P(('crop', 'slab')), may hold values from -1.5 to 1.5
- embedding_mean: float32 [20480, 768], P('slab', 'crop'), may hold values from -0.00012207031 to 0.00012207031
- attention_in_mean: float32 [768, 2304], P('slab', 'crop'), may hold values from -0.00012207031 to 0.00012207031
- attention_out_mean: float32 [768, 768], P('slab', 'crop'), may hold values from -0.00012207031 to 0.00012207031
- expand_up_mean: float32 [768, 3072], P('slab', 'crop'), may hold values from -0.00012207031 to 0.00012207031
- expand_down_mean: float32 [3072, 768], P('slab', 'crop'), may hold values from -0.00012207031 to 0.00012207031
- upsample_mean: float32 [768, 1024], P('slab', 'crop'), may hold values from -0.00012207031 to 0.00012207031
- convolve_one_mean: float32 [6912, 128], P('slab', 'crop'), may hold values from -0.00012207031 to 0.00012207031
- convolve_two_mean: float32 [3456, 128], P('slab', 'crop'), may hold values from -0.00012207031 to 0.00012207031
- positions_mean: float32 [512, 768], P('slab', 'crop'), may hold values from -7.6293945e-06 to 7.6293945e-06
- vectors_mean: float32 [9216], P(('crop', 'slab')), may hold values from -0.00061035156 to 0.00061035156
- embedding_square: float32 [20480, 768], P('slab', 'crop'), may hold values from 2.0772044e-09 to 8.293021e-09
- attention_in_square: float32 [768, 2304], P('slab', 'crop'), may hold values from 2.0772044e-09 to 8.293021e-09
- attention_out_square: float32 [768, 768], P('slab', 'crop'), may hold values from 2.0772044e-09 to 8.293021e-09
- expand_up_square: float32 [768, 3072], P('slab', 'crop'), may hold values from 2.0772044e-09 to 8.293021e-09
- expand_down_square: float32 [3072, 768], P('slab', 'crop'), may hold values from 2.0772044e-09 to 8.293021e-09
- upsample_square: float32 [768, 1024], P('slab', 'crop'), may hold values from 2.0772044e-09 to 8.293021e-09
- convolve_one_square: float32 [6912, 128], P('slab', 'crop'), may hold values from 2.0772044e-09 to 8.293021e-09
- convolve_two_square: float32 [3456, 128], P('slab', 'crop'), may hold values from 2.0772044e-09 to 8.293021e-09
- positions_square: float32 [512, 768], P('slab', 'crop'), may hold values from 6.864573e-12 to 2.7381162e-11
- vectors_square: float32 [9216], P(('crop', 'slab')), may hold values from 5.2127564e-08 to 2.0772043e-07
Outputs:
- block_output: bfloat16 [8, 16, 16, 16, 128], P('crop', 'slab')
- patch_grad: bfloat16 [8, 8, 64, 16384], P('crop', 'slab')
- skip_grad: bfloat16 [8, 16, 16, 16, 128], P('crop', 'slab')
- grad_norm: float32 [], replicated
- embedding_new: float32 [20480, 768], P('slab', 'crop')
- attention_in_new: float32 [768, 2304], P('slab', 'crop')
- attention_out_new: float32 [768, 768], P('slab', 'crop')
- expand_up_new: float32 [768, 3072], P('slab', 'crop')
- expand_down_new: float32 [3072, 768], P('slab', 'crop')
- upsample_new: float32 [768, 1024], P('slab', 'crop')
- convolve_one_new: float32 [6912, 128], P('slab', 'crop')
- convolve_two_new: float32 [3456, 128], P('slab', 'crop')
- positions_new: float32 [512, 768], P('slab', 'crop')
- vectors_new: float32 [9216], P(('crop', 'slab'))
- embedding_mean_new: float32 [20480, 768], P('slab', 'crop')
- attention_in_mean_new: float32 [768, 2304], P('slab', 'crop')
- attention_out_mean_new: float32 [768, 768], P('slab', 'crop')
- expand_up_mean_new: float32 [768, 3072], P('slab', 'crop')
- expand_down_mean_new: float32 [3072, 768], P('slab', 'crop')
- upsample_mean_new: float32 [768, 1024], P('slab', 'crop')
- convolve_one_mean_new: float32 [6912, 128], P('slab', 'crop')
- convolve_two_mean_new: float32 [3456, 128], P('slab', 'crop')
- positions_mean_new: float32 [512, 768], P('slab', 'crop')
- vectors_mean_new: float32 [9216], P(('crop', 'slab'))
- embedding_square_new: float32 [20480, 768], P('slab', 'crop')
- attention_in_square_new: float32 [768, 2304], P('slab', 'crop')
- attention_out_square_new: float32 [768, 768], P('slab', 'crop')
- expand_up_square_new: float32 [768, 3072], P('slab', 'crop')
- expand_down_square_new: float32 [3072, 768], P('slab', 'crop')
- upsample_square_new: float32 [768, 1024], P('slab', 'crop')
- convolve_one_square_new: float32 [6912, 128], P('slab', 'crop')
- convolve_two_square_new: float32 [3456, 128], P('slab', 'crop')
- positions_square_new: float32 [512, 768], P('slab', 'crop')
- vectors_square_new: float32 [9216], P(('crop', 'slab'))
All inputs are finite; a program needn't handle non-finite values.
Results may differ from a plain program's by a relative error of at most 0.022.
Values may be sent and summed in bfloat16 or wider, within the bound.
No kernel may reach another device: no remote copies, remote signals or barrier semaphores. Data moves between devices by JAX's collectives and lax.ppermute only.
A program may use at most 320 MiB of HBM per device.

v0:
```python
import jax
import jax.numpy as jnp
from jax import lax
from jax.sharding import PartitionSpec as P

D = 768
HEADS = 12
HDIM = 64
FF = 3072
PATCH = 4096
CHANS = 4
DEC = 128
SIDE = 8
MB = 2
STEP = 10


BETA_ONE = 0.9
BETA_TWO = 0.95
RATE = 0.07
DECAY = 0.05
VECTOR_RATE = 0.4
VECTOR_DECAY = 0.0
EPSILON = 1e-08
CLIP = 1.0
CONTRACT_ROWS = (((0,), (0,)), ((), ()))
CONTRACT_COLS = (((1,), (1,)), ((), ()))


def with_halo(block, sides, width):
    for axis, dim in sides:
        count = lax.axis_size(axis)
        forward = [(i, i + 1) for i in range(count - 1)]
        backward = [(target, source) for source, target in forward]
        low = lax.ppermute(
            lax.slice_in_dim(block, block.shape[dim] - width, None, axis=dim), axis, forward
        )
        high = lax.ppermute(lax.slice_in_dim(block, 0, width, axis=dim), axis, backward)
        block = jnp.concatenate([low, block, high], axis=dim)
    return block


def layer_norm(values, gain, shift):
    center = values - jnp.mean(values, -1, keepdims=True)
    spread = jnp.mean(center * center, -1, keepdims=True)
    return center * lax.rsqrt(spread + 1e-06) * gain + shift


def gelu_exact(values):
    return jax.nn.gelu(values, approximate=False)


def gelu_slope(values):
    return (
        0.5 * (1.0 + lax.erf(values * 0.7071067811865476))
        + values * jnp.exp(-0.5 * values * values) * 0.3989422804014327
    )


def matmul(left, right):
    return jnp.dot(left, right, preferred_element_type=jnp.float32)


def matmul_left_t(left, right):
    return lax.dot_general(left, right, CONTRACT_ROWS, preferred_element_type=jnp.float32)


def matmul_right_t(left, right):
    return lax.dot_general(left, right, CONTRACT_COLS, preferred_element_type=jnp.float32)


def fetch_weights(shards):
    (
        embed_low,
        triple_low,
        output_low,
        up_low,
        down_low,
        lift_low,
        first_low,
        second_low,
        posit_low,
        vector_low,
    ) = [entry.astype(jnp.bfloat16) for entry in shards]
    slab_whole = (
        lax.all_gather(embed_low, "slab", axis=0, tiled=True),
        lax.all_gather(triple_low, "slab", axis=0, tiled=True),
        lax.all_gather(output_low, "slab", axis=0, tiled=True),
        lax.all_gather(up_low, "slab", axis=0, tiled=True),
        lax.all_gather(down_low, "slab", axis=0, tiled=True),
        lax.all_gather(lift_low, "slab", axis=0, tiled=True),
        lax.all_gather(first_low, "slab", axis=0, tiled=True),
        lax.all_gather(second_low, "slab", axis=0, tiled=True),
        lax.all_gather(vector_low, "slab", axis=0, tiled=True),
    )
    return (
        lax.all_gather(slab_whole[0], "crop", axis=1, tiled=True),
        lax.all_gather(slab_whole[1], "crop", axis=1, tiled=True),
        lax.all_gather(slab_whole[2], "crop", axis=1, tiled=True),
        lax.all_gather(slab_whole[3], "crop", axis=1, tiled=True),
        lax.all_gather(slab_whole[4], "crop", axis=1, tiled=True),
        lax.all_gather(slab_whole[5], "crop", axis=1, tiled=True),
        lax.all_gather(slab_whole[6], "crop", axis=1, tiled=True),
        lax.all_gather(slab_whole[7], "crop", axis=1, tiled=True),
        lax.all_gather(posit_low, "crop", axis=1, tiled=True),
        lax.all_gather(slab_whole[8], "crop", axis=0, tiled=True),
    )


def with_rims(volume):
    rimmed = with_halo(volume, (("slab", 1),), 1)
    return jnp.pad(rimmed, ((0, 0), (0, 0), (1, 1), (1, 1), (0, 0)))


def columns(volume):
    padded = with_rims(volume)
    crop_count, layers, breadth = (volume.shape[0], volume.shape[1], volume.shape[2])
    pieces = [
        padded[
            :,
            shift_z : shift_z + layers,
            shift_y : shift_y + breadth,
            shift_x : shift_x + breadth,
            :,
        ]
        for shift_z in range(3)
        for shift_y in range(3)
        for shift_x in range(3)
    ]
    return jnp.concatenate(pieces, -1).reshape(crop_count * layers * breadth * breadth, -1)


def back_conv(grad_out, kernel, inputs):
    outputs = kernel.shape[1]
    flipped = (
        kernel.reshape(27, inputs, outputs)[::-1].transpose(0, 2, 1).reshape(27 * outputs, inputs)
    )
    return matmul(columns(grad_out), flipped).reshape(grad_out.shape[:-1] + (inputs,))


def slab_totals(first, second):
    return lax.psum((jnp.sum(first, (1, 2, 3)), jnp.sum(second, (1, 2, 3))), "slab")


def norm_forward(values, voxel_count):
    totals = slab_totals(values, values * values)
    average = totals[0] / voxel_count
    inverse = lax.rsqrt(totals[1] / voxel_count - average * average + 1e-05)
    return ((values - average[:, None, None, None, :]) * inverse[:, None, None, None, :], inverse)


def norm_backward(grad, normed, inverse, voxel_count):
    totals = slab_totals(grad, grad * normed)
    first_mean = totals[0][:, None, None, None, :] / voxel_count
    second_mean = totals[1][:, None, None, None, :] / voxel_count
    return inverse[:, None, None, None, :] * (grad - first_mean - normed * second_mean)


def to_volume(lifted, crop_count):
    layers = lifted.shape[0] // (crop_count * SIDE * SIDE)
    shaped = lifted.reshape(crop_count, layers, SIDE, SIDE, 2, 2, 2, DEC)
    return shaped.transpose(0, 1, 4, 2, 5, 3, 6, 7).reshape(
        crop_count, 2 * layers, 2 * SIDE, 2 * SIDE, DEC
    )


def to_tokens(volume):
    crop_count, layers = (volume.shape[0], volume.shape[1] // 2)
    shaped = volume.reshape(crop_count, layers, 2, SIDE, 2, SIDE, 2, DEC)
    return shaped.transpose(0, 1, 3, 5, 2, 4, 6, 7).reshape(
        crop_count * layers * SIDE * SIDE, 8 * DEC
    )


def attention_probs(query, pairs_all):
    crop_count, length = (pairs_all.shape[0], pairs_all.shape[1])
    keys_all = pairs_all[..., :D].reshape(crop_count, length, HEADS, HDIM)
    values_all = pairs_all[..., D:].reshape(crop_count, length, HEADS, HDIM)
    scores = jnp.einsum(
        "cqhd,ckhd->chqk", query, keys_all, preferred_element_type=jnp.float32
    ) * HDIM ** (-0.5)
    probs = jax.nn.softmax(scores, axis=-1)
    return (probs, probs.astype(jnp.bfloat16), keys_all, values_all)


def embed_mri(pixel_rows, matrix):
    return matmul(pixel_rows, matrix[PATCH:])


def embed_ct(pixel_rows, matrix):
    return matmul(pixel_rows[:, :PATCH], matrix[:PATCH])


def back_mri(pixel_rows, segment, running_ct, running_mri):
    return (running_ct, running_mri + matmul_left_t(pixel_rows, segment))


def back_ct(pixel_rows, segment, running_ct, running_mri):
    return (running_ct + matmul_left_t(pixel_rows[:, :PATCH], segment), running_mri)


def data_mri(segment, matrix):
    return matmul_right_t(segment, matrix[PATCH:])


def data_ct(segment, matrix):
    head_part = matmul_right_t(segment, matrix[:PATCH])
    return jnp.concatenate(
        [head_part, jnp.zeros((segment.shape[0], (CHANS - 1) * PATCH), jnp.float32)], -1
    )


def adam_update(weight, gradient, mean_old, square_old, factor, step_rate, step_decay):
    clipped = gradient * factor
    mean_new = BETA_ONE * mean_old + (1.0 - BETA_ONE) * clipped
    square_new = BETA_TWO * square_old + (1.0 - BETA_TWO) * clipped * clipped
    direction = (
        mean_new
        / (1.0 - BETA_ONE**STEP)
        / (jnp.sqrt(square_new / (1.0 - BETA_TWO**STEP)) + EPSILON)
    )
    return (weight - step_rate * (direction + step_decay * weight), mean_new, square_new)


def local(
    patches,
    modality,
    skip_feats,
    cotangent,
    embedding,
    attention_in,
    attention_out,
    expand_up,
    expand_down,
    upsample,
    convolve_one,
    convolve_two,
    positions,
    vectors,
    embedding_mean,
    attention_in_mean,
    attention_out_mean,
    expand_up_mean,
    expand_down_mean,
    upsample_mean,
    convolve_one_mean,
    convolve_two_mean,
    positions_mean,
    vectors_mean,
    embedding_square,
    attention_in_square,
    attention_out_square,
    expand_up_square,
    expand_down_square,
    upsample_square,
    convolve_one_square,
    convolve_two_square,
    positions_square,
    vectors_square,
):
    shards = (
        embedding,
        attention_in,
        attention_out,
        expand_up,
        expand_down,
        upsample,
        convolve_one,
        convolve_two,
        positions,
        vectors,
    )
    means_in = (
        embedding_mean,
        attention_in_mean,
        attention_out_mean,
        expand_up_mean,
        expand_down_mean,
        upsample_mean,
        convolve_one_mean,
        convolve_two_mean,
        positions_mean,
        vectors_mean,
    )
    squares_in = (
        embedding_square,
        attention_in_square,
        attention_out_square,
        expand_up_square,
        expand_down_square,
        upsample_square,
        convolve_one_square,
        convolve_two_square,
        positions_square,
        vectors_square,
    )
    step_rates = (RATE,) * 9 + (VECTOR_RATE,)
    step_decays = (DECAY,) * 9 + (VECTOR_DECAY,)
    crop_batch = patches.shape[0] // MB
    local_tokens = patches.shape[1] * patches.shape[2]
    slab_count = lax.axis_size("slab")
    length = local_tokens * slab_count
    voxel_count = skip_feats.shape[1] * skip_feats.shape[2] * skip_feats.shape[3] * slab_count
    score_scale = HDIM ** (-0.5)
    running_ct = jnp.zeros((PATCH, D), jnp.float32)
    running_mri = jnp.zeros((CHANS * PATCH, D), jnp.float32)
    summed = None
    outputs, patch_grads, skip_grads = ([], [], [])
    for batch_index in range(MB):
        first_crop = batch_index * crop_batch
        last_crop = first_crop + crop_batch
        gathered = fetch_weights(shards)
        (
            embed_full,
            triple_full,
            output_full,
            up_full,
            down_full,
            lift_full,
            first_full,
            second_full,
            posit_full,
            vector_full,
        ) = gathered
        vector_rows = vector_full.astype(jnp.float32).reshape(12, D)
        position_rows = posit_full.astype(jnp.float32)
        pixels = patches[first_crop:last_crop]
        modal_kinds = modality[first_crop:last_crop]
        crop_index = 0
        pixel_rows = pixels[crop_index].reshape(local_tokens, CHANS * PATCH)
        modal_kind = modal_kinds[crop_index]
        product = lax.cond(modal_kind == 1, embed_mri, embed_ct, pixel_rows, embed_full)
        embedded = (
            product + jnp.where(modal_kind == 1, vector_rows[7], vector_rows[6]) + position_rows
        )
        normed_one, pull_one = jax.vjp(layer_norm, embedded, vector_rows[0], vector_rows[1])
        normed_one = normed_one.astype(jnp.bfloat16)
        triple = matmul(normed_one, triple_full).astype(jnp.bfloat16)
        query = triple[:, :D].reshape(crop_batch, local_tokens, HEADS, HDIM)
        pairs_local = triple[:, D:].reshape(crop_batch, local_tokens, 2 * D)
        pairs_all = lax.all_gather(pairs_local, "slab", axis=1, tiled=True)
        probs, probs_low, keys_all, values_all = attention_probs(query, pairs_all)
        mixed = (
            jnp.einsum("chqk,ckhd->cqhd", probs_low, values_all, preferred_element_type=jnp.float32)
            .reshape(crop_batch * local_tokens, D)
            .astype(jnp.bfloat16)
        )
        hidden_one = embedded + matmul(mixed, output_full) + vector_rows[4]
        normed_two, pull_two = jax.vjp(layer_norm, hidden_one, vector_rows[2], vector_rows[3])
        normed_two = normed_two.astype(jnp.bfloat16)
        inner_act, pull_gelu = jax.vjp(
            gelu_exact, matmul(normed_two, up_full) + vector_rows[8:].reshape(FF)
        )
        activated = inner_act.astype(jnp.bfloat16)
        hidden_two = hidden_one + matmul(activated, down_full) + vector_rows[5]
        hidden_low = hidden_two.astype(jnp.bfloat16)
        volume = to_volume(matmul(hidden_low, lift_full), crop_batch)
        joined = jnp.concatenate(
            [volume.astype(jnp.bfloat16), skip_feats[first_crop:last_crop]], -1
        )
        cols_one = columns(joined)
        conv_one = matmul(cols_one, first_full).reshape(volume.shape)
        normed_a, inverse_a = norm_forward(conv_one, voxel_count)
        first_act = gelu_exact(normed_a).astype(jnp.bfloat16)
        cols_two = columns(first_act)
        conv_two = matmul(cols_two, second_full).reshape(volume.shape)
        normed_b, inverse_b = norm_forward(conv_two, voxel_count)
        before = normed_b + volume
        outputs.append(gelu_exact(before).astype(jnp.bfloat16))
        gathered = fetch_weights(lax.optimization_barrier((shards, before))[0])
        (
            embed_full,
            triple_full,
            output_full,
            up_full,
            down_full,
            lift_full,
            first_full,
            second_full,
            posit_full,
            vector_full,
        ) = gathered
        grad_before = cotangent[first_crop:last_crop].astype(jnp.float32) * gelu_slope(before)
        grad_conv_two = norm_backward(grad_before, normed_b, inverse_b, voxel_count).astype(
            jnp.bfloat16
        )
        weight_second = matmul_left_t(cols_two, grad_conv_two.reshape(-1, DEC))
        grad_first = back_conv(grad_conv_two, second_full, DEC) * gelu_slope(normed_a)
        grad_conv_one = norm_backward(grad_first, normed_a, inverse_a, voxel_count).astype(
            jnp.bfloat16
        )
        weight_first = matmul_left_t(cols_one, grad_conv_one.reshape(-1, DEC))
        grad_joined = back_conv(grad_conv_one, first_full, 2 * DEC)
        skip_grads.append(grad_joined[..., DEC:].astype(jnp.bfloat16))
        grad_lifted = to_tokens(grad_before + grad_joined[..., :DEC]).astype(jnp.bfloat16)
        weight_lift = matmul_left_t(hidden_low, grad_lifted)
        grad_hidden = matmul_right_t(grad_lifted, lift_full)
        bias_down = jnp.sum(grad_hidden, 0)
        grad_branch = grad_hidden.astype(jnp.bfloat16)
        weight_down = matmul_left_t(activated, grad_branch)
        grad_inner = pull_gelu(matmul_right_t(grad_branch, down_full))[0]
        bias_up = jnp.sum(grad_inner, 0)
        grad_inner_low = grad_inner.astype(jnp.bfloat16)
        weight_up = matmul_left_t(normed_two, grad_inner_low)
        back_two = pull_two(matmul_right_t(grad_inner_low, up_full))
        grad_hidden = grad_hidden + back_two[0]
        bias_out = jnp.sum(grad_hidden, 0)
        grad_branch = grad_hidden.astype(jnp.bfloat16)
        weight_out = matmul_left_t(mixed, grad_branch)
        grad_mixed = (
            matmul_right_t(grad_branch, output_full)
            .astype(jnp.bfloat16)
            .reshape(crop_batch, local_tokens, HEADS, HDIM)
        )
        pairs_back = lax.optimization_barrier((pairs_local, grad_mixed))[0]
        pairs_all = lax.all_gather(pairs_back, "slab", axis=1, tiled=True)
        probs, probs_low, keys_all, values_all = attention_probs(query, pairs_all)
        grad_probs = jnp.einsum(
            "cqhd,ckhd->chqk", grad_mixed, values_all, preferred_element_type=jnp.float32
        )
        centre = jnp.sum(probs * grad_probs, -1, keepdims=True)
        grad_scores = (probs * (grad_probs - centre)).astype(jnp.bfloat16)
        grad_query = (
            jnp.einsum("chqk,ckhd->cqhd", grad_scores, keys_all, preferred_element_type=jnp.float32)
            * score_scale
        )
        grad_keys = (
            jnp.einsum("chqk,cqhd->ckhd", grad_scores, query, preferred_element_type=jnp.float32)
            * score_scale
        )
        grad_values = jnp.einsum(
            "chqk,cqhd->ckhd", probs_low, grad_mixed, preferred_element_type=jnp.float32
        )
        pair_terms = jnp.concatenate(
            [grad_keys.reshape(crop_batch, length, D), grad_values.reshape(crop_batch, length, D)],
            -1,
        )
        grad_pairs = lax.psum_scatter(
            pair_terms.astype(jnp.bfloat16), "slab", scatter_dimension=1, tiled=True
        ).astype(jnp.float32)
        grad_triple = jnp.concatenate(
            [grad_query.reshape(-1, D), grad_pairs.reshape(-1, 2 * D)], -1
        ).astype(jnp.bfloat16)
        weight_triple = matmul_left_t(normed_one, grad_triple)
        back_one = pull_one(matmul_right_t(grad_triple, triple_full))
        grad_hidden = grad_hidden + back_one[0]
        grad_low = grad_hidden.astype(jnp.bfloat16)
        grad_crops = grad_hidden.reshape(crop_batch, local_tokens, D)
        crop_index = 0
        pixel_rows = pixels[crop_index].reshape(local_tokens, CHANS * PATCH)
        modal_kind = modal_kinds[crop_index]
        column_sums = jnp.sum(grad_crops[crop_index], 0)
        bias_ct = jnp.where(modal_kind == 1, 0.0, column_sums)
        bias_mri = jnp.where(modal_kind == 1, column_sums, 0.0)
        running_ct, running_mri = lax.cond(
            modal_kind == 1, back_mri, back_ct, pixel_rows, grad_low, running_ct, running_mri
        )
        pixel_grad = lax.cond(modal_kind == 1, data_mri, data_ct, grad_low, embed_full)
        patch_grads.append(
            pixel_grad.astype(jnp.bfloat16).reshape(
                patches.shape[1], patches.shape[2], CHANS * PATCH
            )
        )
        vector_grad = jnp.concatenate(
            [
                jnp.stack(
                    [
                        back_one[1],
                        back_one[2],
                        back_two[1],
                        back_two[2],
                        bias_out,
                        bias_down,
                        bias_ct,
                        bias_mri,
                    ]
                ),
                bias_up.reshape(4, D),
            ],
            0,
        ).reshape(12 * D)
        batch_grads = (
            weight_triple,
            weight_out,
            weight_up,
            weight_down,
            weight_lift,
            weight_first,
            weight_second,
            jnp.sum(grad_crops, 0),
            vector_grad,
        )
        summed = (
            batch_grads
            if summed is None
            else tuple(
                (
                    jnp.add(left_term, right_term)
                    for left_term, right_term in zip(summed, batch_grads)
                )
            )
        )
    embed_grad = jnp.concatenate([running_ct, running_mri], 0)
    reduced = (
        lax.psum_scatter(
            embed_grad.astype(jnp.bfloat16), "crop", scatter_dimension=1, tiled=True
        ).astype(jnp.float32),
        lax.psum_scatter(
            summed[0].astype(jnp.bfloat16), "crop", scatter_dimension=1, tiled=True
        ).astype(jnp.float32),
        lax.psum_scatter(
            summed[1].astype(jnp.bfloat16), "crop", scatter_dimension=1, tiled=True
        ).astype(jnp.float32),
        lax.psum_scatter(
            summed[2].astype(jnp.bfloat16), "crop", scatter_dimension=1, tiled=True
        ).astype(jnp.float32),
        lax.psum_scatter(
            summed[3].astype(jnp.bfloat16), "crop", scatter_dimension=1, tiled=True
        ).astype(jnp.float32),
        lax.psum_scatter(
            summed[4].astype(jnp.bfloat16), "crop", scatter_dimension=1, tiled=True
        ).astype(jnp.float32),
        lax.psum_scatter(
            summed[5].astype(jnp.bfloat16), "crop", scatter_dimension=1, tiled=True
        ).astype(jnp.float32),
        lax.psum_scatter(
            summed[6].astype(jnp.bfloat16), "crop", scatter_dimension=1, tiled=True
        ).astype(jnp.float32),
        lax.psum_scatter(
            summed[7].astype(jnp.bfloat16), "crop", scatter_dimension=1, tiled=True
        ).astype(jnp.float32),
        lax.psum_scatter(
            summed[8].astype(jnp.bfloat16), "crop", scatter_dimension=0, tiled=True
        ).astype(jnp.float32),
    )
    final = (
        lax.psum_scatter(
            reduced[0].astype(jnp.bfloat16), "slab", scatter_dimension=0, tiled=True
        ).astype(jnp.float32),
        lax.psum_scatter(
            reduced[1].astype(jnp.bfloat16), "slab", scatter_dimension=0, tiled=True
        ).astype(jnp.float32),
        lax.psum_scatter(
            reduced[2].astype(jnp.bfloat16), "slab", scatter_dimension=0, tiled=True
        ).astype(jnp.float32),
        lax.psum_scatter(
            reduced[3].astype(jnp.bfloat16), "slab", scatter_dimension=0, tiled=True
        ).astype(jnp.float32),
        lax.psum_scatter(
            reduced[4].astype(jnp.bfloat16), "slab", scatter_dimension=0, tiled=True
        ).astype(jnp.float32),
        lax.psum_scatter(
            reduced[5].astype(jnp.bfloat16), "slab", scatter_dimension=0, tiled=True
        ).astype(jnp.float32),
        lax.psum_scatter(
            reduced[6].astype(jnp.bfloat16), "slab", scatter_dimension=0, tiled=True
        ).astype(jnp.float32),
        lax.psum_scatter(
            reduced[7].astype(jnp.bfloat16), "slab", scatter_dimension=0, tiled=True
        ).astype(jnp.float32),
        lax.psum_scatter(
            reduced[9].astype(jnp.bfloat16), "slab", scatter_dimension=0, tiled=True
        ).astype(jnp.float32),
    )
    gradients = (
        final[0],
        final[1],
        final[2],
        final[3],
        final[4],
        final[5],
        final[6],
        final[7],
        reduced[8],
        final[8],
    )
    local_sum = jnp.float32(0.0)
    for gradient in gradients:
        local_sum = local_sum + jnp.sum(gradient * gradient)
    grad_norm = jnp.sqrt(lax.psum(local_sum, ("crop", "slab")))
    factor = jnp.minimum(1.0, CLIP / grad_norm)
    news, means, squares = ([], [], [])
    for weight, gradient, mean_old, square_old, step_rate, step_decay in zip(
        shards, gradients, means_in, squares_in, step_rates, step_decays
    ):
        weight_new, mean_new, square_new = adam_update(
            weight, gradient, mean_old, square_old, factor, step_rate, step_decay
        )
        news.append(weight_new)
        means.append(mean_new)
        squares.append(square_new)
    block_output = jnp.concatenate(outputs, 0)
    patch_grad = jnp.stack(patch_grads, 0)
    skip_grad = jnp.concatenate(skip_grads, 0)
    return (
        block_output,
        patch_grad,
        skip_grad,
        grad_norm,
        news[0],
        news[1],
        news[2],
        news[3],
        news[4],
        news[5],
        news[6],
        news[7],
        news[8],
        news[9],
        means[0],
        means[1],
        means[2],
        means[3],
        means[4],
        means[5],
        means[6],
        means[7],
        means[8],
        means[9],
        squares[0],
        squares[1],
        squares[2],
        squares[3],
        squares[4],
        squares[5],
        squares[6],
        squares[7],
        squares[8],
        squares[9],
    )


def solution(mesh):
    return jax.shard_map(
        local,
        mesh=mesh,
        in_specs=(
            P("crop", "slab", None, None),
            P("crop"),
            P("crop", "slab", None, None, None),
            P("crop", "slab", None, None, None),
            P("slab", "crop"),
            P("slab", "crop"),
            P("slab", "crop"),
            P("slab", "crop"),
            P("slab", "crop"),
            P("slab", "crop"),
            P("slab", "crop"),
            P("slab", "crop"),
            P("slab", "crop"),
            P(("crop", "slab")),
            P("slab", "crop"),
            P("slab", "crop"),
            P("slab", "crop"),
            P("slab", "crop"),
            P("slab", "crop"),
            P("slab", "crop"),
            P("slab", "crop"),
            P("slab", "crop"),
            P("slab", "crop"),
            P(("crop", "slab")),
            P("slab", "crop"),
            P("slab", "crop"),
            P("slab", "crop"),
            P("slab", "crop"),
            P("slab", "crop"),
            P("slab", "crop"),
            P("slab", "crop"),
            P("slab", "crop"),
            P("slab", "crop"),
            P(("crop", "slab")),
        ),
        out_specs=(
            P("crop", "slab", None, None, None),
            P("crop", "slab", None, None),
            P("crop", "slab", None, None, None),
            P(),
            P("slab", "crop"),
            P("slab", "crop"),
            P("slab", "crop"),
            P("slab", "crop"),
            P("slab", "crop"),
            P("slab", "crop"),
            P("slab", "crop"),
            P("slab", "crop"),
            P("slab", "crop"),
            P(("crop", "slab")),
            P("slab", "crop"),
            P("slab", "crop"),
            P("slab", "crop"),
            P("slab", "crop"),
            P("slab", "crop"),
            P("slab", "crop"),
            P("slab", "crop"),
            P("slab", "crop"),
            P("slab", "crop"),
            P(("crop", "slab")),
            P("slab", "crop"),
            P("slab", "crop"),
            P("slab", "crop"),
            P("slab", "crop"),
            P("slab", "crop"),
            P("slab", "crop"),
            P("slab", "crop"),
            P("slab", "crop"),
            P("slab", "crop"),
            P(("crop", "slab")),
        ),
        check_vma=False,
    )
```

profile of v0, /device:TPU:0, one launch (start us, length us, event | category | flops | bytes accessed | tf_op | source)
XLA Modules:
  0.0 2563.4 jit_solution(13908242728112255569)
XLA Ops:
  9.9 80.8 %all-gather.33.cloned.1.call-done = bf16[20480,192]{0,1:T(8,128)(2,1)} async-done(((bf16[2560,192]{0,1:T(8,128)(2,1)}), bf16[20480,192]{0,1:T(8,128)(2,1)}) %all-gather.33.cloned.1.call-update) | async-done | bytes 7864336 | tf_op jit(solution)/shard_map/all_gather | solution.py:86
  169.6 202.6 %all-gather.35.cloned.1.call-done = bf16[20480,768]{0,1:T(8,128)(2,1)} async-done(((bf16[20480,192]{0,1:T(8,128)(2,1)}), bf16[20480,768]{0,1:T(8,128)(2,1)}) %all-gather.35.cloned.1.call-update) | async-done | bytes 31457296 | tf_op jit(solution)/shard_map/all_gather | solution.py:97
  372.3 51.0 %conditional.7 = (f32[64,768]{1,0:T(8,128)S(1)}) conditional(s32[]{:T(128)} %convert_element_type.482, (bf16[64,16384]{1,0:T(8,128)(2,1)}, bf16[20480,768]{0,1:T(8,128)(2,1)}) %tuple.59, (bf16[20480,768]{0,1:T(8,128)(2,1)}, bf16[64,16384]{1,0:T(8,128)(2,1)}) %tuple.60), branch_computations={%region_16.17_spmd, %region_17.18_spmd} | conditional | flops 1610612736 | bytes 90374152 | solution.py:332
  372.3 39.8 %copy.276 = bf16[20480,768]{1,0:T(8,128)(2,1)} copy(bf16[20480,768]{0,1:T(8,128)(2,1)} %get-tuple-element.315) | data formatting | bytes 62914560 | tf_op jit(solution)/shard_map
  423.3 51.6 %conditional.6 = (f32[64,768]{1,0:T(8,128)S(1)}) conditional(s32[]{:T(128)} %convert_element_type.453, (bf16[64,16384]{1,0:T(8,128)(2,1)S(1)}, bf16[20480,768]{0,1:T(8,128)(2,1)}) %tuple.57, (bf16[20480,768]{0,1:T(8,128)(2,1)}, bf16[64,16384]{1,0:T(8,128)(2,1)S(1)}) %tuple.58), branch_computations={%region_0.0_spmd, %region_1.0_spmd} | conditional | flops 1610612736 | bytes 90374152 | solution.py:332
  423.3 40.7 %copy.265 = bf16[20480,768]{1,0:T(8,128)(2,1)} copy(bf16[20480,768]{0,1:T(8,128)(2,1)} %get-tuple-element.311) | data formatting | bytes 62914560 | tf_op jit(solution)/shard_map
  687.5 55.4 %all-gather.47.cloned.1.call-done = bf16[3072,768]{0,1:T(8,128)(2,1)} async-done(((bf16[3072,192]{0,1:T(8,128)(2,1)}), bf16[3072,768]{0,1:T(8,128)(2,1)}) %all-gather.47.cloned.1.call-update) | async-done | bytes 4718608 | tf_op jit(solution)/shard_map/all_gather | solution.py:101
  1161.7 32.7 %all-gather.73.cloned.1.call-done = bf16[768,2304]{0,1:T(8,128)(2,1)} async-done(((bf16[768,576]{0,1:T(8,128)(2,1)}), bf16[768,2304]{0,1:T(8,128)(2,1)}) %all-gather.73.cloned.1.call-update) | async-done | bytes 3538960 | tf_op jit(solution)/shard_map/all_gather | solution.py:98
  1225.3 50.4 %conditional.11 = (f32[16384,768]{1,0:T(8,128)}, bf16[4096,768]{0,1:T(8,128)(2,1)}) conditional(s32[]{:T(128)} %convert_element_type.482, (bf16[64,16384]{1,0:T(8,128)(2,1)}, bf16[64,768]{1,0:T(8,128)(2,1)S(1)}, f32[4096,768]{1,0:T(8,128)}, f32[16384,768]{1,0:T(8,128)}) %tuple.65, (bf16[64,16384]{1,0:T(8,128)(2,1)}, ...), branch_computations={%region_70.71_spmd, %region_71.72_spmd} | conditional | flops 1626341376 | bytes 134316048 | solution.py:455
  1225.5 33.4 %convolution_add_fusion = f32[16384,768]{1,0:T(8,128)} fusion(f32[16384,768]{1,0:T(8,128)} %get-tuple-element.95, bf16[64,16384]{1,0:T(8,128)(2,1)} %get-tuple-element.96, bf16[64,768]{1,0:T(8,128)(2,1)S(1)} %get-tuple-element.97), kind=kOutput, calls=%fused_computation.30 | convolution fusion | flops 1623195648 | bytes 102858752 | tf_op jit(solution)/shard_map/cond/branch_1_fun/dot_general | solution.py:65
  1275.8 37.9 %copy.307 = bf16[16384,768]{0,1:T(8,128)(2,1)} copy(f32[16384,768]{1,0:T(8,128)} %get-tuple-element.155) | data formatting | bytes 75497472 | tf_op jit(solution)/shard_map/cond | solution.py:455
  1367.3 36.0 %reduce-scatter.54.cloned.1.call-done = bf16[6912,32]{0,1:T(8,128)(2,1)} async-done(((bf16[6912,128]{0,1:T(8,128)(2,1)}), bf16[6912,32]{0,1:T(8,128)(2,1)}) %reduce-scatter.54.cloned.1.call-update) | async-done | bytes 442384 | tf_op jit(solution)/shard_map/reduce_scatter | solution.py:523
  1405.9 57.4 %reduce-scatter.48.cloned.1.call-done = bf16[3072,192]{0,1:T(8,128)(2,1)} async-done(((bf16[3072,768]{0,1:T(8,128)(2,1)}), bf16[3072,192]{0,1:T(8,128)(2,1)}) %reduce-scatter.48.cloned.1.call-update) | async-done | bytes 1179664 | tf_op jit(solution)/shard_map/reduce_scatter | solution.py:517
  1465.9 57.5 %reduce-scatter.44.cloned.1.call-done = bf16[768,768]{1,0:T(8,128)(2,1)} async-done(((bf16[768,3072]{1,0:T(8,128)(2,1)}), bf16[768,768]{1,0:T(8,128)(2,1)}) %reduce-scatter.44.cloned.1.call-update) | async-done | bytes 1179664 | tf_op jit(solution)/shard_map/reduce_scatter | solution.py:514
  1523.4 50.9 %reduce-scatter.40.cloned.1.call-done = bf16[768,576]{0,1:T(8,128)(2,1)} async-done(((bf16[768,2304]{0,1:T(8,128)(2,1)}), bf16[768,576]{0,1:T(8,128)(2,1)}) %reduce-scatter.40.cloned.1.call-update) | async-done | bytes 884752 | tf_op jit(solution)/shard_map/reduce_scatter | solution.py:508
  1576.6 273.6 %reduce-scatter.36.cloned.1.call-done = bf16[20480,192]{0,1:T(8,128)(2,1)} async-done(((bf16[20480,768]{0,1:T(8,128)(2,1)}), bf16[20480,192]{0,1:T(8,128)(2,1)}) %reduce-scatter.36.cloned.1.call-update) | async-done | bytes 7864336 | tf_op jit(solution)/shard_map/reduce_scatter | solution.py:505
  1917.5 277.9 %all-gather.55.cloned.1.call-done = bf16[20480,768]{0,1:T(8,128)(2,1)} async-done(((bf16[20480,192]{0,1:T(8,128)(2,1)}), bf16[20480,768]{0,1:T(8,128)(2,1)}) %all-gather.55.cloned.1.call-update) | async-done | bytes 31457296 | tf_op jit(solution)/shard_map/all_gather | solution.py:97
  2195.5 53.1 %conditional.8 = (bf16[1,1,64,16384]{3,2,1,0:T(8,128)(2,1)S(1)}) conditional(s32[]{:T(128)} %convert_element_type.453, (bf16[20480,768]{0,1:T(8,128)(2,1)}, bf16[64,768]{1,0:T(8,128)(2,1)S(1)}) %tuple.62, (bf16[20480,768]{0,1:T(8,128)(2,1)}, bf16[64,768]{1,0:T(8,128)(2,1)S(1)}) %tuple.62), branch_computations={%region_48.49_spmd, %region_49.50_spmd} | conditional | flops 1611661312 | bytes 90275848 | solution.py:458
  2195.5 40.6 %copy.297 = bf16[20480,768]{1,0:T(8,128)(2,1)} copy(bf16[20480,768]{0,1:T(8,128)(2,1)} %get-tuple-element.319) | data formatting | bytes 62914560 | tf_op jit(solution)/shard_map
  2248.5 54.8 %conditional.9 = (bf16[1,1,64,16384]{3,2,1,0:T(8,128)(2,1)}) conditional(s32[]{:T(128)} %convert_element_type.482, (bf16[20480,768]{0,1:T(8,128)(2,1)}, bf16[64,768]{1,0:T(8,128)(2,1)S(1)}) %tuple.63, (bf16[20480,768]{0,1:T(8,128)(2,1)}, bf16[64,768]{1,0:T(8,128)(2,1)S(1)}) %tuple.63), branch_computations={%region_66.67_spmd, %region_67.68_spmd} | conditional | flops 1611661312 | bytes 90275848 | solution.py:458
  2248.8 40.7 %copy.306 = bf16[20480,768]{1,0:T(8,128)(2,1)} copy(bf16[20480,768]{0,1:T(8,128)(2,1)} %get-tuple-element.323) | data formatting | bytes 62914560 | tf_op jit(solution)/shard_map
  2361.7 31.4 %reduce-scatter.62.cloned.1.call-done = bf16[96,576]{1,0:T(8,128)(2,1)} async-done(((bf16[768,576]{1,0:T(8,128)(2,1)}), bf16[96,576]{1,0:T(8,128)(2,1)}) %reduce-scatter.62.cloned.1.call-update) | async-done | bytes 110608
  2394.7 83.6 %reduce-scatter.38.cloned.1.call-done = bf16[2560,192]{0,1:T(8,128)(2,1)} async-done(((bf16[20480,192]{0,1:T(8,128)(2,1)}), bf16[2560,192]{0,1:T(8,128)(2,1)}) %reduce-scatter.38.cloned.1.call-update) | async-done | bytes 983056 | tf_op jit(solution)/shard_map/reduce_scatter | solution.py:537
  2491.2 37.7 %psum.135 = f32[]{:T(128)} all-reduce(f32[]{:T(128)S(6)} %add.639), channel_id=1, replica_groups=mesh['crop'=4,'slab'=8] {'crop','slab'}, use_global_device_ids=true, to_apply=%region_117.118 | all-reduce | flops 1 | bytes 8 | tf_op jit(solution)/shard_map/psum | solution.py:580
  (1213 shorter events, 1045.2 us)
Async XLA Ops:
  109.8 391.7 %all-gather.41.cloned.1.call-start = ((), (), s32[]{:S(2)}) async-start(), calls=%async_computation.23 | async-start | bytes 1327104 | tf_op jit(solution)/shard_map/all_gather | solution.py:89
  110.6 391.7 %all-gather.45.cloned.1.call-start = ((), (), s32[]{:S(2)}) async-start(), calls=%async_computation.25 | async-start | bytes 1327104 | tf_op jit(solution)/shard_map/all_gather | solution.py:90
  111.4 448.3 %all-gather.61.cloned.1.call-start = ((), (), s32[]{:S(2)}) async-start(), calls=%async_computation.33 | async-start | bytes 1327104 | tf_op jit(solution)/shard_map/all_gather | solution.py:90
  112.1 448.2 %all-gather.65.cloned.1.call-start = ((), (), s32[]{:S(2)}) async-start(), calls=%async_computation.35 | async-start | bytes 1327104 | tf_op jit(solution)/shard_map/all_gather | solution.py:89
  112.9 535.0 %all-gather.57.cloned.1.call-start = ((), (), s32[]{:S(2)}) async-start(), calls=%async_computation.31 | async-start | bytes 2211840 | tf_op jit(solution)/shard_map/all_gather | solution.py:103
  129.0 524.9 %all-gather.79.cloned.1.call-start = ((), (), s32[]{:S(2)}) async-start(), calls=%async_computation.53 | async-start | bytes 1769472 | tf_op jit(solution)/shard_map/all_gather | solution.py:341
  543.9 494.0 %all-gather.59.cloned.1.call-start = ((), (), s32[]{:S(2)}) async-start(), calls=%async_computation.32 | async-start | bytes 1966080 | tf_op jit(solution)/shard_map/all_gather | solution.py:102
  559.6 482.4 %all-gather.63.cloned.1.call-start = ((), (), s32[]{:S(2)}) async-start(), calls=%async_computation.34 | async-start | bytes 5898240 | tf_op jit(solution)/shard_map/all_gather | solution.py:101
  560.2 491.7 %all-gather.67.cloned.1.call-start = ((), (), s32[]{:S(2)}) async-start(), calls=%async_computation.36 | async-start | bytes 5898240 | tf_op jit(solution)/shard_map/all_gather | solution.py:100
  561.0 500.0 %all-gather.71.cloned.1.call-start = ((), (), s32[]{:S(2)}) async-start(), calls=%async_computation.38 | async-start | bytes 1474560 | tf_op jit(solution)/shard_map/all_gather | solution.py:99
  577.2 498.4 %all-gather.75.cloned.1.call-start = ((), (), s32[]{:S(2)}) async-start(), calls=%async_computation.40 | async-start | bytes 1769472 | tf_op jit(solution)/shard_map/all_gather | solution.py:416
  653.4 500.7 %reduce-scatter.58.cloned.1.call-start = ((), (), s32[]{:S(2)}) async-start(), calls=%async_computation.54 | async-start | bytes 1769472
  1150.9 423.4 %reduce-scatter.40.cloned.1.call-start = ((), (), s32[]{:S(2)}) async-start(), calls=%async_computation.43 | async-start | bytes 4423680 | tf_op jit(solution)/shard_map/reduce_scatter | solution.py:508
  1161.7 688.5 %reduce-scatter.36.cloned.1.call-start = ((), (), s32[]{:S(2)}) async-start(), calls=%async_computation.41 | async-start | bytes 39321600 | tf_op jit(solution)/shard_map/reduce_scatter | solution.py:505
  1335.8 548.7 %reduce-scatter.70.cloned.1.call-start = ((), (), s32[]{:S(2)}) async-start(), calls=%async_computation.60 | async-start | bytes 995328
  1338.1 577.5 %reduce-scatter.64.cloned.1.call-start = ((), (), s32[]{:S(2)}) async-start(), calls=%async_computation.57 | async-start | bytes 442368
  1340.0 855.4 %all-gather.55.cloned.1.call-start = ((), (), s32[]{:S(2)}) async-start(), calls=%async_computation.30 | async-start | bytes 39321600 | tf_op jit(solution)/shard_map/all_gather | solution.py:97
  1340.6 991.3 %reduce-scatter.72.cloned.1.call-start = ((), (), s32[]{:S(2)}) async-start(), calls=%async_computation.61 | async-start | bytes 245760
  1341.5 991.9 %reduce-scatter.52.cloned.1.call-start = ((), (), s32[]{:S(2)}) async-start(), calls=%async_computation.49 | async-start | bytes 442368 | tf_op jit(solution)/shard_map/reduce_scatter | solution.py:552
  1367.2 967.6 %reduce-scatter.68.cloned.1.call-start = ((), (), s32[]{:S(2)}) async-start(), calls=%async_computation.59 | async-start | bytes 1990656
  1405.8 930.7 %reduce-scatter.66.cloned.1.call-start = ((), (), s32[]{:S(2)}) async-start(), calls=%async_computation.58 | async-start | bytes 1769472
  1465.8 894.3 %reduce-scatter.46.cloned.1.call-start = ((), (), s32[]{:S(2)}) async-start(), calls=%async_computation.46 | async-start | bytes 1327104 | tf_op jit(solution)/shard_map/reduce_scatter | solution.py:546
  1523.4 869.7 %reduce-scatter.62.cloned.1.call-start = ((), (), s32[]{:S(2)}) async-start(), calls=%async_computation.56 | async-start | bytes 1105920
  1576.5 901.8 %reduce-scatter.38.cloned.1.call-start = ((), (), s32[]{:S(2)}) async-start(), calls=%async_computation.42 | async-start | bytes 8847360 | tf_op jit(solution)/shard_map/reduce_scatter | solution.py:537
  (247 other events, 9914.1 us)
Sparse Core Ops, SparseCore 0:
  10.2 80.4 all-gather.32
  92.5 279.6 all-gather.34
  374.7 47.2 all-gather.36
  527.4 31.0 all-gather.56
  621.3 62.7 all-gather.42
  685.8 57.0 all-gather.46
  744.7 30.8 all-gather.48
  831.7 32.1 all-gather.50
  898.1 57.0 all-gather.62
  957.1 57.0 all-gather.66
  1075.6 36.3 reduce-scatter.57
  1114.9 32.5 reduce-scatter.59
  1149.2 45.1 all-gather.72
  1256.9 77.7 all-gather.52
  1370.8 32.4 reduce-scatter.53
  1406.1 57.0 reduce-scatter.47
  1466.3 57.0 reduce-scatter.43
  1527.0 47.2 reduce-scatter.39
  1577.2 272.8 reduce-scatter.35
  1852.6 31.8 reduce-scatter.69
  1917.5 277.9 all-gather.54
  2258.6 33.0 reduce-scatter.67
  2294.6 32.3 reduce-scatter.65
  2395.3 83.0 reduce-scatter.37
  (19 shorter events, 512.0 us)
where the time goes:
time: 2580 us; the launch traced here: 2560 us
  waiting for transfers between devices  1440 us (56%)
  local copies, waits for them, and re-layouts  371 us (14%)
  blocking collectives  353 us (14%)
  matrix products  227 us (9%)
  other arithmetic  108 us (4%)
  starting transfers between devices  32.3 us (1%)
  between operations  32.1 us (1%)
    all_gather x2, waiting for transfers between devices, fetch_weights(): lax.all_gather(slab_whole[0], 'crop', axis=1, tiled=True)  481 us
    reduce_scatter x1, waiting for transfers between devices, local(): lax.psum_scatter(embed_grad.astype(jnp.bfloat16), 'crop', scatter_dimensi...  274 us
    another operation x8, local copies, waits for them, and re-layouts  162 us
    unnamed x751, local copies, waits for them, and re-layouts  115 us
    unnamed x51, waiting for transfers between devices  90.6 us
    dot_general x16, matrix products, matmul_left_t(): lax.dot_general(left, right, CONTRACT_ROWS, preferred_element_type=jnp.fl...  87.3 us
    reduce_scatter x1, waiting for transfers between devices, local(): lax.psum_scatter(reduced[0].astype(jnp.bfloat16), 'slab', scatter_dimensi...  83.6 us
    all_gather x2, waiting for transfers between devices, fetch_weights(): lax.all_gather(embed_low, 'slab', axis=0, tiled=True)  80.8 us
  transfers between devices with their start and end apart: 59, of which 21 were waited for; matrix products, arithmetic and copies ran while one was open for 26% of the time, Pallas kernels for 0%

commit v1 on v0

v1 whole, which is shorter than its diff:
```python
import math

import jax
import jax.numpy as jnp
from jax import lax
from jax.sharding import Mesh
from jax.sharding import PartitionSpec as P

D = 768
HEADS = 12
HDIM = 64
FF = 3072
PATCH = 4096
CHANS = 4
DEC = 128
SIDE = 8
STEP = 10


BETA_ONE = 0.9
BETA_TWO = 0.95
RATE = 0.07
DECAY = 0.05
VECTOR_RATE = 0.4
VECTOR_DECAY = 0.0
EPSILON = 1e-08
CLIP = 1.0
CONTRACT_ROWS = (((0,), (0,)), ((), ()))
CONTRACT_COLS = (((1,), (1,)), ((), ()))


def layer_norm(values, gain, shift):
    center = values - jnp.mean(values, -1, keepdims=True)
    spread = jnp.mean(center * center, -1, keepdims=True)
    return center * lax.rsqrt(spread + 1e-06) * gain + shift


def gelu_exact(values):
    return jax.nn.gelu(values, approximate=False)


def gelu_slope(values):
    return (
        0.5 * (1.0 + lax.erf(values * 0.7071067811865476))
        + values * jnp.exp(-0.5 * values * values) * 0.3989422804014327
    )


def matmul(left, right):
    return jnp.dot(left, right, preferred_element_type=jnp.float32)


def matmul_left_t(left, right):
    return lax.dot_general(left, right, CONTRACT_ROWS, preferred_element_type=jnp.float32)


def matmul_right_t(left, right):
    return lax.dot_general(left, right, CONTRACT_COLS, preferred_element_type=jnp.float32)


SLAB = ("z", "core")
SWAP = [(0, 1), (1, 0)]


def flip_pairs(count, step):
    return [(i, i ^ step) for i in range(count)]


def slab_sum(values):
    values = values + lax.ppermute(values, "core", SWAP)
    count, step = lax.axis_size("z"), 1
    while step < count:
        values = values + lax.ppermute(values, "z", flip_pairs(count, step))
        step *= 2
    return values


def crop_sum(values):
    count, step = lax.axis_size("crop"), 1
    while step < count:
        values = values + lax.ppermute(values, "crop", flip_pairs(count, step))
        step *= 2
    return values


def crop_swap(pieces):
    return lax.all_to_all(pieces, "crop", 0, 0, tiled=True)


def crop_stack(block):
    count = lax.axis_size("crop")
    own = lax.axis_index("crop")
    if count != 4:
        return lax.all_gather(block, "crop", axis=0)
    half = block.shape[0] // 2
    upper, lower = block[:half], block[half:]
    upper_x = lax.ppermute(upper, "crop", flip_pairs(4, 1))
    lower_y = lax.ppermute(lower, "crop", flip_pairs(4, 2))
    upper_y = lax.ppermute(jnp.stack([upper, upper_x]), "crop", flip_pairs(4, 2))
    lower_x = lax.ppermute(jnp.stack([lower, lower_y]), "crop", flip_pairs(4, 1))
    upper_parts = [upper, upper_x, upper_y[0], upper_y[1]]
    lower_parts = [lower, lower_x[0], lower_y, lower_x[1]]
    whole = jnp.zeros((4,) + block.shape, block.dtype)
    zeros = (0,) * (block.ndim - 1)
    for shift in range(4):
        place = own ^ shift
        whole = lax.dynamic_update_slice(whole, upper_parts[shift][None], (place, 0) + zeros)
        whole = lax.dynamic_update_slice(whole, lower_parts[shift][None], (place, half) + zeros)
    return whole


def gather_pack(pack):
    own = crop_stack(lax.all_gather(pack, "z", axis=0))
    other = lax.ppermute(own, "core", SWAP)
    first = lax.axis_index("core") == 0
    return (jnp.where(first, own, other), jnp.where(first, other, own))


def pick(pair, start, rows, chunks):
    both = jnp.stack([part[:, :, start : start + rows * chunks] for part in pair])
    _, crops, layers, _, width = both.shape
    shaped = both.reshape(2, crops, layers, chunks, rows, width)
    return shaped.transpose(2, 0, 1, 4, 3, 5).reshape(-1, chunks * width)


def to_pack(full, chunks):
    crops, layers = lax.axis_size("crop"), lax.axis_size("z")
    width = full.shape[1] // chunks
    shaped = full.reshape(layers, 2, crops, -1, chunks, width)
    return shaped.transpose(0, 1, 2, 4, 3, 5).reshape(layers, 2, crops, -1, width)


def halve(block, axis, index, dim):
    keep = lax.dynamic_index_in_dim(block, index, dim, keepdims=False)
    send = lax.dynamic_index_in_dim(block, 1 - index, dim, keepdims=False)
    got = lax.ppermute(send, axis[0], axis[1])
    return (keep.astype(jnp.float32) + got.astype(jnp.float32)).astype(jnp.bfloat16)


def scatter_pack(pack):
    core = lax.axis_index("core")
    crops = lax.axis_size("crop")
    pack = halve(pack, ("core", SWAP), core, 1)
    if crops != 4:
        pack = lax.psum_scatter(pack, "crop", scatter_dimension=1, tiled=False)
    else:
        own = lax.axis_index("crop")
        side_y, side_x = own // 2, own % 2
        along_y, along_x = ("crop", flip_pairs(4, 2)), ("crop", flip_pairs(4, 1))
        layers, _, rows, width = pack.shape
        half = rows // 2
        upper = pack[:, :, :half].reshape(layers, 2, 2, half, width)
        lower = pack[:, :, half:].reshape(layers, 2, 2, rows - half, width)
        upper = halve(halve(upper, along_y, side_y, 1), along_x, side_x, 1)
        lower = halve(halve(lower, along_x, side_x, 2), along_y, side_y, 1)
        pack = jnp.concatenate([upper, lower], 1)
    return lax.psum_scatter(pack, "z", scatter_dimension=0, tiled=False)


def with_rims(volume):
    layers, cores = lax.axis_size("z"), lax.axis_size("core")
    count = layers * cores
    forward = [(i, i + 1) for i in range(count - 1)]
    backward = [(target, source) for source, target in forward]
    low = lax.ppermute(volume[:, -1:], SLAB, forward)
    high = lax.ppermute(volume[:, :1], SLAB, backward)
    rimmed = jnp.concatenate([low, volume, high], axis=1)
    return jnp.pad(rimmed, ((0, 0), (0, 0), (1, 1), (1, 1), (0, 0)))


def columns(volume):
    padded = with_rims(volume)
    crop_count, layers, breadth = (volume.shape[0], volume.shape[1], volume.shape[2])
    pieces = [
        padded[
            :,
            shift_z : shift_z + layers,
            shift_y : shift_y + breadth,
            shift_x : shift_x + breadth,
            :,
        ]
        for shift_z in range(3)
        for shift_y in range(3)
        for shift_x in range(3)
    ]
    return jnp.concatenate(pieces, -1).reshape(crop_count * layers * breadth * breadth, -1)


def back_conv(grad_out, kernel, inputs):
    outputs = kernel.shape[1]
    flipped = (
        kernel.reshape(27, inputs, outputs)[::-1].transpose(0, 2, 1).reshape(27 * outputs, inputs)
    )
    return matmul(columns(grad_out), flipped).reshape(grad_out.shape[:-1] + (inputs,))


def slab_totals(first, second):
    both = jnp.stack([jnp.sum(first, (1, 2, 3)), jnp.sum(second, (1, 2, 3))])
    return slab_sum(both)


def norm_forward(values, voxel_count):
    totals = slab_totals(values, values * values)
    average = totals[0] / voxel_count
    inverse = lax.rsqrt(totals[1] / voxel_count - average * average + 1e-05)
    return ((values - average[:, None, None, None, :]) * inverse[:, None, None, None, :], inverse)


def norm_backward(grad, normed, inverse, voxel_count):
    totals = slab_totals(grad, grad * normed)
    first_mean = totals[0][:, None, None, None, :] / voxel_count
    second_mean = totals[1][:, None, None, None, :] / voxel_count
    return inverse[:, None, None, None, :] * (grad - first_mean - normed * second_mean)


def heads_out(block, parts):
    crop_count, tokens = block.shape[0], block.shape[1]
    slab_count = lax.axis_size(SLAB)
    shaped = block.reshape(crop_count, tokens, parts, HEADS, HDIM).transpose(0, 3, 1, 2, 4)
    shaped = shaped.reshape(crop_count * HEADS, tokens, parts * HDIM)
    spare = -shaped.shape[0] % slab_count
    shaped = jnp.pad(shaped, ((0, spare), (0, 0), (0, 0)))
    return lax.all_to_all(shaped, SLAB, 0, 1, tiled=True)


def heads_back(block, crop_count, parts):
    shaped = lax.all_to_all(block, SLAB, 1, 0, tiled=True)[: crop_count * HEADS]
    tokens = shaped.shape[1]
    shaped = shaped.reshape(crop_count, HEADS, tokens, parts, HDIM).transpose(0, 2, 3, 1, 4)
    return shaped.reshape(crop_count * tokens, parts * D)


def to_volume(lifted, crop_count):
    layers = lifted.shape[0] // (crop_count * SIDE * SIDE)
    shaped = lifted.reshape(crop_count, layers, SIDE, SIDE, 2, 2, 2, DEC)
    return shaped.transpose(0, 1, 4, 2, 5, 3, 6, 7).reshape(
        crop_count, 2 * layers, 2 * SIDE, 2 * SIDE, DEC
    )


def to_tokens(volume):
    crop_count, layers = (volume.shape[0], volume.shape[1] // 2)
    shaped = volume.reshape(crop_count, layers, 2, SIDE, 2, SIDE, 2, DEC)
    return shaped.transpose(0, 1, 3, 5, 2, 4, 6, 7).reshape(
        crop_count * layers * SIDE * SIDE, 8 * DEC
    )


def adam_update(weight, gradient, mean_old, square_old, factor, step_rate, step_decay):
    clipped = gradient * factor
    mean_new = BETA_ONE * mean_old + (1.0 - BETA_ONE) * clipped
    square_new = BETA_TWO * square_old + (1.0 - BETA_TWO) * clipped * clipped
    direction = (
        mean_new
        / (1.0 - BETA_ONE**STEP)
        / (jnp.sqrt(square_new / (1.0 - BETA_TWO**STEP)) + EPSILON)
    )
    return (weight - step_rate * (direction + step_decay * weight), mean_new, square_new)


def local(
    patches,
    modality,
    skip_feats,
    cotangent,
    embedding,
    attention_in,
    attention_out,
    expand_up,
    expand_down,
    upsample,
    convolve_one,
    convolve_two,
    positions,
    vectors,
    embedding_mean,
    attention_in_mean,
    attention_out_mean,
    expand_up_mean,
    expand_down_mean,
    upsample_mean,
    convolve_one_mean,
    convolve_two_mean,
    positions_mean,
    vectors_mean,
    embedding_square,
    attention_in_square,
    attention_out_square,
    expand_up_square,
    expand_down_square,
    upsample_square,
    convolve_one_square,
    convolve_two_square,
    positions_square,
    vectors_square,
):
    shards = (
        embedding,
        attention_in,
        attention_out,
        expand_up,
        expand_down,
        upsample,
        convolve_one,
        convolve_two,
        positions,
        vectors,
    )
    means_in = (
        embedding_mean,
        attention_in_mean,
        attention_out_mean,
        expand_up_mean,
        expand_down_mean,
        upsample_mean,
        convolve_one_mean,
        convolve_two_mean,
        positions_mean,
        vectors_mean,
    )
    squares_in = (
        embedding_square,
        attention_in_square,
        attention_out_square,
        expand_up_square,
        expand_down_square,
        upsample_square,
        convolve_one_square,
        convolve_two_square,
        positions_square,
        vectors_square,
    )
    step_rates = (RATE,) * 9 + (VECTOR_RATE,)
    step_decays = (DECAY,) * 9 + (VECTOR_DECAY,)
    crops = lax.axis_size("crop")
    layers = lax.axis_size("z")
    slab_count = 2 * layers
    crop_batch = patches.shape[0]
    local_tokens = patches.shape[1] * patches.shape[2]
    rows_in = crop_batch * local_tokens
    voxel_count = skip_feats.shape[1] * skip_feats.shape[2] * skip_feats.shape[3] * slab_count
    score_scale = HDIM ** (-0.5)
    unit = D // crops

    lows = [entry.astype(jnp.bfloat16) for entry in shards]
    embed_rows = embedding.shape[0]
    share = embed_rows // crops
    block = math.gcd(share, PATCH)
    groups = share // block
    row_count = attention_in.shape[0] // crops
    down_count = expand_down.shape[0] // crops
    wide = jnp.concatenate(
        [
            lows[0].reshape(groups, crops, block, unit).transpose(1, 0, 2, 3).reshape(crops, share, unit),
            lows[1].reshape(crops, row_count, 3, unit).transpose(0, 2, 1, 3).reshape(crops, -1, unit),
            lows[2].reshape(crops, row_count, unit),
            lows[3].reshape(crops, row_count, 4, unit).transpose(0, 2, 1, 3).reshape(crops, -1, unit),
            lows[4].reshape(crops, down_count, unit),
            jnp.broadcast_to(lows[8][None], (crops,) + lows[8].shape),
        ],
        1,
    )
    first_count = -(-convolve_one.shape[0] // crops)
    second_count = -(-convolve_two.shape[0] // crops)
    narrow = jnp.concatenate(
        [
            jnp.pad(lows[6], ((0, crops * first_count - lows[6].shape[0]), (0, 0))).reshape(
                crops, first_count, -1
            ),
            jnp.pad(lows[7], ((0, crops * second_count - lows[7].shape[0]), (0, 0))).reshape(
                crops, second_count, -1
            ),
        ],
        1,
    )
    wide = crop_swap(wide)
    lift_rows = crop_swap(lows[5].reshape(crops, row_count, -1))
    narrow = crop_swap(narrow)
    marks = []
    edge = 0
    for size in (share, 3 * row_count, row_count, 4 * row_count, down_count, lows[8].shape[0]):
        marks.append(wide[:, edge : edge + size])
        edge += size
    embed_part = marks[0].transpose(1, 0, 2).reshape(share, D)
    triple_part = marks[1].reshape(3, crops, row_count, unit).transpose(0, 2, 1, 3).reshape(-1, D)
    output_part = marks[2].transpose(1, 0, 2).reshape(row_count, D)
    up_part = marks[3].reshape(4, crops, row_count, unit).transpose(0, 2, 1, 3).reshape(-1, D)
    down_part = marks[4].transpose(1, 0, 2).reshape(down_count, D)
    position_rows = marks[5].transpose(1, 0, 2).reshape(-1, D).astype(jnp.float32)
    lift_part = (
        lift_rows.transpose(1, 0, 2).reshape(row_count, 8, DEC).transpose(1, 0, 2).reshape(-1, DEC)
    )
    narrow_part = narrow.transpose(1, 0, 2).reshape(-1, DEC)
    slim = jnp.concatenate([lift_part, narrow_part], 0)
    slim_rows = -(-slim.shape[0] // 48) * 8
    slim = jnp.pad(slim, ((0, 6 * slim_rows - slim.shape[0]), (0, 0)))
    slim = slim.reshape(6, slim_rows, DEC).transpose(1, 0, 2).reshape(slim_rows, D)
    vector_size = vectors.shape[0]
    vector_part = jnp.pad(lows[9][None], ((0, 7), (0, D - vector_size)))

    embed_full = lax.all_gather(embed_part, SLAB, axis=0, tiled=True)
    pair_one = gather_pack(jnp.concatenate([triple_part, output_part, vector_part], 0))
    pair_two = gather_pack(jnp.concatenate([up_part, down_part, slim], 0))
    triple_full = pick(pair_one, 0, row_count, 3)
    output_full = pick(pair_one, 3 * row_count, row_count, 1)
    vector_full = jnp.stack([part[:, :, 4 * row_count, :vector_size] for part in pair_one])
    vector_full = vector_full.transpose(1, 2, 0, 3).reshape(12 * D)
    up_full = pick(pair_two, 0, row_count, 4)
    down_full = pick(pair_two, 4 * row_count, down_count, 1)
    slim_start = 4 * row_count + down_count
    slim_pair = [
        part[:, :, slim_start:]
        .reshape(crops, layers, slim_rows, 6, DEC)
        .transpose(0, 1, 3, 2, 4)
        .reshape(crops, layers, 6 * slim_rows, DEC)
        for part in pair_two
    ]
    lift_full = pick(slim_pair, 0, row_count, 8)
    first_start = 8 * row_count
    second_start = first_start + first_count
    first_full = (
        pick(slim_pair, first_start, first_count, 1)
        .reshape(slab_count, -1, DEC)[:, : convolve_one.shape[0]]
        .reshape(-1, DEC)
    )
    second_full = (
        pick(slim_pair, second_start, second_count, 1)
        .reshape(slab_count, -1, DEC)[:, : convolve_two.shape[0]]
        .reshape(-1, DEC)
    )
    vector_rows = vector_full.astype(jnp.float32).reshape(12, D)

    pieces = (CHANS * PATCH) // (block * crops)
    ct_size = PATCH // crops
    pixels = patches.reshape(rows_in, pieces, crops, block).transpose(2, 0, 1, 3)
    pixels = crop_swap(pixels.reshape(crops * rows_in, pieces * block))
    kinds_own = jnp.broadcast_to(modality.astype(jnp.float32)[:, None], (crop_batch, 128))
    kinds_all = jnp.concatenate([kinds_own[None]] * crops, 0)
    kinds_all = crop_swap(kinds_all).reshape(crops * crop_batch, 128)[:, :1]
    is_mri = (
        jnp.broadcast_to(kinds_all[:, :, None] > 0.5, (crops * crop_batch, local_tokens, 1))
        .reshape(-1, 1)
    )
    none = jnp.zeros((), jnp.bfloat16)
    pixel_rows = jnp.concatenate(
        [jnp.where(is_mri, none, pixels[:, :ct_size]), jnp.where(is_mri, pixels, none)], 1
    )
    partial = matmul(pixel_rows, embed_full).astype(jnp.bfloat16)
    partial = crop_swap(partial.reshape(crops, rows_in, D)).astype(jnp.float32)
    product = jnp.sum(partial, 0)
    own_mri = jnp.broadcast_to(
        (modality == 1)[:, None, None], (crop_batch, local_tokens, 1)
    ).reshape(-1, 1)
    embedded = (
        product
        + jnp.where(own_mri, vector_rows[7], vector_rows[6])
        + jnp.concatenate([position_rows] * crop_batch, 0)
    )
    normed_one, pull_one = jax.vjp(layer_norm, embedded, vector_rows[0], vector_rows[1])
    normed_one = normed_one.astype(jnp.bfloat16)
    triple = matmul(normed_one, triple_full).astype(jnp.bfloat16)
    triple = heads_out(triple.reshape(crop_batch, local_tokens, 3 * D), 3)
    query, keys, values = triple[..., :HDIM], triple[..., HDIM : 2 * HDIM], triple[..., 2 * HDIM :]
    scores = (
        jnp.einsum("pqd,pkd->pqk", query, keys, preferred_element_type=jnp.float32) * score_scale
    )
    probs = jax.nn.softmax(scores, axis=-1)
    probs_low = probs.astype(jnp.bfloat16)
    mixed = jnp.einsum("pqk,pkd->pqd", probs_low, values, preferred_element_type=jnp.float32)
    mixed = heads_back(mixed.astype(jnp.bfloat16), crop_batch, 1)
    hidden_one = embedded + matmul(mixed, output_full) + vector_rows[4]
    normed_two, pull_two = jax.vjp(layer_norm, hidden_one, vector_rows[2], vector_rows[3])
    normed_two = normed_two.astype(jnp.bfloat16)
    inner = matmul(normed_two, up_full) + vector_rows[8:].reshape(FF)
    activated = gelu_exact(inner).astype(jnp.bfloat16)
    hidden_two = hidden_one + matmul(activated, down_full) + vector_rows[5]
    hidden_low = hidden_two.astype(jnp.bfloat16)
    volume = to_volume(matmul(hidden_low, lift_full), crop_batch)
    joined = jnp.concatenate([volume.astype(jnp.bfloat16), skip_feats], -1)
    cols_one = columns(joined)
    conv_one = matmul(cols_one, first_full).reshape(volume.shape)
    normed_a, inverse_a = norm_forward(conv_one, voxel_count)
    first_act = gelu_exact(normed_a).astype(jnp.bfloat16)
    cols_two = columns(first_act)
    conv_two = matmul(cols_two, second_full).reshape(volume.shape)
    normed_b, inverse_b = norm_forward(conv_two, voxel_count)
    before = normed_b + volume
    block_output = gelu_exact(before).astype(jnp.bfloat16)

    grad_before = cotangent.astype(jnp.float32) * gelu_slope(before)
    grad_conv_two = norm_backward(grad_before, normed_b, inverse_b, voxel_count).astype(
        jnp.bfloat16
    )
    weight_second = matmul_left_t(cols_two, grad_conv_two.reshape(-1, DEC))
    grad_first = back_conv(grad_conv_two, second_full, DEC) * gelu_slope(normed_a)
    grad_conv_one = norm_backward(grad_first, normed_a, inverse_a, voxel_count).astype(
        jnp.bfloat16
    )
    weight_first = matmul_left_t(cols_one, grad_conv_one.reshape(-1, DEC))
    grad_joined = back_conv(grad_conv_one, first_full, 2 * DEC)
    skip_grad = grad_joined[..., DEC:].astype(jnp.bfloat16)
    grad_lifted = to_tokens(grad_before + grad_joined[..., :DEC]).astype(jnp.bfloat16)
    weight_lift = matmul_left_t(hidden_low, grad_lifted)
    grad_hidden = matmul_right_t(grad_lifted, lift_full)
    bias_down = jnp.sum(grad_hidden, 0)
    grad_branch = grad_hidden.astype(jnp.bfloat16)
    weight_down = matmul_left_t(activated, grad_branch)
    grad_inner = matmul_right_t(grad_branch, down_full) * gelu_slope(inner)
    bias_up = jnp.sum(grad_inner, 0)
    grad_inner_low = grad_inner.astype(jnp.bfloat16)
    weight_up = matmul_left_t(normed_two, grad_inner_low)

    def slab_pad(full, target):
        shaped = full.reshape(slab_count, -1, full.shape[1])
        return jnp.pad(shaped, ((0, 0), (0, target - shaped.shape[1]), (0, 0))).reshape(
            -1, full.shape[1]
        )

    slim_pack = jnp.concatenate(
        [
            to_pack(weight_lift.astype(jnp.bfloat16), 8),
            to_pack(slab_pad(weight_first.astype(jnp.bfloat16), crops * first_count), 1),
            to_pack(slab_pad(weight_second.astype(jnp.bfloat16), crops * second_count), 1),
        ],
        3,
    )
    slim_pack = jnp.pad(
        slim_pack, ((0, 0),) * 3 + ((0, 6 * slim_rows - slim_pack.shape[3]), (0, 0))
    )
    slim_pack = (
        slim_pack.reshape(layers, 2, crops, 6, slim_rows, DEC)
        .transpose(0, 1, 2, 4, 3, 5)
        .reshape(layers, 2, crops, slim_rows, D)
    )
    sum_two = scatter_pack(
        jnp.concatenate(
            [
                to_pack(weight_up.astype(jnp.bfloat16), 4),
                to_pack(weight_down.astype(jnp.bfloat16), 1),
                slim_pack,
            ],
            3,
        )
    )

    back_two = pull_two(matmul_right_t(grad_inner_low, up_full))
    grad_hidden = grad_hidden + back_two[0]
    bias_out = jnp.sum(grad_hidden, 0)
    grad_branch = grad_hidden.astype(jnp.bfloat16)
    weight_out = matmul_left_t(mixed, grad_branch)
    grad_mixed = matmul_right_t(grad_branch, output_full).astype(jnp.bfloat16)
    grad_mixed = heads_out(grad_mixed.reshape(crop_batch, local_tokens, D), 1)
    grad_probs = jnp.einsum(
        "pqd,pkd->pqk", grad_mixed, values, preferred_element_type=jnp.float32
    )
    centre = jnp.sum(probs * grad_probs, -1, keepdims=True)
    grad_scores = (probs * (grad_probs - centre)).astype(jnp.bfloat16)
    grad_query = (
        jnp.einsum("pqk,pkd->pqd", grad_scores, keys, preferred_element_type=jnp.float32)
        * score_scale
    )
    grad_keys = (
        jnp.einsum("pqk,pqd->pkd", grad_scores, query, preferred_element_type=jnp.float32)
        * score_scale
    )
    grad_values = jnp.einsum(
        "pqk,pqd->pkd", probs_low, grad_mixed, preferred_element_type=jnp.float32
    )
    grad_triple = jnp.concatenate([grad_query, grad_keys, grad_values], -1).astype(jnp.bfloat16)
    grad_triple = heads_back(grad_triple, crop_batch, 3)
    weight_triple = matmul_left_t(normed_one, grad_triple)
    back_one = pull_one(matmul_right_t(grad_triple, triple_full))
    grad_hidden = grad_hidden + back_one[0]
    grad_low = grad_hidden.astype(jnp.bfloat16)

    grad_rows = crop_stack(grad_low).reshape(crops * rows_in, D)
    weight_embed = matmul_left_t(pixel_rows, grad_rows).astype(jnp.bfloat16)
    embed_sum = lax.psum_scatter(weight_embed, SLAB, scatter_dimension=0, tiled=True)
    pixel_grad = matmul_right_t(grad_rows, embed_full)
    ct_grad = jnp.pad(pixel_grad[:, :ct_size], ((0, 0), (0, (CHANS - 1) * ct_size)))
    pixel_grad = jnp.where(is_mri, pixel_grad[:, ct_size:], ct_grad).astype(jnp.bfloat16)
    pixel_grad = crop_swap(pixel_grad).reshape(crops, rows_in, pieces, block)
    patch_grad = pixel_grad.transpose(1, 2, 0, 3).reshape(patches.shape)

    bias_ct = jnp.sum(jnp.where(own_mri, 0.0, grad_hidden), 0)
    bias_mri = jnp.sum(jnp.where(own_mri, grad_hidden, 0.0), 0)
    position_grad = jnp.sum(grad_hidden.reshape(crop_batch, local_tokens, D), 0)
    vector_grad = jnp.concatenate(
        [
            jnp.stack(
                [
                    back_one[1],
                    back_one[2],
                    back_two[1],
                    back_two[2],
                    bias_out,
                    bias_down,
                    bias_ct,
                    bias_mri,
                ]
            ),
            bias_up.reshape(4, D),
        ],
        0,
    ).astype(jnp.bfloat16)
    vector_pack = vector_grad.reshape(crops, layers, 2, 1, vector_size).transpose(1, 2, 0, 3, 4)
    vector_pack = jnp.pad(vector_pack, ((0, 0),) * 3 + ((0, 7), (0, D - vector_size)))
    sum_one = scatter_pack(
        jnp.concatenate(
            [
                to_pack(weight_triple.astype(jnp.bfloat16), 3),
                to_pack(weight_out.astype(jnp.bfloat16), 1),
                vector_pack,
            ],
            3,
        )
    )

    def by_units(rows, chunks):
        shaped = rows.reshape(chunks, -1, crops, unit).transpose(0, 2, 1, 3)
        return shaped.reshape(crops, -1, unit)

    def join_units(got, chunks):
        return (
            got.reshape(crops, chunks, -1, unit).transpose(0, 2, 1, 3).reshape(-1, chunks * unit)
        )

    embed_got = crop_swap(by_units(embed_sum, 1)).astype(jnp.float32)
    embed_grad = (
        embed_got.reshape(crops, groups, block, unit).transpose(1, 0, 2, 3).reshape(-1, unit)
    )
    wide_two = jnp.concatenate(
        [by_units(sum_two[: 4 * row_count], 4), by_units(sum_two[4 * row_count : slim_start], 1)], 1
    )
    wide_two = crop_swap(wide_two).astype(jnp.float32)
    up_grad = join_units(wide_two[:, : 4 * row_count], 4)
    down_grad = join_units(wide_two[:, 4 * row_count :], 1)
    slim_sum = (
        sum_two[slim_start:].reshape(slim_rows, 6, DEC).transpose(1, 0, 2).reshape(-1, DEC)
    )
    lift_sum = slim_sum[:first_start].reshape(8, row_count, DEC).transpose(1, 0, 2)
    lift_sum = lift_sum.reshape(row_count, crops, -1).transpose(1, 0, 2)
    lift_grad = crop_swap(lift_sum).astype(jnp.float32).reshape(upsample.shape)
    narrow_sum = slim_sum[first_start : second_start + second_count]
    narrow_sum = narrow_sum.reshape(-1, crops, DEC // crops).transpose(1, 0, 2)
    narrow_got = crop_swap(narrow_sum).astype(jnp.float32)
    first_grad = narrow_got[:, :first_count].reshape(-1, DEC // crops)[: convolve_one.shape[0]]
    second_grad = narrow_got[:, first_count:].reshape(-1, DEC // crops)[: convolve_two.shape[0]]
    wide_one = jnp.concatenate(
        [
            by_units(sum_one[: 3 * row_count], 3),
            by_units(sum_one[3 * row_count : 4 * row_count], 1),
            by_units(position_grad.astype(jnp.bfloat16), 1),
        ],
        1,
    )
    wide_one = crop_swap(wide_one).astype(jnp.float32)
    triple_grad = join_units(wide_one[:, : 3 * row_count], 3)
    output_grad = join_units(wide_one[:, 3 * row_count : 4 * row_count], 1)
    position_grad = jnp.sum(wide_one[:, 4 * row_count :], 0)
    vector_final = sum_one[4 * row_count, :vector_size].astype(jnp.float32)
    gradients = (
        embed_grad,
        triple_grad,
        output_grad,
        up_grad,
        down_grad,
        lift_grad,
        first_grad,
        second_grad,
        position_grad,
        vector_final,
    )
    local_sum = jnp.float32(0.0)
    for gradient in gradients:
        local_sum = local_sum + jnp.sum(gradient * gradient)
    grad_norm = jnp.sqrt(crop_sum(slab_sum(local_sum.reshape(1, 1))))[0, 0]
    factor = jnp.minimum(1.0, CLIP / grad_norm)
    news, means, squares = ([], [], [])
    for weight, gradient, mean_old, square_old, step_rate, step_decay in zip(
        shards, gradients, means_in, squares_in, step_rates, step_decays
    ):
        weight_new, mean_new, square_new = adam_update(
            weight, gradient, mean_old, square_old, factor, step_rate, step_decay
        )
        news.append(weight_new)
        means.append(mean_new)
        squares.append(square_new)
    return (
        block_output,
        patch_grad,
        skip_grad,
        grad_norm,
        news[0],
        news[1],
        news[2],
        news[3],
        news[4],
        news[5],
        news[6],
        news[7],
        news[8],
        news[9],
        means[0],
        means[1],
        means[2],
        means[3],
        means[4],
        means[5],
        means[6],
        means[7],
        means[8],
        means[9],
        squares[0],
        squares[1],
        squares[2],
        squares[3],
        squares[4],
        squares[5],
        squares[6],
        squares[7],
        squares[8],
        squares[9],
    )


def solution(mesh):
    crops, slabs = mesh.devices.shape
    mesh = Mesh(mesh.devices.reshape(crops, slabs // 2, 2), ("crop", "z", "core"))
    return jax.shard_map(
        local,
        mesh=mesh,
        in_specs=(
            P("crop", ("z", "core"), None, None),
            P("crop"),
            P("crop", ("z", "core"), None, None, None),
            P("crop", ("z", "core"), None, None, None),
            P(("z", "core"), "crop"),
            P(("z", "core"), "crop"),
            P(("z", "core"), "crop"),
            P(("z", "core"), "crop"),
            P(("z", "core"), "crop"),
            P(("z", "core"), "crop"),
            P(("z", "core"), "crop"),
            P(("z", "core"), "crop"),
            P(("z", "core"), "crop"),
            P(("crop", "z", "core")),
            P(("z", "core"), "crop"),
            P(("z", "core"), "crop"),
            P(("z", "core"), "crop"),
            P(("z", "core"), "crop"),
            P(("z", "core"), "crop"),
            P(("z", "core"), "crop"),
            P(("z", "core"), "crop"),
            P(("z", "core"), "crop"),
            P(("z", "core"), "crop"),
            P(("crop", "z", "core")),
            P(("z", "core"), "crop"),
            P(("z", "core"), "crop"),
            P(("z", "core"), "crop"),
            P(("z", "core"), "crop"),
            P(("z", "core"), "crop"),
            P(("z", "core"), "crop"),
            P(("z", "core"), "crop"),
            P(("z", "core"), "crop"),
            P(("z", "core"), "crop"),
            P(("crop", "z", "core")),
        ),
        out_specs=(
            P("crop", ("z", "core"), None, None, None),
            P("crop", ("z", "core"), None, None),
            P("crop", ("z", "core"), None, None, None),
            P(),
            P(("z", "core"), "crop"),
            P(("z", "core"), "crop"),
            P(("z", "core"), "crop"),
            P(("z", "core"), "crop"),
            P(("z", "core"), "crop"),
            P(("z", "core"), "crop"),
            P(("z", "core"), "crop"),
            P(("z", "core"), "crop"),
            P(("z", "core"), "crop"),
            P(("crop", "z", "core")),
            P(("z", "core"), "crop"),
            P(("z", "core"), "crop"),
            P(("z", "core"), "crop"),
            P(("z", "core"), "crop"),
            P(("z", "core"), "crop"),
            P(("z", "core"), "crop"),
            P(("z", "core"), "crop"),
            P(("z", "core"), "crop"),
            P(("z", "core"), "crop"),
            P(("crop", "z", "core")),
            P(("z", "core"), "crop"),
            P(("z", "core"), "crop"),
            P(("z", "core"), "crop"),
            P(("z", "core"), "crop"),
            P(("z", "core"), "crop"),
            P(("z", "core"), "crop"),
            P(("z", "core"), "crop"),
            P(("z", "core"), "crop"),
            P(("z", "core"), "crop"),
            P(("crop", "z", "core")),
        ),
        check_vma=False,
    )
```

time: 2580 us -> 980 us (0.38)
  waiting for transfers between devices: 1440 us -> 277 us
  blocking collectives: 353 us -> 23.9 us
  matrix products: 227 us -> 97 us
  starting transfers between devices: 32.3 us -> 138 us
  local copies, waits for them, and re-layouts: 371 us -> 274 us
    all_gather x24 -> x2, waiting for transfers between devices: 741 us -> 0.01 us  [the longest x1 0.01 us: gather_pack(): own = crop_stack(lax.all_gather(pack, 'z', axis=0))]
    reduce_scatter x11 -> x3, waiting for transfers between devices: 606 us -> 0.04 us  [the longest x2 0.02 us: scatter_pack(): return lax.psum_scatter(pack, 'z', scatter_dimension=0, tiled=False)]
    all_gather x14 -> x1, blocking collectives: 212 us -> 23.9 us  [gather_pack(): own = crop_stack(lax.all_gather(pack, 'z', axis=0))]
    ppermute x16 -> x49, waiting for transfers between devices: 0.82 us -> 173 us  [the longest x10 69.7 us: halve(): got = lax.ppermute(send, axis[0], axis[1])]
    another operation x9 -> x22, local copies, waits for them, and re-layouts: 166 us -> 25.4 us  [the longest x10 17 us: pick(): both = jnp.stack([part[:, :, start:start + rows * chunks] for part in pair])]
    all_to_all x0 -> x16, waiting for transfers between devices: none -> 103 us  [the longest x12 80.6 us: crop_swap(): return lax.all_to_all(pieces, 'crop', 0, 0, tiled=True)]
    psum x5 -> x0, blocking collectives: 99.1 us -> none  [the longest x4 61.4 us: slab_totals(): lax.psum((jnp.sum(first, (1, 2, 3)), jnp.sum(second, (1, 2, 3))), 'slab')]
    unnamed x51 -> x5, waiting for transfers between devices: 90.6 us -> 0.08 us
  transfers between devices with their start and end apart: 59 -> 70, of which waited for: 21 -> 42; matrix products, arithmetic and copies ran while one was open for 26% -> 38% of each run, Pallas kernels for 0% -> 0%
where the time goes in v1:
time: 980 us; the launch traced here: 967 us
  waiting for transfers between devices  277 us (28%)
  local copies, waits for them, and re-layouts  274 us (28%)
  starting transfers between devices  138 us (14%)
  other arithmetic  128 us (13%)
  matrix products  97 us (10%)
  between operations  28.8 us (3%)
  blocking collectives  23.9 us (2%)
    all_to_all x12, waiting for transfers between devices, crop_swap(): return lax.all_to_all(pieces, 'crop', 0, 0, tiled=True)  80.6 us
    ppermute x10, waiting for transfers between devices, halve(): got = lax.ppermute(send, axis[0], axis[1])  69.7 us
    all_to_all x12, starting transfers between devices, crop_swap(): return lax.all_to_all(pieces, 'crop', 0, 0, tiled=True)  47.9 us
    unnamed x382, local copies, waits for them, and re-layouts  47 us
    dot_general x8, matrix products, matmul_left_t(): lax.dot_general(left, right, CONTRACT_ROWS, preferred_element_type=jnp.fl...  38.6 us
    dot_general x10, matrix products, matmul(): return jnp.dot(left, right, preferred_element_type=jnp.float32)  32 us
    ppermute x3, waiting for transfers between devices, crop_stack(): lax.ppermute(jnp.stack([upper, upper_x]), 'crop', flip_pairs(4, 2))  30.2 us
    ppermute x3, waiting for transfers between devices, crop_stack(): lax.ppermute(jnp.stack([lower, lower_y]), 'crop', flip_pairs(4, 1))  24.7 us
  transfers between devices with their start and end apart: 70, of which 42 were waited for; matrix products, arithmetic and copies ran while one was open for 38% of the time, Pallas kernels for 0%

profile of v1, /device:TPU:0, one launch (start us, length us, event | category | flops | bytes accessed | tf_op | source)
XLA Modules:
  0.0 967.1 jit_solution(6691842057709883087)
XLA Ops:
  42.9 16.4 %all-to-all-done.2 = bf16[4,992,192]{1,2,0:T(8,128)(2,1)S(1)} async-done(((bf16[4,992,192]{1,2,0:T(8,128)(2,1)}), bf16[4,992,192]{1,2,0:T(8,128)(2,1)S(1)}, u32[]{:S(2)}, u32[]{:S(2)}) %all-to-all-start.2) | async-done | bytes 1523744 | tf_op jit(solution)/shard_map/all_to_all | solution.py:87
  62.8 23.9 %all-gather = bf16[416,768]{1,0:T(8,128)(2,1)S(1)} all-gather(bf16[104,768]{1,0:T(8,128)(2,1)S(1)} %fusion.123), channel_id=2, replica_groups=mesh['crop'=4,'z'=4,'core'=2] {'z'}, dimensions={0}, use_global_device_ids=true | all-gather | bytes 798720 | tf_op jit(solution)/shard_map/all_gather | solution.py:113
  90.8 7.7 reshape.663
  103.4 7.3 all_to_all.93
  114.8 6.4 collective-permute-done.1
  128.8 6.1 collective-permute-done.3
  138.7 7.6 collective-permute-done.6
  168.7 19.7 %collective-permute-done.7 = bf16[2,2,280,768]{3,2,0,1:T(8,128)(2,1)} collective-permute-done((bf16[2,2,280,768]{3,2,0,1:T(8,128)(2,1)}, bf16[2,2,280,768]{3,2,0,1:T(8,128)(2,1)}, u32[]{:S(2)}, u32[]{:S(2)}) %collective-permute-start.7) | collective-permute-done | bytes 1720352 | tf_op jit(solution)/shard_map/ppermute | solution.py:100
  190.6 24.1 %collective-permute-done.8 = bf16[2,2,280,768]{3,2,0,1:T(8,128)(2,1)} collective-permute-done((bf16[2,2,280,768]{3,2,0,1:T(8,128)(2,1)}, bf16[2,2,280,768]{3,2,0,1:T(8,128)(2,1)}, u32[]{:S(2)}, u32[]{:S(2)}) %collective-permute-start.8) | collective-permute-done | bytes 1720352 | tf_op jit(solution)/shard_map/ppermute | solution.py:99
  248.8 10.1 %fusion.53 = bf16[512,768]{1,0:T(8,128)(2,1)} fusion(bf16[5120,768]{0,1:T(8,128)(2,1)} %all-gather.5.cloned.1.call-done, bf16[512,4096]{1,0:T(8,128)(2,1)} %broadcast_select_fusion.2, bf16[512,1024]{1,0:T(8,128)(2,1)S(1)} %copy-done.68), kind=kOutput, calls=%fused_computation.129 | convolution fusion | flops 4037410816 | bytes 13893632 | tf_op jit(solution)/shard_map/dot_general | solution.py:50
  289.0 8.7 broadcast_select_fusion.1
  368.0 7.7 fusion.37
  485.4 10.2 %fusion.6 = bf16[6912,128]{1,0:T(8,128)(2,1)} fusion(bf16[2,2,16,16,6912]{4,3,2,1,0:T(8,128)(2,1)} %copy-done.96, bf16[2,2,16,16,128]{4,3,2,1,0:T(8,128)(2,1)S(1)} %multiply_convert_fusion.1), kind=kOutput, calls=%fused_computation.12 | convolution fusion | flops 1812824064 | bytes 16187392 | tf_op jit(solution)/shard_map/dot_general | solution.py:54
  519.3 7.4 all-to-all-start.8
  532.2 9.7 %reshape.730 = bf16[4,2,4,24,4,768]{5,4,3,2,1,0:T(4,128)(2,1)} reshape(bf16[768,3072]{1,0:T(8,128)(2,1)} %convolution_convert_fusion.2) | data formatting | bytes 9437184 | tf_op jit(solution)/shard_map/reshape | solution.py:129
  578.0 22.6 %all-to-all-done.9 = bf16[3,512,192]{2,0,1:T(4,128)(2,1)} async-done(((bf16[3,512,192]{2,0,1:T(4,128)(2,1)}), bf16[3,512,192]{2,0,1:T(4,128)(2,1)}, u32[]{:S(2)}, u32[]{:S(2)}) %all-to-all-start.9) | async-done | bytes 589856 | tf_op jit(solution)/shard_map/all_to_all | solution.py:227
  642.8 9.4 fusion.1
  666.1 46.4 %collective-permute-done.37 = bf16[4,2,52,768]{3,0,2,1:T(4,128)(2,1)S(1)} collective-permute-done((bf16[4,2,52,768]{3,0,2,1:T(4,128)(2,1)S(1)}, bf16[4,2,52,768]{3,0,2,1:T(4,128)(2,1)S(1)}, u32[]{:S(2)}, u32[]{:S(2)}) %collective-permute-start.37) | collective-permute-done | bytes 639008 | tf_op jit(solution)/shard_map/ppermute | solution.py:136
  731.9 10.1 %collective-permute-done.43 = bf16[4,140,768]{2,0,1:T(4,128)(2,1)} collective-permute-done((bf16[4,140,768]{2,0,1:T(4,128)(2,1)}, bf16[4,140,768]{2,0,1:T(4,128)(2,1)}, u32[]{:S(2)}, u32[]{:S(2)}) %collective-permute-start.43) | collective-permute-done | bytes 860192 | tf_op jit(solution)/shard_map/ppermute | solution.py:136
  762.6 10.2 %convolution_convert_fusion = bf16[5120,768]{1,0:T(8,128)(2,1)} fusion(bf16[512,768]{1,0:T(8,128)(2,1)S(1)} %bitcast.619, bf16[512,4096]{1,0:T(8,128)(2,1)} %broadcast_select_fusion.2, bf16[512,1024]{1,0:T(8,128)(2,1)S(1)} %copy-done.69), kind=kOutput, calls=%fused_computation.11 | convolution fusion | flops 4040949760 | bytes 13893632 | tf_op jit(solution)/shard_map/dot_general | solution.py:54
  772.8 7.7 fusion.207
  791.1 39.8 %all-to-all-done.10 = bf16[4,128,4096]{2,1,0:T(8,128)(2,1)} async-done(((bf16[4,128,4096]{2,1,0:T(8,128)(2,1)}), bf16[4,128,4096]{2,1,0:T(8,128)(2,1)}, u32[]{:S(2)}, u32[]{:S(2)}) %all-to-all-start.10) | async-done | bytes 4194336 | tf_op jit(solution)/shard_map/all_to_all | solution.py:87
  834.4 7.4 copy.763
  841.9 7.8 reshape.713
  (904 shorter events, 603.7 us)
Async XLA Ops:
  38.0 21.3 %all-to-all-start.2 = ((bf16[4,992,192]{1,2,0:T(8,128)(2,1)}), bf16[4,992,192]{1,2,0:T(8,128)(2,1)S(1)}, u32[]{:S(2)}, u32[]{:S(2)}) async-start(bf16[4,992,192]{1,2,0:T(8,128)(2,1)} %copy.588), calls=%async_computation.2 | async-start | bytes 3145728 | tf_op jit(solution)/shard_map/all_to_all | solution.py:87
  41.6 82.5 %all-gather.7.cloned.1.call-start = ((), (), s32[]{:S(2)}) async-start(), calls=%async_computation.23 | async-start | bytes 2150400 | tf_op jit(solution)/shard_map/all_gather | solution.py:113
  60.9 187.9 %all-gather.5.cloned.1.call-start = ((), (), s32[]{:S(2)}) async-start(), calls=%async_computation.19 | async-start | bytes 8847360 | tf_op jit(solution)/shard_map/all_gather | solution.py:401
  86.8 27.1 %collective-permute-start = (bf16[2,104,768]{2,1,0:T(8,128)(2,1)S(1)}, bf16[2,104,768]{2,1,0:T(8,128)(2,1)S(1)}, u32[]{:S(2)}, u32[]{:S(2)}) collective-permute-start(bf16[2,104,768]{2,1,0:T(8,128)(2,1)S(1)} %bitcast.589), channel_id=1, source_target_pairs={{0,8},{8,0},{16,24},{24,16},{1,9},{9,1},{17,25},{25,17},{2,10},{10... | collective-permute-start | bytes 958472 | tf_op jit(solution)/shard_map/ppermute | solution.py:97
  87.5 66.8 %all-to-all-start = ((f32[4,2,128]{2,1,0:T(2,128)}), f32[4,2,128]{2,1,0:T(2,128)S(1)}, u32[]{:S(2)}, u32[]{:S(2)}) async-start(f32[4,2,128]{2,1,0:T(2,128)} %concatenate.117), calls=%async_computation | async-start | bytes 8192 | tf_op jit(solution)/shard_map/all_to_all | solution.py:87
  128.2 21.7 %collective-permute-start.5 = (bf16[2,280,768]{2,1,0:T(8,128)(2,1)S(1)}, bf16[2,280,768]{2,1,0:T(8,128)(2,1)S(1)}, u32[]{:S(2)}, u32[]{:S(2)}) collective-permute-start(bf16[2,280,768]{2,1,0:T(8,128)(2,1)S(1)} %bitcast.554), channel_id=1, source_target_pairs={{0,8},{8,0},{16,24},{24,16},{1,9},{9,1},{17,25},{25,17},{2,10},{10... | collective-permute-start | bytes 2580488 | tf_op jit(solution)/shard_map/ppermute | solution.py:97
  147.6 40.8 %collective-permute-start.7 = (bf16[2,2,280,768]{3,2,0,1:T(8,128)(2,1)}, bf16[2,2,280,768]{3,2,0,1:T(8,128)(2,1)}, u32[]{:S(2)}, u32[]{:S(2)}) collective-permute-start(bf16[2,2,280,768]{3,2,0,1:T(8,128)(2,1)} %pad_maximum_fusion.7), channel_id=1, source_target_pairs={{0,8},{8,0},{16,24},{24,16},{1,9},{9,1},{17,25},{25,17},{2,10},{10... | collective-permute-start | bytes 5160968 | tf_op jit(solution)/shard_map/ppermute | solution.py:100
  151.4 63.3 %collective-permute-start.8 = (bf16[2,2,280,768]{3,2,0,1:T(8,128)(2,1)}, bf16[2,2,280,768]{3,2,0,1:T(8,128)(2,1)}, u32[]{:S(2)}, u32[]{:S(2)}) collective-permute-start(bf16[2,2,280,768]{3,2,0,1:T(8,128)(2,1)} %pad_maximum_fusion.8), channel_id=1, source_target_pairs={{0,16},{8,24},{16,0},{24,8},{1,17},{9,25},{17,1},{25,9},{2,18},{10... | collective-permute-start | bytes 5160968 | tf_op jit(solution)/shard_map/ppermute | solution.py:99
  154.3 72.8 %all-to-all-start.1 = ((bf16[4,128,4096]{2,1,0:T(8,128)(2,1)}), bf16[4,128,4096]{2,1,0:T(8,128)(2,1)}, u32[]{:S(2)}, u32[]{:S(2)}) async-start(bf16[4,128,4096]{2,1,0:T(8,128)(2,1)} %all_to_all.93), calls=%async_computation.1 | async-start | bytes 8388608 | tf_op jit(solution)/shard_map/all_to_all | solution.py:87
  162.3 71.7 %collective-permute-start.4 = (bf16[4,4,104,768]{3,1,0,2:T(4,128)(2,1)S(1)}, bf16[4,4,104,768]{3,1,0,2:T(4,128)(2,1)}, u32[]{:S(2)}, u32[]{:S(2)}) collective-permute-start(bf16[4,4,104,768]{3,1,0,2:T(4,128)(2,1)S(1)} %copy_dynamic-update-slice_fusion), channel_id=1, source_target_pairs={{0,1},{1,0},{2,3},{3,2},{4,5},{5,4},{6,7},{7,6},{8,9},{9,8},{10,11... | collective-permute-start | bytes 7667720 | tf_op jit(solution)/shard_map/ppermute | solution.py:114
  222.0 67.0 %collective-permute-start.9 = (bf16[4,4,280,768]{3,2,0,1:T(8,128)(2,1)}, bf16[4,4,280,768]{3,2,0,1:T(8,128)(2,1)}, u32[]{:S(2)}, u32[]{:S(2)}) collective-permute-start(bf16[4,4,280,768]{3,2,0,1:T(8,128)(2,1)} %slice_dynamic-update-slice_fusion), channel_id=1, source_target_pairs={{0,1},{1,0},{2,3},{3,2},{4,5},{5,4},{6,7},{7,6},{8,9},{9,8},{10,11... | collective-permute-start | bytes 20643848 | tf_op jit(solution)/shard_map/ppermute | solution.py:114
  284.6 51.7 %all-to-all-start.4 = ((bf16[24,64,192]{2,1,0:T(8,128)(2,1)}), bf16[24,64,192]{2,1,0:T(8,128)(2,1)}, u32[]{:S(2)}, u32[]{:S(2)}) async-start(bf16[24,64,192]{2,1,0:T(8,128)(2,1)} %copy.606), calls=%async_computation.4 | async-start | bytes 1572864 | tf_op jit(solution)/shard_map/all_to_all | solution.py:223
  519.3 38.1 %all-to-all-start.8 = ((bf16[8,2,6144]{2,1,0:T(2,128)(2,1)}), bf16[8,2,6144]{2,1,0:T(2,128)(2,1)S(1)}, u32[]{:S(2)}, u32[]{:S(2)}) async-start(bf16[8,2,6144]{2,1,0:T(2,128)(2,1)} %reshape.781), calls=%async_computation.8 | async-start | bytes 393216 | tf_op jit(solution)/shard_map/all_to_all | solution.py:223
  556.9 85.8 %collective-permute-start.39 = (bf16[4,4,280,768]{3,2,1,0:T(8,128)(2,1)}, bf16[4,4,280,768]{3,2,1,0:T(8,128)(2,1)}, u32[]{:S(2)}, u32[]{:S(2)}) collective-permute-start(bf16[4,4,280,768]{3,2,1,0:T(8,128)(2,1)} %dynamic-slice_bitcast_fusion), channel_id=1, source_target_pairs={{0,1},{1,0},{2,3},{3,2},{4,5},{5,4},{6,7},{7,6},{8,9},{9,8},{10,11... | collective-permute-start | bytes 20643848 | tf_op jit(solution)/shard_map/ppermute | solution.py:136
  569.1 31.5 %all-to-all-start.9 = ((bf16[3,512,192]{2,0,1:T(4,128)(2,1)}), bf16[3,512,192]{2,0,1:T(4,128)(2,1)}, u32[]{:S(2)}, u32[]{:S(2)}) async-start(bf16[3,512,192]{2,0,1:T(4,128)(2,1)} %copy.655), calls=%async_computation.9 | async-start | bytes 2097152 | tf_op jit(solution)/shard_map/all_to_all | solution.py:227
  573.9 275.8 %reduce-scatter.6.cloned.1.call-start = ((), (), s32[]{:S(2)}) async-start(), calls=%async_computation.21 | async-start | bytes 798720 | tf_op jit(solution)/shard_map/reduce_scatter | solution.py:157
  641.4 22.7 %collective-permute-start.35 = (bf16[4,2,52,768]{3,0,2,1:T(4,128)(2,1)S(1)}, bf16[4,2,52,768]{3,0,2,1:T(4,128)(2,1)S(1)}, u32[]{:S(2)}, u32[]{:S(2)}) collective-permute-start(bf16[4,2,52,768]{3,0,2,1:T(4,128)(2,1)S(1)} %bitcast.630), channel_id=1, source_target_pairs={{0,16},{8,24},{16,0},{24,8},{1,17},{9,25},{17,1},{25,9},{2,18},{10... | collective-permute-start | bytes 1916936 | tf_op jit(solution)/shard_map/ppermute | solution.py:136
  658.3 62.2 %collective-permute-start.42 = (bf16[4,2,140,768]{3,0,2,1:T(4,128)(2,1)S(1)}, bf16[4,2,140,768]{3,0,2,1:T(4,128)(2,1)S(1)}, u32[]{:S(2)}, u32[]{:S(2)}) collective-permute-start(bf16[4,2,140,768]{3,0,2,1:T(4,128)(2,1)S(1)} %bitcast.596), channel_id=1, source_target_pairs={{0,8},{8,0},{16,24},{24,16},{1,9},{9,1},{17,25},{25,17},{2,10},{10... | collective-permute-start | bytes 5160968 | tf_op jit(solution)/shard_map/ppermute | solution.py:136
  660.3 52.2 %collective-permute-start.37 = (bf16[4,2,52,768]{3,0,2,1:T(4,128)(2,1)S(1)}, bf16[4,2,52,768]{3,0,2,1:T(4,128)(2,1)S(1)}, u32[]{:S(2)}, u32[]{:S(2)}) collective-permute-start(bf16[4,2,52,768]{3,0,2,1:T(4,128)(2,1)S(1)} %dynamic-slice_bitcast_fusion.4), channel_id=1, source_target_pairs={{0,8},{8,0},{16,24},{24,16},{1,9},{9,1},{17,25},{25,17},{2,10},{10... | collective-permute-start | bytes 1916936 | tf_op jit(solution)/shard_map/ppermute | solution.py:136
  663.3 61.1 %collective-permute-start.40 = (bf16[4,2,140,768]{3,0,2,1:T(4,128)(2,1)S(1)}, bf16[4,2,140,768]{3,0,2,1:T(4,128)(2,1)S(1)}, u32[]{:S(2)}, u32[]{:S(2)}) collective-permute-start(bf16[4,2,140,768]{3,0,2,1:T(4,128)(2,1)S(1)} %bitcast.597), channel_id=1, source_target_pairs={{0,16},{8,24},{16,0},{24,8},{1,17},{9,25},{17,1},{25,9},{2,18},{10... | collective-permute-start | bytes 5160968 | tf_op jit(solution)/shard_map/ppermute | solution.py:136
  664.7 53.6 %collective-permute-start.36 = (bf16[4,52,768]{2,0,1:T(4,128)(2,1)S(1)}, bf16[4,52,768]{2,0,1:T(4,128)(2,1)S(1)}, u32[]{:S(2)}, u32[]{:S(2)}) collective-permute-start(bf16[4,52,768]{2,0,1:T(4,128)(2,1)S(1)} %dynamic-slice_bitcast_fusion.6), channel_id=1, source_target_pairs={{0,8},{8,0},{16,24},{24,16},{1,9},{9,1},{17,25},{25,17},{2,10},{10... | collective-permute-start | bytes 958472 | tf_op jit(solution)/shard_map/ppermute | solution.py:136
  730.2 125.8 %reduce-scatter.8.cloned.1.call-start = ((), (), s32[]{:S(2)}) async-start(), calls=%async_computation.22 | async-start | bytes 2150400 | tf_op jit(solution)/shard_map/reduce_scatter | solution.py:157
  749.6 132.9 %reduce-scatter.4.cloned.1.call-start = ((), (), s32[]{:S(2)}) async-start(), calls=%async_computation.20 | async-start | bytes 8847360 | tf_op jit(solution)/shard_map/reduce_scatter | solution.py:578
  783.9 47.1 %all-to-all-start.10 = ((bf16[4,128,4096]{2,1,0:T(8,128)(2,1)}), bf16[4,128,4096]{2,1,0:T(8,128)(2,1)}, u32[]{:S(2)}, u32[]{:S(2)}) async-start(bf16[4,128,4096]{2,1,0:T(8,128)(2,1)} %bitcast.521), calls=%async_computation.10 | async-start | bytes 8388608 | tf_op jit(solution)/shard_map/all_to_all | solution.py:87
  (183 other events, 1401.8 us)
Sparse Core Ops, SparseCore 0:
  61.0 44.9 all-gather.6
  107.6 75.9 all-gather.4
  730.3 19.8 reduce-scatter.5
  753.0 36.4 reduce-scatter.7
  791.8 83.7 reduce-scatter.3

commit v2 on v1

v2 whole, which is shorter than its diff:
```python
import math

import jax
import jax.numpy as jnp
from jax import lax
from jax.experimental import pallas as pl
from jax.experimental.pallas import tpu as pltpu
from jax.sharding import Mesh
from jax.sharding import PartitionSpec as P

D = 768
HEADS = 12
HDIM = 64
FF = 3072
PATCH = 4096
CHANS = 4
DEC = 128
SIDE = 8
STEP = 10


BETA_ONE = 0.9
BETA_TWO = 0.95
RATE = 0.07
DECAY = 0.05
VECTOR_RATE = 0.4
VECTOR_DECAY = 0.0
EPSILON = 1e-08
CLIP = 1.0
CONTRACT_ROWS = (((0,), (0,)), ((), ()))
CONTRACT_COLS = (((1,), (1,)), ((), ()))


def layer_norm(values, gain, shift):
    center = values - jnp.mean(values, -1, keepdims=True)
    spread = jnp.mean(center * center, -1, keepdims=True)
    return center * lax.rsqrt(spread + 1e-06) * gain + shift


def gelu_exact(values):
    return jax.nn.gelu(values, approximate=False)


def gelu_slope(values):
    return (
        0.5 * (1.0 + lax.erf(values * 0.7071067811865476))
        + values * jnp.exp(-0.5 * values * values) * 0.3989422804014327
    )


def matmul(left, right):
    return jnp.dot(left, right, preferred_element_type=jnp.float32)


def matmul_left_t(left, right):
    return lax.dot_general(left, right, CONTRACT_ROWS, preferred_element_type=jnp.float32)


def matmul_right_t(left, right):
    return lax.dot_general(left, right, CONTRACT_COLS, preferred_element_type=jnp.float32)


SLAB = ("z", "core")
SWAP = [(0, 1), (1, 0)]


def flip_pairs(count, step):
    return [(i, i ^ step) for i in range(count)]


def slab_sum(values):
    values = values + lax.ppermute(values, "core", SWAP)
    count, step = lax.axis_size("z"), 1
    while step < count:
        values = values + lax.ppermute(values, "z", flip_pairs(count, step))
        step *= 2
    return values


def crop_swap(pieces):
    return lax.all_to_all(pieces, "crop", 0, 0, tiled=True)


def flips(value, axis):
    count = lax.axis_size(axis)
    return [value] + [
        lax.ppermute(value, axis, flip_pairs(count, shift)) for shift in range(1, count)
    ]


def flips_of(pieces, axis):
    count = lax.axis_size(axis)
    return [pieces[0]] + [
        lax.ppermute(pieces[shift], axis, flip_pairs(count, shift)) for shift in range(1, count)
    ]


def total_of(pieces):
    total = pieces[0].astype(jnp.float32)
    for piece in pieces[1:]:
        total = total + piece.astype(jnp.float32)
    return total


def moves(plan, inputs, outputs):
    place = jnp.stack([lax.axis_index("crop"), lax.axis_index("core")]).astype(jnp.int32)

    def kernel(place_ref, *refs):
        crop, core = place_ref[0], place_ref[1]
        sources, targets = refs[: len(inputs)], refs[len(inputs) : -1]
        copies = [
            pltpu.make_async_copy(
                sources[source].at[from_index(crop, core)],
                targets[target].at[to_index(crop, core)],
                refs[-1].at[number],
            )
            for number, (source, from_index, target, to_index) in enumerate(plan)
        ]
        for copy in copies:
            copy.start()
        for copy in copies:
            copy.wait()

    size = sum(math.prod(shape) for shape in outputs)
    return pl.pallas_call(
        kernel,
        in_specs=[pl.BlockSpec(memory_space=pltpu.SMEM)]
        + [pl.BlockSpec(memory_space=pl.ANY)] * len(inputs),
        out_specs=[pl.BlockSpec(memory_space=pltpu.VMEM)] * len(outputs),
        out_shape=[jax.ShapeDtypeStruct(shape, jnp.bfloat16) for shape in outputs],
        scratch_shapes=[pltpu.SemaphoreType.DMA((len(plan),))],
        compiler_params=pltpu.CompilerParams(vmem_limit_bytes=4 * size + 2**22),
        cost_estimate=pl.CostEstimate(flops=0, transcendentals=0, bytes_accessed=4 * size),
    )(place, *inputs)


def chunk_at(spot, crop, core):
    kind, number, width = spot
    if kind == "row":
        return (slice(None), core, crop, number)
    return (slice(None), core, crop, slice(None), pl.ds(number * width, width))


def pack_at(number, lanes):
    if lanes is None:
        return (slice(None), number)
    return (slice(None), number, slice(None), pl.ds(lanes, DEC))


def gather_plan(spots):
    plan = []
    crops = lax.axis_size("crop")
    for side in range(2):
        for shift in range(crops):
            for number, lanes, target, spot in spots:
                plan.append(
                    (
                        side * crops + shift,
                        lambda crop, core, number=number, lanes=lanes: pack_at(number, lanes),
                        target,
                        lambda crop, core, side=side, shift=shift, spot=spot: chunk_at(
                            spot, crop ^ shift, core ^ side
                        ),
                    )
                )
    return plan


def core_swap(pieces):
    return [lax.ppermute(piece, "core", SWAP) for piece in pieces]


def scatter_plan(spots):
    plan = []
    for side in range(2):
        for shift in range(lax.axis_size("crop")):
            for number, lanes, source, spot in spots:
                plan.append(
                    (
                        source,
                        lambda crop, core, side=side, shift=shift, spot=spot: chunk_at(
                            spot, crop ^ shift, core ^ side
                        ),
                        side,
                        lambda crop, core, shift=shift, number=number, lanes=lanes: (shift,)
                        + pack_at(number, lanes),
                    )
                )
    return plan


def scatter_cores(weights, spots, chunks):
    crops, layers = lax.axis_size("crop"), lax.axis_size("z")
    shape = (crops, layers, chunks, weights[0].shape[3], D)
    return moves(scatter_plan(spots), weights, [shape, shape])


def core_sum(keep, send):
    got = lax.ppermute(send, "core", SWAP)
    return [
        (keep[shift].astype(jnp.float32) + got[shift].astype(jnp.float32)).astype(jnp.bfloat16)
        for shift in range(keep.shape[0])
    ]


def row_pad(rows, count):
    return jnp.pad(rows, ((0, count - rows.shape[0]), (0, 0)))


def slab_trim(full, piece, size):
    layers, cores, crops = full.shape[:3]
    rows = full.reshape(layers * cores, crops, -1, DEC)[:, :, :piece]
    return rows.reshape(layers * cores, -1, DEC)[:, :size].reshape(-1, DEC)


def slab_fill(full, piece, chunks, rows):
    layers, crops = lax.axis_size("z"), lax.axis_size("crop")
    shaped = full.reshape(2 * layers, -1, DEC)
    shaped = jnp.pad(shaped, ((0, 0), (0, crops * piece - shaped.shape[1]), (0, 0)))
    shaped = shaped.reshape(2 * layers, crops, piece, DEC)
    shaped = jnp.pad(shaped, ((0, 0), (0, 0), (0, chunks * rows - piece), (0, 0)))
    return shaped.reshape(layers, 2, crops, chunks, rows, DEC)


def to_units(rows, unit):
    crops, size = rows.shape[0], rows.shape[1] * rows.shape[2]
    flat = jnp.pad(rows.reshape(crops, size), ((0, 0), (0, -size % unit)))
    return flat.reshape(crops, -1, unit)


def from_units(units, rows, width):
    return units.reshape(units.shape[0], -1)[:, : rows * width].reshape(-1, rows, width)


def after(value, earlier):
    return lax.optimization_barrier((value, earlier))[0]


def z_scatter(pack):
    return lax.psum_scatter(pack, "z", scatter_dimension=0, tiled=False)


def neighbours(volume):
    count = lax.axis_size(SLAB)
    forward = [(i, i + 1) for i in range(count - 1)]
    backward = [(target, source) for source, target in forward]
    low = lax.ppermute(volume[:, -1:], SLAB, forward)
    high = lax.ppermute(volume[:, :1], SLAB, backward)
    return low, high


def with_planes(volume, rims):
    low, high = rims
    return jnp.concatenate([low.astype(volume.dtype), volume, high.astype(volume.dtype)], axis=1)


def inside(rimmed):
    place, last = lax.axis_index(SLAB), lax.axis_size(SLAB) - 1
    plane = lax.broadcasted_iota(jnp.int32, rimmed.shape, 1)
    outside = ((plane == 0) & (place == 0)) | (
        (plane == rimmed.shape[1] - 1) & (place == last)
    )
    return jnp.where(outside, jnp.zeros((), rimmed.dtype), rimmed)


def columns(rimmed):
    padded = jnp.pad(rimmed, ((0, 0), (0, 0), (1, 1), (1, 1), (0, 0)))
    crop_count, layers, breadth = (rimmed.shape[0], rimmed.shape[1] - 2, rimmed.shape[2])
    pieces = [
        padded[
            :,
            shift_z : shift_z + layers,
            shift_y : shift_y + breadth,
            shift_x : shift_x + breadth,
            :,
        ]
        for shift_z in range(3)
        for shift_y in range(3)
        for shift_x in range(3)
    ]
    return jnp.concatenate(pieces, -1).reshape(crop_count * layers * breadth * breadth, -1)


def back_conv(grad_rimmed, kernel, inputs):
    outputs = kernel.shape[1]
    flipped = (
        kernel.reshape(27, inputs, outputs)[::-1].transpose(0, 2, 1).reshape(27 * outputs, inputs)
    )
    crop_count, planes, breadth = grad_rimmed.shape[:3]
    return matmul(columns(grad_rimmed), flipped).reshape(
        crop_count, planes - 2, breadth, breadth, inputs
    )


def slab_totals(first, second):
    both = jnp.stack([jnp.sum(first, (1, 2, 3)), jnp.sum(second, (1, 2, 3))])
    return slab_sum(both)


def over_voxels(values):
    return values[:, None, None, None, :]


def norm_scales(values, voxel_count):
    totals = slab_totals(values, values * values)
    average = totals[0] / voxel_count
    inverse = lax.rsqrt(totals[1] / voxel_count - average * average + 1e-05)
    return over_voxels(average), over_voxels(inverse)


def norm_slopes(grad, normed, voxel_count):
    totals = slab_totals(grad, grad * normed)
    return over_voxels(totals[0] / voxel_count), over_voxels(totals[1] / voxel_count)


def heads_out(block, parts):
    crop_count, tokens = block.shape[0], block.shape[1]
    slab_count = lax.axis_size(SLAB)
    shaped = block.reshape(crop_count, tokens, parts, HEADS, HDIM).transpose(0, 3, 1, 2, 4)
    shaped = shaped.reshape(crop_count * HEADS, tokens, parts * HDIM)
    spare = -shaped.shape[0] % slab_count
    shaped = jnp.pad(shaped, ((0, spare), (0, 0), (0, 0)))
    return lax.all_to_all(shaped, SLAB, 0, 1, tiled=True)


def heads_back(block, crop_count, parts):
    shaped = lax.all_to_all(block, SLAB, 1, 0, tiled=True)[: crop_count * HEADS]
    tokens = shaped.shape[1]
    shaped = shaped.reshape(crop_count, HEADS, tokens, parts, HDIM).transpose(0, 2, 3, 1, 4)
    return shaped.reshape(crop_count * tokens, parts * D)


def to_volume(lifted, crop_count):
    layers = lifted.shape[0] // (crop_count * SIDE * SIDE)
    shaped = lifted.reshape(crop_count, layers, SIDE, SIDE, 2, 2, 2, DEC)
    return shaped.transpose(0, 1, 4, 2, 5, 3, 6, 7).reshape(
        crop_count, 2 * layers, 2 * SIDE, 2 * SIDE, DEC
    )


def to_tokens(volume):
    crop_count, layers = (volume.shape[0], volume.shape[1] // 2)
    shaped = volume.reshape(crop_count, layers, 2, SIDE, 2, SIDE, 2, DEC)
    return shaped.transpose(0, 1, 3, 5, 2, 4, 6, 7).reshape(
        crop_count * layers * SIDE * SIDE, 8 * DEC
    )


def adam_update(weight, gradient, mean_old, square_old, factor, step_rate, step_decay):
    clipped = gradient * factor
    mean_new = BETA_ONE * mean_old + (1.0 - BETA_ONE) * clipped
    square_new = BETA_TWO * square_old + (1.0 - BETA_TWO) * clipped * clipped
    direction = (
        mean_new
        / (1.0 - BETA_ONE**STEP)
        / (jnp.sqrt(square_new / (1.0 - BETA_TWO**STEP)) + EPSILON)
    )
    return (weight - step_rate * (direction + step_decay * weight), mean_new, square_new)


def local(
    patches,
    modality,
    skip_feats,
    cotangent,
    embedding,
    attention_in,
    attention_out,
    expand_up,
    expand_down,
    upsample,
    convolve_one,
    convolve_two,
    positions,
    vectors,
    embedding_mean,
    attention_in_mean,
    attention_out_mean,
    expand_up_mean,
    expand_down_mean,
    upsample_mean,
    convolve_one_mean,
    convolve_two_mean,
    positions_mean,
    vectors_mean,
    embedding_square,
    attention_in_square,
    attention_out_square,
    expand_up_square,
    expand_down_square,
    upsample_square,
    convolve_one_square,
    convolve_two_square,
    positions_square,
    vectors_square,
):
    shards = (
        embedding,
        attention_in,
        attention_out,
        expand_up,
        expand_down,
        upsample,
        convolve_one,
        convolve_two,
        positions,
        vectors,
    )
    means_in = (
        embedding_mean,
        attention_in_mean,
        attention_out_mean,
        expand_up_mean,
        expand_down_mean,
        upsample_mean,
        convolve_one_mean,
        convolve_two_mean,
        positions_mean,
        vectors_mean,
    )
    squares_in = (
        embedding_square,
        attention_in_square,
        attention_out_square,
        expand_up_square,
        expand_down_square,
        upsample_square,
        convolve_one_square,
        convolve_two_square,
        positions_square,
        vectors_square,
    )
    step_rates = (RATE,) * 9 + (VECTOR_RATE,)
    step_decays = (DECAY,) * 9 + (VECTOR_DECAY,)
    crops = lax.axis_size("crop")
    layers = lax.axis_size("z")
    slab_count = 2 * layers
    crop_batch = patches.shape[0]
    local_tokens = patches.shape[1] * patches.shape[2]
    rows_in = crop_batch * local_tokens
    voxel_count = skip_feats.shape[1] * skip_feats.shape[2] * skip_feats.shape[3] * slab_count
    score_scale = HDIM ** (-0.5)
    unit = D // crops

    lows = [entry.astype(jnp.bfloat16) for entry in shards]
    embed_rows = embedding.shape[0]
    share = embed_rows // crops
    block = math.gcd(share, PATCH)
    groups = share // block
    row_count = attention_in.shape[0] // crops
    down_count = expand_down.shape[0] // crops
    embed_wide = (
        lows[0].reshape(groups, crops, block, unit).transpose(1, 0, 2, 3).reshape(crops, share, unit)
    )
    first_count = -(-convolve_one.shape[0] // crops)
    second_count = -(-convolve_two.shape[0] // crops)
    narrow = jnp.concatenate(
        [
            jnp.pad(lows[6], ((0, crops * first_count - lows[6].shape[0]), (0, 0))).reshape(
                crops, first_count, -1
            ),
            jnp.pad(lows[7], ((0, crops * second_count - lows[7].shape[0]), (0, 0))).reshape(
                crops, second_count, -1
            ),
        ],
        1,
    )
    up_rows = expand_up.shape[0]
    class_size = FF // crops
    per_class = class_size // crops
    up_units = lows[3].reshape(up_rows, -1, crops, down_count).transpose(2, 0, 1, 3)
    up_units = to_units(up_units.reshape(crops, up_rows, per_class), unit)
    lift_units = to_units(lows[5].reshape(crops, row_count, -1), unit)
    narrow_units = to_units(narrow, unit)
    wide = jnp.concatenate(
        [
            lows[1].reshape(crops, row_count, 3, unit).transpose(0, 2, 1, 3).reshape(crops, -1, unit),
            lows[2].reshape(crops, row_count, unit),
            up_units,
            lows[4].reshape(crops, down_count, unit),
            jnp.broadcast_to(lows[8][None], (crops,) + lows[8].shape),
            lift_units,
            narrow_units,
        ],
        1,
    )
    pieces = (CHANS * PATCH) // (block * crops)
    ct_size = PATCH // crops
    own_crop = lax.axis_index("crop")
    own_mri = jnp.broadcast_to(
        (modality == 1)[:, None, None], (crop_batch, local_tokens, 1)
    ).reshape(-1, 1)
    marks = jnp.broadcast_to(own_mri.astype(jnp.float32), (rows_in, 128))
    is_mri = jnp.concatenate(flips(marks, "crop"), 0)[:, :1] > 0.5
    pixels = patches.reshape(rows_in, pieces, crops, block).transpose(2, 0, 1, 3)
    pixels = pixels.reshape(crops, rows_in, pieces * block)
    pixels = [
        lax.dynamic_index_in_dim(pixels, own_crop ^ shift, 0, keepdims=False)
        for shift in range(crops)
    ]
    pixel_parts = flips_of(pixels, "crop")
    wide = crop_swap(after(wide, is_mri))
    embed_part = crop_swap(after(embed_wide, (wide, pixels)))
    embed_part = embed_part.transpose(1, 0, 2).reshape(share, D)
    marks = []
    edge = 0
    for size in (3 * row_count, row_count, up_units.shape[1], down_count, lows[8].shape[0],
                 lift_units.shape[1], narrow_units.shape[1]):
        marks.append(wide[:, edge : edge + size])
        edge += size
    lift_rows = from_units(marks[5], row_count, 8 * DEC // crops)
    narrow = from_units(marks[6], first_count + second_count, DEC // crops)
    triple_part = marks[0].reshape(3, crops, row_count, unit).transpose(0, 2, 1, 3).reshape(-1, D)
    output_part = marks[1].transpose(1, 0, 2).reshape(row_count, D)
    up_part = from_units(marks[2], up_rows, per_class).transpose(1, 0, 2).reshape(-1, D)
    down_part = marks[3].transpose(1, 0, 2).reshape(down_count, D)
    position_rows = marks[4].transpose(1, 0, 2).reshape(-1, D).astype(jnp.float32)
    lift_part = (
        lift_rows.transpose(1, 0, 2).reshape(row_count, 8, DEC).transpose(1, 0, 2).reshape(-1, DEC)
    )
    narrow_part = narrow.transpose(1, 0, 2).reshape(-1, DEC)
    first_chunks, second_chunks = -(-first_count // row_count), -(-second_count // row_count)
    slim = jnp.concatenate(
        [
            lift_part,
            row_pad(narrow_part[:first_count], first_chunks * row_count),
            row_pad(narrow_part[first_count:], second_chunks * row_count),
        ],
        0,
    )
    slim_chunks = -(-(8 + first_chunks + second_chunks) // 6)
    slim = row_pad(slim, 6 * slim_chunks * row_count)
    slim = slim.reshape(slim_chunks, 6, row_count, DEC).transpose(0, 2, 1, 3).reshape(-1, D)
    vector_size = vectors.shape[0]
    vector_part = jnp.pad(lows[9][None], ((0, row_count - 1), (0, D - vector_size)))

    quarter = 6
    packs = jnp.concatenate([triple_part, output_part, vector_part, slim], 0)
    packs = lax.all_gather(packs.reshape(-1, row_count, D), "z", axis=0)
    packs = after(packs, pixel_parts)
    pack_one, pack_slim = packs[:, :5], packs[:, 5:]
    embed_full = lax.all_gather(embed_part, SLAB, axis=0, tiled=True)
    up_size = up_part.shape[0]
    ff_part = after(jnp.concatenate([up_part, down_part], 0), embed_full)
    ff_full = lax.all_gather(ff_part, SLAB, axis=0)
    up_full = ff_full[:, :up_size].reshape(D, class_size)
    down_full = ff_full[:, up_size:].reshape(class_size, D)
    one_spots = [
        (0, None, 0, ("lane", 0, D)),
        (1, None, 0, ("lane", 1, D)),
        (2, None, 0, ("lane", 2, D)),
        (3, None, 1, ("lane", 0, D)),
        (4, None, 2, ("lane", 0, D)),
    ]
    slim_list = [(0, ("lane", k, DEC)) for k in range(8)]
    slim_list += [(1, ("row", k, DEC)) for k in range(first_chunks)]
    slim_list += [(2, ("row", k, DEC)) for k in range(second_chunks)]
    slim_spots = [
        (number // quarter, number % quarter * DEC, target, spot)
        for number, (target, spot) in enumerate(slim_list)
    ]
    lead = (layers, 2, crops)
    none = jnp.zeros((), jnp.bfloat16)
    one_own = flips(pack_one, "crop")
    pixels = jnp.concatenate(after(pixel_parts, one_own), 0)
    pixel_rows = jnp.concatenate(
        [jnp.where(is_mri, none, pixels[:, :ct_size]), jnp.where(is_mri, pixels, none)], 1
    )
    partial = matmul(pixel_rows, embed_full).astype(jnp.bfloat16).reshape(crops, rows_in, D)
    product = total_of(flips_of(list(partial), "crop"))
    one_other = core_swap(after(one_own, partial))
    triple_full, output_full, vector_full = moves(
        gather_plan(one_spots),
        one_own + one_other,
        [lead + (row_count, 3 * D), lead + (row_count, D), lead + (row_count, D)],
    )
    triple_full = triple_full.reshape(D, 3 * D)
    output_full = output_full.reshape(D, D)
    vector_full = vector_full[:, :, :, 0, :vector_size].transpose(2, 0, 1, 3).reshape(12 * D)
    vector_rows = vector_full.astype(jnp.float32).reshape(12, D)
    embedded = (
        product
        + jnp.where(own_mri, vector_rows[7], vector_rows[6])
        + jnp.concatenate([position_rows] * crop_batch, 0)
    )
    normed_one, pull_one = jax.vjp(layer_norm, embedded, vector_rows[0], vector_rows[1])
    normed_one = normed_one.astype(jnp.bfloat16)
    triple = matmul(normed_one, triple_full).astype(jnp.bfloat16)
    triple = heads_out(triple.reshape(crop_batch, local_tokens, 3 * D), 3)
    query, keys, values = triple[..., :HDIM], triple[..., HDIM : 2 * HDIM], triple[..., 2 * HDIM :]
    scores = (
        jnp.einsum("pqd,pkd->pqk", query, keys, preferred_element_type=jnp.float32) * score_scale
    )
    probs = jax.nn.softmax(scores, axis=-1)
    probs_low = probs.astype(jnp.bfloat16)
    mixed = jnp.einsum("pqk,pkd->pqd", probs_low, values, preferred_element_type=jnp.float32)
    slim_own = flips(pack_slim, "crop")
    mixed = after(mixed.astype(jnp.bfloat16), slim_own)
    mixed = heads_back(mixed, crop_batch, 1)
    slim_other = core_swap(slim_own)
    hidden_one = embedded + matmul(mixed, output_full) + vector_rows[4]
    hidden_one = after(hidden_one, slim_other)
    lift_full, first_full, second_full = moves(
        gather_plan(slim_spots),
        slim_own + slim_other,
        [
            lead + (row_count, 8 * DEC),
            lead + (first_chunks, row_count, DEC),
            lead + (second_chunks, row_count, DEC),
        ],
    )
    lift_full = lift_full.reshape(D, 8 * DEC)
    first_full = slab_trim(first_full, first_count, convolve_one.shape[0])
    second_full = slab_trim(second_full, second_count, convolve_two.shape[0])
    normed_two, pull_two = jax.vjp(layer_norm, hidden_one, vector_rows[2], vector_rows[3])
    normed_two = normed_two.astype(jnp.bfloat16)
    normed_all = jnp.concatenate(flips(normed_two, "crop"), 0)
    bias_class = vector_rows[8:].reshape(slab_count, crops, down_count)
    bias_class = lax.dynamic_index_in_dim(bias_class, own_crop, 1, keepdims=False).reshape(-1)
    inner = matmul(normed_all, up_full) + bias_class
    activated = gelu_exact(inner).astype(jnp.bfloat16)
    partial = matmul(activated, down_full).astype(jnp.bfloat16).reshape(crops, rows_in, D)
    product = total_of(flips_of(list(partial), "crop"))
    hidden_two = hidden_one + product + vector_rows[5]
    hidden_low = hidden_two.astype(jnp.bfloat16)
    volume = to_volume(matmul(hidden_low, lift_full), crop_batch)
    joined = jnp.concatenate([volume.astype(jnp.bfloat16), skip_feats], -1)
    joined = with_planes(joined, neighbours(joined))
    volume_rimmed = with_planes(
        volume, (joined[:, :1, ..., :DEC], joined[:, -1:, ..., :DEC])
    )
    target_rimmed = with_planes(cotangent, neighbours(cotangent)).astype(jnp.float32)
    cols_one = columns(joined)
    conv_one = matmul(cols_one, first_full).reshape(volume.shape)
    conv_one_rimmed = with_planes(conv_one, neighbours(conv_one.astype(jnp.bfloat16)))
    average_a, inverse_a = norm_scales(conv_one, voxel_count)
    normed_a = (conv_one_rimmed - average_a) * inverse_a
    first_act = inside(gelu_exact(normed_a).astype(jnp.bfloat16))
    cols_two = columns(first_act)
    conv_two = matmul(cols_two, second_full).reshape(volume.shape)
    conv_two_rimmed = with_planes(conv_two, neighbours(conv_two.astype(jnp.bfloat16)))
    average_b, inverse_b = norm_scales(conv_two, voxel_count)
    normed_b = (conv_two_rimmed - average_b) * inverse_b
    before = normed_b + volume_rimmed
    block_output = gelu_exact(before[:, 1:-1]).astype(jnp.bfloat16)

    grad_before = target_rimmed * gelu_slope(before)
    mean_b, slope_b = norm_slopes(grad_before[:, 1:-1], normed_b[:, 1:-1], voxel_count)
    grad_conv_two = inverse_b * (grad_before - mean_b - normed_b * slope_b)
    grad_conv_two = inside(grad_conv_two.astype(jnp.bfloat16))
    weight_second = matmul_left_t(cols_two, grad_conv_two[:, 1:-1].reshape(-1, DEC))
    grad_first = back_conv(grad_conv_two, second_full, DEC) * gelu_slope(normed_a[:, 1:-1])
    grad_first_rimmed = with_planes(grad_first, neighbours(grad_first.astype(jnp.bfloat16)))
    mean_a, slope_a = norm_slopes(grad_first, normed_a[:, 1:-1], voxel_count)
    grad_conv_one = inverse_a * (grad_first_rimmed - mean_a - normed_a * slope_a)
    grad_conv_one = inside(grad_conv_one.astype(jnp.bfloat16))
    weight_first = matmul_left_t(cols_one, grad_conv_one[:, 1:-1].reshape(-1, DEC))
    grad_joined = back_conv(grad_conv_one, first_full, 2 * DEC)
    skip_grad = grad_joined[..., DEC:].astype(jnp.bfloat16)
    grad_lifted = to_tokens(grad_before[:, 1:-1] + grad_joined[..., :DEC]).astype(jnp.bfloat16)
    weight_lift = matmul_left_t(hidden_low, grad_lifted)
    grad_hidden = matmul_right_t(grad_lifted, lift_full)
    bias_down = jnp.sum(grad_hidden, 0)
    grad_branch = grad_hidden.astype(jnp.bfloat16)
    grad_all = jnp.concatenate(flips(grad_branch, "crop"), 0)
    grad_inner = matmul_right_t(grad_all, down_full) * gelu_slope(inner)
    bias_up = jnp.sum(grad_inner, 0)
    grad_inner_low = grad_inner.astype(jnp.bfloat16)
    partial = matmul_right_t(grad_inner_low, up_full).astype(jnp.bfloat16)
    partial = partial.reshape(crops, rows_in, D)
    weight_down = matmul_left_t(activated, grad_all).astype(jnp.bfloat16)
    weight_up = matmul_left_t(normed_all, grad_inner_low).astype(jnp.bfloat16)
    ff_grads = jnp.concatenate(
        [weight_up.reshape(slab_count, -1, D), weight_down.reshape(slab_count, -1, D)], 1
    )

    slim_move = scatter_cores(
        [
            weight_lift.astype(jnp.bfloat16).reshape(lead + (row_count, 8 * DEC)),
            slab_fill(weight_first.astype(jnp.bfloat16), first_count, first_chunks, row_count),
            slab_fill(weight_second.astype(jnp.bfloat16), second_count, second_chunks, row_count),
        ],
        slim_spots,
        slim_chunks,
    )
    slim_parts = core_sum(*slim_move)
    partial = after(partial, slim_move[1])
    back_two = pull_two(total_of(flips_of(list(partial), "crop")))
    grad_hidden = grad_hidden + back_two[0]
    bias_out = jnp.sum(grad_hidden, 0)
    grad_branch = grad_hidden.astype(jnp.bfloat16)
    weight_out = matmul_left_t(mixed, grad_branch)
    grad_mixed = matmul_right_t(grad_branch, output_full).astype(jnp.bfloat16)
    grad_mixed = after(grad_mixed, slim_parts)
    slim_got = flips_of(slim_parts, "crop")
    grad_mixed = heads_out(grad_mixed.reshape(crop_batch, local_tokens, D), 1)
    grad_probs = jnp.einsum(
        "pqd,pkd->pqk", grad_mixed, values, preferred_element_type=jnp.float32
    )
    centre = jnp.sum(probs * grad_probs, -1, keepdims=True)
    grad_scores = (probs * (grad_probs - centre)).astype(jnp.bfloat16)
    grad_query = (
        jnp.einsum("pqk,pkd->pqd", grad_scores, keys, preferred_element_type=jnp.float32)
        * score_scale
    )
    grad_keys = (
        jnp.einsum("pqk,pqd->pkd", grad_scores, query, preferred_element_type=jnp.float32)
        * score_scale
    )
    grad_values = jnp.einsum(
        "pqk,pqd->pkd", probs_low, grad_mixed, preferred_element_type=jnp.float32
    )
    grad_triple = jnp.concatenate([grad_query, grad_keys, grad_values], -1).astype(jnp.bfloat16)
    grad_triple = heads_back(grad_triple, crop_batch, 3)
    grad_triple = after(grad_triple, slim_got)
    ff_grads = after(ff_grads, grad_triple)
    ff_sum = lax.psum_scatter(ff_grads, SLAB, scatter_dimension=0, tiled=False)
    weight_triple = matmul_left_t(normed_one, grad_triple)
    back_one = pull_one(matmul_right_t(grad_triple, triple_full))
    grad_hidden = grad_hidden + back_one[0]
    grad_low = grad_hidden.astype(jnp.bfloat16)

    grad_rows = jnp.concatenate(flips(grad_low, "crop"), 0)
    weight_embed = matmul_left_t(pixel_rows, grad_rows).astype(jnp.bfloat16)
    slim_sum = total_of(after(slim_got, weight_embed)).astype(jnp.bfloat16)
    embed_sum = lax.psum_scatter(weight_embed, SLAB, scatter_dimension=0, tiled=True)
    pixel_grad = matmul_right_t(after(grad_rows, weight_embed), embed_full)
    ct_grad = jnp.pad(pixel_grad[:, :ct_size], ((0, 0), (0, (CHANS - 1) * ct_size)))
    pixel_grad = jnp.where(is_mri, pixel_grad[:, ct_size:], ct_grad).astype(jnp.bfloat16)
    pixel_got = flips_of(list(pixel_grad.reshape(crops, rows_in, pieces * block)), "crop")
    pixel_got = jnp.stack(pixel_got)
    patch_grad = jnp.stack(
        [
            lax.dynamic_index_in_dim(pixel_got, own_crop ^ part, 0, keepdims=False)
            for part in range(crops)
        ]
    )
    patch_grad = patch_grad.reshape(crops, rows_in, pieces, block).transpose(1, 2, 0, 3)
    patch_grad = patch_grad.reshape(patches.shape)

    bias_ct = jnp.sum(jnp.where(own_mri, 0.0, grad_hidden), 0)
    bias_mri = jnp.sum(jnp.where(own_mri, grad_hidden, 0.0), 0)
    position_grad = jnp.sum(grad_hidden.reshape(crop_batch, local_tokens, D), 0)
    at_class = lax.broadcasted_iota(jnp.int32, (slab_count, crops, down_count), 1) == own_crop
    bias_full = jnp.where(at_class, bias_up.reshape(slab_count, 1, down_count), 0.0)
    vector_grad = jnp.concatenate(
        [
            jnp.stack(
                [
                    back_one[1],
                    back_one[2],
                    back_two[1],
                    back_two[2],
                    bias_out,
                    bias_down,
                    bias_ct,
                    bias_mri,
                ]
            ),
            bias_full.reshape(4, D),
        ],
        0,
    ).astype(jnp.bfloat16)
    vector_pack = vector_grad.reshape(crops, layers, 2, 1, vector_size).transpose(1, 2, 0, 3, 4)
    vector_pack = jnp.pad(
        vector_pack, ((0, 0),) * 3 + ((0, row_count - 1), (0, D - vector_size))
    )
    weight_triple = after(weight_triple.astype(jnp.bfloat16), weight_embed)
    one_parts = core_sum(*scatter_cores(
        [
            weight_triple.reshape(lead + (row_count, 3 * D)),
            weight_out.astype(jnp.bfloat16).reshape(lead + (row_count, D)),
            vector_pack,
        ],
        one_spots,
        5,
    ))
    one_sum = total_of(flips_of(one_parts, "crop")).astype(jnp.bfloat16)
    sums = jnp.concatenate([slim_sum, one_sum], 1)
    sums = z_scatter(after(sums, (embed_sum, pixel_grad)))
    sums = sums.reshape(-1, D)
    one_row = slim_chunks * row_count

    def by_units(rows, chunks):
        shaped = rows.reshape(chunks, -1, crops, unit).transpose(0, 2, 1, 3)
        return shaped.reshape(crops, -1, unit)

    def join_units(got, chunks):
        return (
            got.reshape(crops, chunks, -1, unit).transpose(0, 2, 1, 3).reshape(-1, chunks * unit)
        )

    embed_got = crop_swap(by_units(embed_sum, 1)).astype(jnp.float32)
    embed_grad = (
        embed_got.reshape(crops, groups, block, unit).transpose(1, 0, 2, 3).reshape(-1, unit)
    )
    sum_one = sums[one_row:]
    slim_all = sums[:one_row].reshape(slim_chunks, row_count, 6, DEC)
    slim_all = slim_all.transpose(0, 2, 1, 3).reshape(-1, DEC)
    first_start = 8 * row_count
    second_start = first_start + first_chunks * row_count
    lift_sum = slim_all[:first_start].reshape(8, row_count, DEC).transpose(1, 0, 2)
    lift_sum = lift_sum.reshape(row_count, crops, -1).transpose(1, 0, 2)
    narrow_sum = jnp.concatenate(
        [
            slim_all[first_start : first_start + first_count],
            slim_all[second_start : second_start + second_count],
        ],
        0,
    )
    narrow_sum = narrow_sum.reshape(-1, crops, DEC // crops).transpose(1, 0, 2)
    lift_units, narrow_units = to_units(lift_sum, unit), to_units(narrow_sum, unit)
    up_units = ff_sum[:up_size].reshape(up_rows, crops, per_class).transpose(1, 0, 2)
    up_units = to_units(up_units, unit)
    wide = jnp.concatenate(
        [
            up_units,
            by_units(ff_sum[up_size:], 1),
            by_units(sum_one[: 3 * row_count], 3),
            by_units(sum_one[3 * row_count : 4 * row_count], 1),
            by_units(position_grad.astype(jnp.bfloat16), 1),
            lift_units,
            narrow_units,
        ],
        1,
    )
    wide = crop_swap(wide).astype(jnp.float32)
    marks = []
    edge = 0
    for size in (up_units.shape[1], down_count, 3 * row_count, row_count, position_grad.shape[0],
                 lift_units.shape[1], narrow_units.shape[1]):
        marks.append(wide[:, edge : edge + size])
        edge += size
    up_grad = from_units(marks[0], up_rows, per_class)
    up_grad = up_grad.reshape(crops, up_rows, -1, down_count).transpose(1, 2, 0, 3)
    up_grad = up_grad.reshape(expand_up.shape)
    down_grad = join_units(marks[1], 1)
    triple_grad = join_units(marks[2], 3)
    output_grad = join_units(marks[3], 1)
    position_grad = jnp.sum(marks[4], 0)
    lift_grad = from_units(marks[5], row_count, 8 * DEC // crops).reshape(upsample.shape)
    narrow_got = from_units(marks[6], first_count + second_count, DEC // crops)
    first_grad = narrow_got[:, :first_count].reshape(-1, DEC // crops)[: convolve_one.shape[0]]
    second_grad = narrow_got[:, first_count:].reshape(-1, DEC // crops)[: convolve_two.shape[0]]
    vector_final = sum_one[4 * row_count, :vector_size].astype(jnp.float32)
    gradients = (
        embed_grad,
        triple_grad,
        output_grad,
        up_grad,
        down_grad,
        lift_grad,
        first_grad,
        second_grad,
        position_grad,
        vector_final,
    )
    local_sum = jnp.float32(0.0)
    for gradient in (embed_sum, ff_sum, lift_sum, narrow_sum, sum_one, position_grad):
        wide_grad = gradient.astype(jnp.float32)
        local_sum = local_sum + jnp.sum(wide_grad * wide_grad)
    grad_norm = jnp.sqrt(slab_sum(total_of(flips(local_sum.reshape(1, 1), "crop"))))[0, 0]
    factor = jnp.minimum(1.0, CLIP / grad_norm)
    news, means, squares = ([], [], [])
    for weight, gradient, mean_old, square_old, step_rate, step_decay in zip(
        shards, gradients, means_in, squares_in, step_rates, step_decays
    ):
        weight_new, mean_new, square_new = adam_update(
            weight, gradient, mean_old, square_old, factor, step_rate, step_decay
        )
        news.append(weight_new)
        means.append(mean_new)
        squares.append(square_new)
    return (
        block_output,
        patch_grad,
        skip_grad,
        grad_norm,
        news[0],
        news[1],
        news[2],
        news[3],
        news[4],
        news[5],
        news[6],
        news[7],
        news[8],
        news[9],
        means[0],
        means[1],
        means[2],
        means[3],
        means[4],
        means[5],
        means[6],
        means[7],
        means[8],
        means[9],
        squares[0],
        squares[1],
        squares[2],
        squares[3],
        squares[4],
        squares[5],
        squares[6],
        squares[7],
        squares[8],
        squares[9],
    )


def solution(mesh):
    crops, slabs = mesh.devices.shape
    mesh = Mesh(mesh.devices.reshape(crops, slabs // 2, 2), ("crop", "z", "core"))
    return jax.shard_map(
        local,
        mesh=mesh,
        in_specs=(
            P("crop", ("z", "core"), None, None),
            P("crop"),
            P("crop", ("z", "core"), None, None, None),
            P("crop", ("z", "core"), None, None, None),
            P(("z", "core"), "crop"),
            P(("z", "core"), "crop"),
            P(("z", "core"), "crop"),
            P(("z", "core"), "crop"),
            P(("z", "core"), "crop"),
            P(("z", "core"), "crop"),
            P(("z", "core"), "crop"),
            P(("z", "core"), "crop"),
            P(("z", "core"), "crop"),
            P(("crop", "z", "core")),
            P(("z", "core"), "crop"),
            P(("z", "core"), "crop"),
            P(("z", "core"), "crop"),
            P(("z", "core"), "crop"),
            P(("z", "core"), "crop"),
            P(("z", "core"), "crop"),
            P(("z", "core"), "crop"),
            P(("z", "core"), "crop"),
            P(("z", "core"), "crop"),
            P(("crop", "z", "core")),
            P(("z", "core"), "crop"),
            P(("z", "core"), "crop"),
            P(("z", "core"), "crop"),
            P(("z", "core"), "crop"),
            P(("z", "core"), "crop"),
            P(("z", "core"), "crop"),
            P(("z", "core"), "crop"),
            P(("z", "core"), "crop"),
            P(("z", "core"), "crop"),
            P(("crop", "z", "core")),
        ),
        out_specs=(
            P("crop", ("z", "core"), None, None, None),
            P("crop", ("z", "core"), None, None),
            P("crop", ("z", "core"), None, None, None),
            P(),
            P(("z", "core"), "crop"),
            P(("z", "core"), "crop"),
            P(("z", "core"), "crop"),
            P(("z", "core"), "crop"),
            P(("z", "core"), "crop"),
            P(("z", "core"), "crop"),
            P(("z", "core"), "crop"),
            P(("z", "core"), "crop"),
            P(("z", "core"), "crop"),
            P(("crop", "z", "core")),
            P(("z", "core"), "crop"),
            P(("z", "core"), "crop"),
            P(("z", "core"), "crop"),
            P(("z", "core"), "crop"),
            P(("z", "core"), "crop"),
            P(("z", "core"), "crop"),
            P(("z", "core"), "crop"),
            P(("z", "core"), "crop"),
            P(("z", "core"), "crop"),
            P(("crop", "z", "core")),
            P(("z", "core"), "crop"),
            P(("z", "core"), "crop"),
            P(("z", "core"), "crop"),
            P(("z", "core"), "crop"),
            P(("z", "core"), "crop"),
            P(("z", "core"), "crop"),
            P(("z", "core"), "crop"),
            P(("z", "core"), "crop"),
            P(("z", "core"), "crop"),
            P(("crop", "z", "core")),
        ),
        check_vma=False,
    )
```

time: 980 us -> 854 us (0.87)
  local copies, waits for them, and re-layouts: 274 us -> 201 us
  other arithmetic: 128 us -> 93.1 us
  waiting for transfers between devices: 277 us -> 253 us
  Pallas kernels: 0 us -> 13.5 us
    all_to_all x12 -> x3, waiting for transfers between devices: 80.6 us -> 13 us  [crop_swap(): return lax.all_to_all(pieces, 'crop', 0, 0, tiled=True)]
    ppermute x34 -> x62, starting transfers between devices: 42.3 us -> 82.4 us  [the longest x21 36.4 us: flips(): lax.ppermute(value, axis, flip_pairs(count, shift))]
    all_to_all x12 -> x3, starting transfers between devices: 47.9 us -> 12.2 us  [crop_swap(): return lax.all_to_all(pieces, 'crop', 0, 0, tiled=True)]
    ppermute x34 -> x62, waiting for transfers between devices: 150 us -> 180 us  [the longest x21 127 us: flips_of(): lax.ppermute(pieces[shift], axis, flip_pairs(count, shift))]
    all_to_all x0 -> x2, blocking collectives: none -> 29.2 us  [the longest x1 16.3 us: crop_swap(): return lax.all_to_all(pieces, 'crop', 0, 0, tiled=True)]
    reshape x18 -> x21, local copies, waits for them, and re-layouts: 48.5 us -> 23.1 us  [the longest x1 7.83 us: local(): patch_grad = patch_grad.reshape(patches.shape)]
    all_gather x1 -> x0, blocking collectives: 23.9 us -> none  [gather_pack(): own = crop_stack(lax.all_gather(pack, 'z', axis=0))]
    all_to_all x2 -> x1, waiting for transfers between devices: 0.01 us -> 20.5 us  [heads_out(): return lax.all_to_all(shaped, SLAB, 0, 1, tiled=True)]
  transfers between devices with their start and end apart: 70 -> 89, of which waited for: 42 -> 40; matrix products, arithmetic and copies ran while one was open for 38% -> 29% of each run, Pallas kernels for 0% -> 2%
where the time goes in v2:
time: 854 us; the launch traced here: 844 us
  waiting for transfers between devices  253 us (30%)
  local copies, waits for them, and re-layouts  201 us (24%)
  starting transfers between devices  137 us (16%)
  other arithmetic  93.1 us (11%)
  matrix products  90 us (11%)
  blocking collectives  29.2 us (3%)
  between operations  26.8 us (3%)
  Pallas kernels  13.5 us (2%)
    ppermute x21, waiting for transfers between devices, flips_of(): lax.ppermute(pieces[shift], axis, flip_pairs(count, shift))  127 us
    ppermute x21, waiting for transfers between devices, flips(): lax.ppermute(value, axis, flip_pairs(count, shift))  43.1 us
    unnamed x405, local copies, waits for them, and re-layouts  40 us
    ppermute x21, starting transfers between devices, flips(): lax.ppermute(value, axis, flip_pairs(count, shift))  36.4 us
    dot_general x10, matrix products, matmul(): return jnp.dot(left, right, preferred_element_type=jnp.float32)  32.5 us
    dot_general x8, matrix products, matmul_left_t(): lax.dot_general(left, right, CONTRACT_ROWS, preferred_element_type=jnp.fl...  29.8 us
    ppermute x21, starting transfers between devices, flips_of(): lax.ppermute(pieces[shift], axis, flip_pairs(count, shift))  25.5 us
    all_to_all x2, waiting for transfers between devices, heads_back(): shaped = lax.all_to_all(block, SLAB, 1, 0, tiled=True)[:crop_count * HEADS]  24.6 us
  transfers between devices with their start and end apart: 89, of which 40 were waited for; matrix products, arithmetic and copies ran while one was open for 29% of the time, Pallas kernels for 2%

profile of v2, /device:TPU:0, one launch (start us, length us, event | category | flops | bytes accessed | tf_op | source)
XLA Modules:
  0.0 843.6 jit_solution(4280317610367345703)
XLA Ops:
  31.7 10.0 %all-to-all-done = bf16[4,438,192]{1,2,0:T(8,128)(2,1)S(1)} async-done(((bf16[4,438,192]{1,2,0:T(8,128)(2,1)}), bf16[4,438,192]{1,2,0:T(8,128)(2,1)S(1)}, u32[]{:S(2)}, u32[]{:S(2)}) %all-to-all-start) | async-done | bytes 672800 | tf_op jit(solution)/shard_map/all_to_all | solution.py:81
  48.0 7.8 reshape.661
  60.7 7.3 reshape.662
  72.6 16.3 %all_to_all.86 = bf16[4,640,192]{1,2,0:T(8,128)(2,1)} all-to-all(bf16[4,640,192]{1,2,0:T(8,128)(2,1)S(1)} %copy.557), channel_id=1, replica_groups=mesh['crop'=4,'z'=4,'core'=2] {'crop'}, dimensions={0} | all-to-all | bytes 1966080 | tf_op jit(solution)/shard_map/all_to_all | solution.py:81
  92.9 23.8 %collective-permute-done.5 = bf16[128,4096]{1,0:T(8,128)(2,1)} collective-permute-done((bf16[128,4096]{1,0:T(8,128)(2,1)}, bf16[128,4096]{1,0:T(8,128)(2,1)}, u32[]{:S(2)}, u32[]{:S(2)}) %collective-permute-start.5) | collective-permute-done | bytes 1048608 | tf_op jit(solution)/shard_map/ppermute | solution.py:94
  116.8 19.1 %collective-permute-done.4 = bf16[128,4096]{1,0:T(8,128)(2,1)} collective-permute-done((bf16[128,4096]{1,0:T(8,128)(2,1)}, bf16[128,4096]{1,0:T(8,128)(2,1)}, u32[]{:S(2)}, u32[]{:S(2)}) %collective-permute-start.4) | collective-permute-done | bytes 1048608 | tf_op jit(solution)/shard_map/ppermute | solution.py:94
  144.8 12.6 %collective-permute-done.8.refs_3_ = bf16[4,5,24,768]{3,2,1,0:T(8,128)(2,1)S(1)} collective-permute-done((bf16[4,5,24,768]{3,2,1,0:T(8,128)(2,1)S(1)}, bf16[4,5,24,768]{3,2,1,0:T(8,128)(2,1)S(1)}, u32[]{:S(2)}, u32[]{:S(2)}) %collective-permute-start.8) | collective-permute-done | bytes 737312 | tf_op jit(solution)/shard_map/ppermute | solution.py:87
  157.5 14.3 %collective-permute-done.7.refs_2_ = bf16[4,5,24,768]{3,2,1,0:T(8,128)(2,1)S(1)} collective-permute-done((bf16[4,5,24,768]{3,2,1,0:T(8,128)(2,1)S(1)}, bf16[4,5,24,768]{3,2,1,0:T(8,128)(2,1)S(1)}, u32[]{:S(2)}, u32[]{:S(2)}) %collective-permute-start.7) | collective-permute-done | bytes 737312 | tf_op jit(solution)/shard_map/ppermute | solution.py:87
  189.1 9.1 %fusion.37 = bf16[512,768]{1,0:T(8,128)(2,1)S(1)} fusion(bf16[5120,768]{0,1:T(8,128)(2,1)} %all-gather.7.cloned.1.call-done, bf16[512,4096]{1,0:T(8,128)(2,1)} %broadcast_select_fusion, bf16[512,1024]{1,0:T(8,128)(2,1)} %slice_select_fusion.1), kind=kOutput, calls=%fused_computation.160 | convolution fusion | flops 4037410816 | bytes 13893632 | tf_op jit(solution)/shard_map/dot_general | solution.py:52
  231.0 20.5 %all-to-all-done.2 = bf16[24,64,192]{2,1,0:T(8,128)(2,1)S(1)} async-done(((bf16[24,64,192]{2,1,0:T(8,128)(2,1)}), bf16[24,64,192]{2,1,0:T(8,128)(2,1)S(1)}, u32[]{:S(2)}, u32[]{:S(2)}) %all-to-all-start.2) | async-done | bytes 589856 | tf_op jit(solution)/shard_map/all_to_all | solution.py:323
  300.0 6.1 fusion.20
  429.0 6.0 fusion.4
  449.7 8.9 %fusion.1 = bf16[6912,128]{1,0:T(8,128)(2,1)S(1)} fusion(bf16[2,2,16,16,6912]{4,3,2,1,0:T(8,128)(2,1)} %copy-done.101, bf16[2,4,16,16,128]{4,3,2,1,0:T(8,128)(2,1)S(1)} %fusion.93), kind=kOutput, calls=%fused_computation.3 | convolution fusion | flops 1812824064 | bytes 16187392 | tf_op jit(solution)/shard_map/dot_general | solution.py:56
  499.5 13.0 %all_to_all.87 = bf16[8,2,6144]{2,1,0:T(2,128)(2,1)S(1)} all-to-all(bf16[8,2,6144]{2,1,0:T(2,128)(2,1)S(1)} %reshape.758), channel_id=1, replica_groups=mesh['crop'=4,'z'=4,'core'=2] {'z','core'}, dimensions={0} | all-to-all | bytes 393216 | tf_op jit(solution)/shard_map/all_to_all | solution.py:323
  530.6 22.9 %all-to-all-done.5 = bf16[3,512,192]{2,0,1:T(4,128)(2,1)} async-done(((bf16[3,512,192]{2,0,1:T(4,128)(2,1)}), bf16[3,512,192]{2,0,1:T(4,128)(2,1)}, u32[]{:S(2)}, u32[]{:S(2)}) %all-to-all-start.5) | async-done | bytes 589856 | tf_op jit(solution)/shard_map/all_to_all | solution.py:327
  584.0 6.8 convolution_convert_fusion
  622.4 8.2 fusion.275
  644.5 10.7 %collective-permute-done.68 = bf16[4,5,24,768]{3,2,1,0:T(8,128)(2,1)S(1)} collective-permute-done((bf16[4,5,24,768]{3,2,1,0:T(8,128)(2,1)S(1)}, bf16[4,5,24,768]{3,2,1,0:T(8,128)(2,1)S(1)}, u32[]{:S(2)}, u32[]{:S(2)}) %collective-permute-start.68) | collective-permute-done | bytes 737312 | tf_op jit(solution)/shard_map/ppermute | solution.py:94
  662.5 9.7 %collective-permute-done.70 = bf16[4,5,24,768]{3,2,1,0:T(8,128)(2,1)} collective-permute-done((bf16[4,5,24,768]{3,2,1,0:T(8,128)(2,1)}, bf16[4,5,24,768]{3,2,1,0:T(8,128)(2,1)}, u32[]{:S(2)}, u32[]{:S(2)}) %collective-permute-start.70) | collective-permute-done | bytes 737312 | tf_op jit(solution)/shard_map/ppermute | solution.py:94
  672.2 24.7 %collective-permute-done.69 = bf16[4,5,24,768]{3,2,1,0:T(8,128)(2,1)} collective-permute-done((bf16[4,5,24,768]{3,2,1,0:T(8,128)(2,1)}, bf16[4,5,24,768]{3,2,1,0:T(8,128)(2,1)}, u32[]{:S(2)}, u32[]{:S(2)}) %collective-permute-start.69) | collective-permute-done | bytes 737312 | tf_op jit(solution)/shard_map/ppermute | solution.py:94
  700.4 18.0 %collective-permute-done.65 = bf16[128,4096]{1,0:T(8,128)(2,1)} collective-permute-done((bf16[128,4096]{1,0:T(8,128)(2,1)}, bf16[128,4096]{1,0:T(8,128)(2,1)}, u32[]{:S(2)}, u32[]{:S(2)}) %collective-permute-start.65) | collective-permute-done | bytes 1048608 | tf_op jit(solution)/shard_map/ppermute | solution.py:94
  723.9 7.4 copy.590
  731.4 7.8 reshape.707
  775.5 8.3 collective-permute-start.73
  (905 shorter events, 517.5 us)
Async XLA Ops:
  31.7 104.2 %all-gather.5.cloned.1.call-start = ((), (), s32[]{:S(2)}) async-start(), calls=%async_computation.11 | async-start | bytes 1658880 | tf_op jit(solution)/shard_map/all_gather | solution.py:539
  46.3 142.8 %all-gather.7.cloned.1.call-start = ((), (), s32[]{:S(2)}) async-start(), calls=%async_computation.12 | async-start | bytes 8847360 | tf_op jit(solution)/shard_map/all_gather | solution.py:542
  88.9 203.8 %all-gather.9.cloned.1.call-start = ((), (), s32[]{:S(2)}) async-start(), calls=%async_computation.16 | async-start | bytes 2654208 | tf_op jit(solution)/shard_map/all_gather | solution.py:545
  90.2 45.7 %collective-permute-start.4 = (bf16[128,4096]{1,0:T(8,128)(2,1)}, bf16[128,4096]{1,0:T(8,128)(2,1)}, u32[]{:S(2)}, u32[]{:S(2)}) collective-permute-start(bf16[128,4096]{1,0:T(8,128)(2,1)} %get-tuple-element.183), channel_id=1, source_target_pairs={{0,16},{8,24},{16,0},{24,8},{1,17},{9,25},{17,1},{25,9},{2,18},{10... | collective-permute-start | bytes 3145736 | tf_op jit(solution)/shard_map/ppermute | solution.py:94
  91.7 44.2 %collective-permute-start.3 = (bf16[128,4096]{1,0:T(8,128)(2,1)S(1)}, bf16[128,4096]{1,0:T(8,128)(2,1)}, u32[]{:S(2)}, u32[]{:S(2)}) collective-permute-start(bf16[128,4096]{1,0:T(8,128)(2,1)S(1)} %get-tuple-element.184), channel_id=1, source_target_pairs={{0,8},{8,0},{16,24},{24,16},{1,9},{9,1},{17,25},{25,17},{2,10},{10... | collective-permute-start | bytes 3145736 | tf_op jit(solution)/shard_map/ppermute | solution.py:94
  138.4 33.4 %collective-permute-start.7 = (bf16[4,5,24,768]{3,2,1,0:T(8,128)(2,1)S(1)}, bf16[4,5,24,768]{3,2,1,0:T(8,128)(2,1)S(1)}, u32[]{:S(2)}, u32[]{:S(2)}) collective-permute-start(bf16[4,5,24,768]{3,2,1,0:T(8,128)(2,1)S(1)} %slice.679.refs_0_), channel_id=1, source_target_pairs={{0,16},{8,24},{16,0},{24,8},{1,17},{9,25},{17,1},{25,9},{2,18},{10... | collective-permute-start | bytes 2211848 | tf_op jit(solution)/shard_map/ppermute | solution.py:87
  139.9 32.2 %collective-permute-start.6 = (bf16[4,5,24,768]{3,2,1,0:T(8,128)(2,1)S(1)}, bf16[4,5,24,768]{3,2,1,0:T(8,128)(2,1)S(1)}, u32[]{:S(2)}, u32[]{:S(2)}) collective-permute-start(bf16[4,5,24,768]{3,2,1,0:T(8,128)(2,1)S(1)} %slice.679.refs_0_), channel_id=1, source_target_pairs={{0,8},{8,0},{16,24},{24,16},{1,9},{9,1},{17,25},{25,17},{2,10},{10... | collective-permute-start | bytes 2211848 | tf_op jit(solution)/shard_map/ppermute | solution.py:87
  227.5 35.6 %collective-permute-start.18 = (bf16[4,4,24,768]{3,2,1,0:T(8,128)(2,1)S(1)}, bf16[4,4,24,768]{3,2,1,0:T(8,128)(2,1)S(1)}, u32[]{:S(2)}, u32[]{:S(2)}) collective-permute-start(bf16[4,4,24,768]{3,2,1,0:T(8,128)(2,1)S(1)} %slice.690.refs_0_), channel_id=1, source_target_pairs={{0,24},{8,16},{16,8},{24,0},{1,25},{9,17},{17,9},{25,1},{2,26},{10... | collective-permute-start | bytes 1769480 | tf_op jit(solution)/shard_map/ppermute | solution.py:87
  229.0 34.1 %collective-permute-start.17 = (bf16[4,4,24,768]{3,2,1,0:T(8,128)(2,1)S(1)}, bf16[4,4,24,768]{3,2,1,0:T(8,128)(2,1)S(1)}, u32[]{:S(2)}, u32[]{:S(2)}) collective-permute-start(bf16[4,4,24,768]{3,2,1,0:T(8,128)(2,1)S(1)} %slice.690.refs_0_), channel_id=1, source_target_pairs={{0,16},{8,24},{16,0},{24,8},{1,17},{9,25},{17,1},{25,9},{2,18},{10... | collective-permute-start | bytes 1769480 | tf_op jit(solution)/shard_map/ppermute | solution.py:87
  229.6 33.6 %collective-permute-start.16 = (bf16[4,4,24,768]{3,2,1,0:T(8,128)(2,1)S(1)}, bf16[4,4,24,768]{3,2,1,0:T(8,128)(2,1)}, u32[]{:S(2)}, u32[]{:S(2)}) collective-permute-start(bf16[4,4,24,768]{3,2,1,0:T(8,128)(2,1)S(1)} %slice.690.refs_0_), channel_id=1, source_target_pairs={{0,8},{8,0},{16,24},{24,16},{1,9},{9,1},{17,25},{25,17},{2,10},{10... | collective-permute-start | bytes 1769480 | tf_op jit(solution)/shard_map/ppermute | solution.py:87
  348.4 45.9 %collective-permute-start.41 = (bf16[2,1,16,16,128]{4,3,2,1,0:T(8,128)(2,1)}, bf16[2,1,16,16,128]{4,3,2,1,0:T(8,128)(2,1)}, u32[]{:S(2)}, u32[]{:S(2)}) collective-permute-start(bf16[2,1,16,16,128]{4,3,2,1,0:T(8,128)(2,1)} %get-tuple-element.217), channel_id=1, source_target_pairs={{0,1},{1,2},{2,3},{3,4},{4,5},{5,6},{6,7},{8,9},{9,10},{10,11},{11... | collective-permute-start | bytes 393224 | tf_op jit(solution)/shard_map/ppermute | solution.py:247
  350.9 43.3 %collective-permute-start.42 = (bf16[2,1,16,16,128]{4,3,2,1,0:T(8,128)(2,1)}, bf16[2,1,16,16,128]{4,3,2,1,0:T(8,128)(2,1)}, u32[]{:S(2)}, u32[]{:S(2)}) collective-permute-start(bf16[2,1,16,16,128]{4,3,2,1,0:T(8,128)(2,1)} %get-tuple-element.218), channel_id=1, source_target_pairs={{1,0},{2,1},{3,2},{4,3},{5,4},{6,5},{7,6},{9,8},{10,9},{11,10},{12... | collective-permute-start | bytes 393224 | tf_op jit(solution)/shard_map/ppermute | solution.py:248
  527.0 173.3 %reduce-scatter.4.cloned.1.call-start = ((), (), s32[]{:S(2)}) async-start(), calls=%async_computation.13 | async-start | bytes 8847360 | tf_op jit(solution)/shard_map/reduce_scatter | solution.py:726
  527.1 38.0 %collective-permute-start.60 = (bf16[4,4,24,768]{3,2,1,0:T(8,128)(2,1)}, bf16[4,4,24,768]{3,2,1,0:T(8,128)(2,1)}, u32[]{:S(2)}, u32[]{:S(2)}) collective-permute-start(bf16[4,4,24,768]{3,2,1,0:T(8,128)(2,1)} %get-tuple-element.170), channel_id=1, source_target_pairs={{0,24},{8,16},{16,8},{24,0},{1,25},{9,17},{17,9},{25,1},{2,26},{10... | collective-permute-start | bytes 1769480 | tf_op jit(solution)/shard_map/ppermute | solution.py:94
  528.4 36.7 %collective-permute-start.59 = (bf16[4,4,24,768]{3,2,1,0:T(8,128)(2,1)}, bf16[4,4,24,768]{3,2,1,0:T(8,128)(2,1)}, u32[]{:S(2)}, u32[]{:S(2)}) collective-permute-start(bf16[4,4,24,768]{3,2,1,0:T(8,128)(2,1)} %get-tuple-element.171), channel_id=1, source_target_pairs={{0,16},{8,24},{16,0},{24,8},{1,17},{9,25},{17,1},{25,9},{2,18},{10... | collective-permute-start | bytes 1769480 | tf_op jit(solution)/shard_map/ppermute | solution.py:94
  530.1 35.0 %collective-permute-start.58 = (bf16[4,4,24,768]{3,2,1,0:T(8,128)(2,1)}, bf16[4,4,24,768]{3,2,1,0:T(8,128)(2,1)}, u32[]{:S(2)}, u32[]{:S(2)}) collective-permute-start(bf16[4,4,24,768]{3,2,1,0:T(8,128)(2,1)} %get-tuple-element.172), channel_id=1, source_target_pairs={{0,8},{8,0},{16,24},{24,16},{1,9},{9,1},{17,25},{25,17},{2,10},{10... | collective-permute-start | bytes 1769480 | tf_op jit(solution)/shard_map/ppermute | solution.py:94
  590.8 148.4 %reduce-scatter.6.cloned.1.call-start = ((), (), s32[]{:S(2)}) async-start(), calls=%async_computation.14 | async-start | bytes 3538944 | tf_op jit(solution)/shard_map/reduce_scatter | solution.py:717
  621.3 127.1 %reduce-scatter.8.cloned.1.call-start = ((), (), s32[]{:S(2)}) async-start(), calls=%async_computation.15 | async-start | bytes 1658880 | tf_op jit(solution)/shard_map/reduce_scatter | solution.py:240
  637.4 34.7 %collective-permute-start.70 = (bf16[4,5,24,768]{3,2,1,0:T(8,128)(2,1)}, bf16[4,5,24,768]{3,2,1,0:T(8,128)(2,1)}, u32[]{:S(2)}, u32[]{:S(2)}) collective-permute-start(bf16[4,5,24,768]{3,2,1,0:T(8,128)(2,1)} %get-tuple-element.168), channel_id=1, source_target_pairs={{0,24},{8,16},{16,8},{24,0},{1,25},{9,17},{17,9},{25,1},{2,26},{10... | collective-permute-start | bytes 2211848 | tf_op jit(solution)/shard_map/ppermute | solution.py:94
  638.9 57.9 %collective-permute-start.69 = (bf16[4,5,24,768]{3,2,1,0:T(8,128)(2,1)}, bf16[4,5,24,768]{3,2,1,0:T(8,128)(2,1)}, u32[]{:S(2)}, u32[]{:S(2)}) collective-permute-start(bf16[4,5,24,768]{3,2,1,0:T(8,128)(2,1)} %get-tuple-element.169), channel_id=1, source_target_pairs={{0,16},{8,24},{16,0},{24,8},{1,17},{9,25},{17,1},{25,9},{2,18},{10... | collective-permute-start | bytes 2211848 | tf_op jit(solution)/shard_map/ppermute | solution.py:94
  641.6 58.7 %collective-permute-start.66 = (bf16[128,4096]{1,0:T(8,128)(2,1)}, bf16[128,4096]{1,0:T(8,128)(2,1)}, u32[]{:S(2)}, u32[]{:S(2)}) collective-permute-start(bf16[128,4096]{1,0:T(8,128)(2,1)} %get-tuple-element.179), channel_id=1, source_target_pairs={{0,24},{8,16},{16,8},{24,0},{1,25},{9,17},{17,9},{25,1},{2,26},{10... | collective-permute-start | bytes 3145736 | tf_op jit(solution)/shard_map/ppermute | solution.py:94
  642.9 75.5 %collective-permute-start.65 = (bf16[128,4096]{1,0:T(8,128)(2,1)}, bf16[128,4096]{1,0:T(8,128)(2,1)}, u32[]{:S(2)}, u32[]{:S(2)}) collective-permute-start(bf16[128,4096]{1,0:T(8,128)(2,1)} %get-tuple-element.180), channel_id=1, source_target_pairs={{0,16},{8,24},{16,0},{24,8},{1,17},{9,25},{17,1},{25,9},{2,18},{10... | collective-permute-start | bytes 3145736 | tf_op jit(solution)/shard_map/ppermute | solution.py:94
  655.3 63.1 %collective-permute-start.64 = (bf16[128,4096]{1,0:T(8,128)(2,1)}, bf16[128,4096]{1,0:T(8,128)(2,1)}, u32[]{:S(2)}, u32[]{:S(2)}) collective-permute-start(bf16[128,4096]{1,0:T(8,128)(2,1)} %get-tuple-element.181), channel_id=1, source_target_pairs={{0,8},{8,0},{16,24},{24,16},{1,9},{9,1},{17,25},{25,17},{2,10},{10... | collective-permute-start | bytes 3145736 | tf_op jit(solution)/shard_map/ppermute | solution.py:94
  769.0 39.5 %all-to-all-start.7 = ((bf16[4,640,192]{1,2,0:T(8,128)(2,1)}), bf16[4,640,192]{1,2,0:T(8,128)(2,1)}, u32[]{:S(2)}, u32[]{:S(2)}) async-start(bf16[4,640,192]{1,2,0:T(8,128)(2,1)} %bitcast.155), calls=%async_computation.10 | async-start | bytes 1966080 | tf_op jit(solution)/shard_map/all_to_all | solution.py:81
  (208 other events, 2116.9 us)
Sparse Core Ops, SparseCore 0:
  46.4 33.2 all-gather.4
  89.0 77.2 all-gather.6
  204.1 35.6 all-gather.8
  590.9 82.9 reduce-scatter.3
  676.1 38.7 reduce-scatter.5
  717.6 30.6 reduce-scatter.7

commit v3 on v2

--- a/solution.py
+++ b/solution.py
@@ -132,6 +132,23 @@
         compiler_params=pltpu.CompilerParams(vmem_limit_bytes=4 * size + 2**22),
         cost_estimate=pl.CostEstimate(flops=0, transcendentals=0, bytes_accessed=4 * size),
     )(place, *inputs)
+
+
+def column_plan(pieces, block, apart):
+    crops = lax.axis_size("crop")
+    plan = []
+    for shift in range(crops):
+        for piece in range(pieces):
+
+            def whole(crop, core, shift=shift, piece=piece):
+                start = (piece * crops + (crop ^ shift)) * block
+                return (slice(None), pl.ds(pl.multiple_of(start, block), block))
+
+            def part(crop, core, piece=piece):
+                return (slice(None), pl.ds(piece * block, block))
+
+            plan.append((0, whole, shift, part) if apart else (shift, part, 0, whole))
+    return plan
 
 
 def chunk_at(spot, crop, core):
@@ -236,8 +253,13 @@
     return lax.optimization_barrier((value, earlier))[0]
 
 
-def z_scatter(pack):
-    return lax.psum_scatter(pack, "z", scatter_dimension=0, tiled=False)
+def z_sum(pack):
+    own = lax.axis_index("z")
+    pieces = [
+        lax.dynamic_index_in_dim(pack, own ^ shift, 0, keepdims=False)
+        for shift in range(pack.shape[0])
+    ]
+    return total_of(flips_of(pieces, "z")).astype(jnp.bfloat16)
 
 
 def neighbours(volume):
@@ -492,15 +514,23 @@
     ).reshape(-1, 1)
     marks = jnp.broadcast_to(own_mri.astype(jnp.float32), (rows_in, 128))
     is_mri = jnp.concatenate(flips(marks, "crop"), 0)[:, :1] > 0.5
-    pixels = patches.reshape(rows_in, pieces, crops, block).transpose(2, 0, 1, 3)
-    pixels = pixels.reshape(crops, rows_in, pieces * block)
-    pixels = [
-        lax.dynamic_index_in_dim(pixels, own_crop ^ shift, 0, keepdims=False)
-        for shift in range(crops)
-    ]
-    pixel_parts = flips_of(pixels, "crop")
-    wide = crop_swap(after(wide, is_mri))
-    embed_part = crop_swap(after(embed_wide, (wide, pixels)))
+    lanes = pieces * block
+    if block % 128 == 0:
+        pixels = moves(
+            column_plan(pieces, block, True),
+            [patches.reshape(rows_in, crops * lanes)],
+            [(rows_in, lanes)] * crops,
+        )
+    else:
+        pixels = patches.reshape(rows_in, pieces, crops, block).transpose(2, 0, 1, 3)
+        pixels = pixels.reshape(crops, rows_in, lanes)
+        pixels = [
+            lax.dynamic_index_in_dim(pixels, own_crop ^ shift, 0, keepdims=False)
+            for shift in range(crops)
+        ]
+    pixel_parts = flips_of(list(pixels), "crop")
+    wide = crop_swap(wide)
+    embed_part = crop_swap(after(embed_wide, (wide, is_mri)))
     embed_part = embed_part.transpose(1, 0, 2).reshape(share, D)
     marks = []
     edge = 0
@@ -541,7 +571,7 @@
     pack_one, pack_slim = packs[:, :5], packs[:, 5:]
     embed_full = lax.all_gather(embed_part, SLAB, axis=0, tiled=True)
     up_size = up_part.shape[0]
-    ff_part = after(jnp.concatenate([up_part, down_part], 0), embed_full)
+    ff_part = after(jnp.concatenate([up_part, down_part], 0), embed_part)
     ff_full = lax.all_gather(ff_part, SLAB, axis=0)
     up_full = ff_full[:, :up_size].reshape(D, class_size)
     down_full = ff_full[:, up_size:].reshape(class_size, D)
@@ -562,12 +592,12 @@
     lead = (layers, 2, crops)
     none = jnp.zeros((), jnp.bfloat16)
     one_own = flips(pack_one, "crop")
-    pixels = jnp.concatenate(after(pixel_parts, one_own), 0)
+    pixels = jnp.concatenate(pixel_parts, 0)
     pixel_rows = jnp.concatenate(
         [jnp.where(is_mri, none, pixels[:, :ct_size]), jnp.where(is_mri, pixels, none)], 1
     )
-    partial = matmul(pixel_rows, embed_full).astype(jnp.bfloat16).reshape(crops, rows_in, D)
-    product = total_of(flips_of(list(partial), "crop"))
+    partial = matmul(pixel_rows, embed_full).astype(jnp.bfloat16)
+    product = total_of(flips_of(list(partial.reshape(crops, rows_in, D)), "crop"))
     one_other = core_swap(after(one_own, partial))
     triple_full, output_full, vector_full = moves(
         gather_plan(one_spots),
@@ -672,7 +702,7 @@
     weight_up = matmul_left_t(normed_all, grad_inner_low).astype(jnp.bfloat16)
     ff_grads = jnp.concatenate(
         [weight_up.reshape(slab_count, -1, D), weight_down.reshape(slab_count, -1, D)], 1
-    )
+    ).reshape(-1, D)
 
     slim_move = scatter_cores(
         [
@@ -714,7 +744,7 @@
     grad_triple = heads_back(grad_triple, crop_batch, 3)
     grad_triple = after(grad_triple, slim_got)
     ff_grads = after(ff_grads, grad_triple)
-    ff_sum = lax.psum_scatter(ff_grads, SLAB, scatter_dimension=0, tiled=False)
+    ff_sum = lax.psum_scatter(ff_grads, SLAB, scatter_dimension=0, tiled=True)
     weight_triple = matmul_left_t(normed_one, grad_triple)
     back_one = pull_one(matmul_right_t(grad_triple, triple_full))
     grad_hidden = grad_hidden + back_one[0]
@@ -723,24 +753,19 @@
     grad_rows = jnp.concatenate(flips(grad_low, "crop"), 0)
     weight_embed = matmul_left_t(pixel_rows, grad_rows).astype(jnp.bfloat16)
     slim_sum = total_of(after(slim_got, weight_embed)).astype(jnp.bfloat16)
-    embed_sum = lax.psum_scatter(weight_embed, SLAB, scatter_dimension=0, tiled=True)
+    embed_sum = lax.psum_scatter(after(weight_embed, ff_sum), SLAB, scatter_dimension=0, tiled=True)
     pixel_grad = matmul_right_t(after(grad_rows, weight_embed), embed_full)
     ct_grad = jnp.pad(pixel_grad[:, :ct_size], ((0, 0), (0, (CHANS - 1) * ct_size)))
     pixel_grad = jnp.where(is_mri, pixel_grad[:, ct_size:], ct_grad).astype(jnp.bfloat16)
-    pixel_got = flips_of(list(pixel_grad.reshape(crops, rows_in, pieces * block)), "crop")
-    pixel_got = jnp.stack(pixel_got)
-    patch_grad = jnp.stack(
-        [
-            lax.dynamic_index_in_dim(pixel_got, own_crop ^ part, 0, keepdims=False)
-            for part in range(crops)
-        ]
-    )
-    patch_grad = patch_grad.reshape(crops, rows_in, pieces, block).transpose(1, 2, 0, 3)
-    patch_grad = patch_grad.reshape(patches.shape)
-
     bias_ct = jnp.sum(jnp.where(own_mri, 0.0, grad_hidden), 0)
     bias_mri = jnp.sum(jnp.where(own_mri, grad_hidden, 0.0), 0)
     position_grad = jnp.sum(grad_hidden.reshape(crop_batch, local_tokens, D), 0)
+    position_grad = position_grad.astype(jnp.bfloat16).reshape(-1, crops, unit).swapaxes(0, 1)
+    position_grad = [
+        lax.dynamic_index_in_dim(position_grad, own_crop ^ shift, 0, keepdims=False)
+        for shift in range(crops)
+    ]
+    position_grad = total_of(flips_of(position_grad, "crop"))
     at_class = lax.broadcasted_iota(jnp.int32, (slab_count, crops, down_count), 1) == own_crop
     bias_full = jnp.where(at_class, bias_up.reshape(slab_count, 1, down_count), 0.0)
     vector_grad = jnp.concatenate(
@@ -775,11 +800,25 @@
         one_spots,
         5,
     ))
-    one_sum = total_of(flips_of(one_parts, "crop")).astype(jnp.bfloat16)
-    sums = jnp.concatenate([slim_sum, one_sum], 1)
-    sums = z_scatter(after(sums, (embed_sum, pixel_grad)))
-    sums = sums.reshape(-1, D)
-    one_row = slim_chunks * row_count
+    one_got = flips_of(one_parts, "crop")
+    one_sum = total_of(one_got).astype(jnp.bfloat16)
+    pixel_got = flips_of(
+        after(list(pixel_grad.reshape(crops, rows_in, pieces * block)), one_got), "crop"
+    )
+    if block % 128 == 0:
+        (patch_grad,) = moves(
+            column_plan(pieces, block, False), pixel_got, [(rows_in, crops * lanes)]
+        )
+    else:
+        pixel_got = jnp.stack(pixel_got)
+        patch_grad = jnp.stack(
+            [
+                lax.dynamic_index_in_dim(pixel_got, own_crop ^ part, 0, keepdims=False)
+                for part in range(crops)
+            ]
+        )
+        patch_grad = patch_grad.reshape(crops, rows_in, pieces, block).transpose(1, 2, 0, 3)
+    patch_grad = patch_grad.reshape(patches.shape)
 
     def by_units(rows, chunks):
         shaped = rows.reshape(chunks, -1, crops, unit).transpose(0, 2, 1, 3)
@@ -790,12 +829,9 @@
             got.reshape(crops, chunks, -1, unit).transpose(0, 2, 1, 3).reshape(-1, chunks * unit)
         )
 
-    embed_got = crop_swap(by_units(embed_sum, 1)).astype(jnp.float32)
-    embed_grad = (
-        embed_got.reshape(crops, groups, block, unit).transpose(1, 0, 2, 3).reshape(-1, unit)
-    )
-    sum_one = sums[one_row:]
-    slim_all = sums[:one_row].reshape(slim_chunks, row_count, 6, DEC)
+    slim_all = z_sum(slim_sum).reshape(slim_chunks, row_count, 6, DEC)
+    sum_one = z_sum(one_sum).reshape(-1, D)
+
     slim_all = slim_all.transpose(0, 2, 1, 3).reshape(-1, DEC)
     first_start = 8 * row_count
     second_start = first_start + first_chunks * row_count
@@ -818,16 +854,24 @@
             by_units(ff_sum[up_size:], 1),
             by_units(sum_one[: 3 * row_count], 3),
             by_units(sum_one[3 * row_count : 4 * row_count], 1),
-            by_units(position_grad.astype(jnp.bfloat16), 1),
             lift_units,
             narrow_units,
+            by_units(embed_sum, 1),
         ],
         1,
     )
-    wide = crop_swap(wide).astype(jnp.float32)
+    local_sum = jnp.float32(0.0)
+    for gradient in (embed_sum, ff_sum, lift_sum, narrow_sum, sum_one, position_grad):
+        wide_grad = gradient.astype(jnp.float32)
+        local_sum = local_sum + jnp.sum(wide_grad * wide_grad)
+    wide = crop_swap(after(wide, local_sum)).astype(jnp.float32)
+    embed_got = wide[:, -share:]
+    embed_grad = (
+        embed_got.astype(jnp.float32).reshape(crops, groups, block, unit).transpose(1, 0, 2, 3).reshape(-1, unit)
+    )
     marks = []
     edge = 0
-    for size in (up_units.shape[1], down_count, 3 * row_count, row_count, position_grad.shape[0],
+    for size in (up_units.shape[1], down_count, 3 * row_count, row_count,
                  lift_units.shape[1], narrow_units.shape[1]):
         marks.append(wide[:, edge : edge + size])
         edge += size
@@ -837,9 +881,8 @@
     down_grad = join_units(marks[1], 1)
     triple_grad = join_units(marks[2], 3)
     output_grad = join_units(marks[3], 1)
-    position_grad = jnp.sum(marks[4], 0)
-    lift_grad = from_units(marks[5], row_count, 8 * DEC // crops).reshape(upsample.shape)
-    narrow_got = from_units(marks[6], first_count + second_count, DEC // crops)
+    lift_grad = from_units(marks[4], row_count, 8 * DEC // crops).reshape(upsample.shape)
+    narrow_got = from_units(marks[5], first_count + second_count, DEC // crops)
     first_grad = narrow_got[:, :first_count].reshape(-1, DEC // crops)[: convolve_one.shape[0]]
     second_grad = narrow_got[:, first_count:].reshape(-1, DEC // crops)[: convolve_two.shape[0]]
     vector_final = sum_one[4 * row_count, :vector_size].astype(jnp.float32)
@@ -855,10 +898,6 @@
         position_grad,
         vector_final,
     )
-    local_sum = jnp.float32(0.0)
-    for gradient in (embed_sum, ff_sum, lift_sum, narrow_sum, sum_one, position_grad):
-        wide_grad = gradient.astype(jnp.float32)
-        local_sum = local_sum + jnp.sum(wide_grad * wide_grad)
     grad_norm = jnp.sqrt(slab_sum(total_of(flips(local_sum.reshape(1, 1), "crop"))))[0, 0]
     factor = jnp.minimum(1.0, CLIP / grad_norm)
     news, means, squares = ([], [], [])

time: 854 us -> 800 us (0.937)
  waiting for transfers between devices: 253 us -> 210 us
  local copies, waits for them, and re-layouts: 201 us -> 179 us
  starting transfers between devices: 137 us -> 149 us
  other arithmetic: 93.1 us -> 83.8 us
  Pallas kernels: 13.5 us -> 22.4 us
    ppermute x21 -> x30, waiting for transfers between devices: 127 us -> 84.9 us  [flips_of(): lax.ppermute(pieces[shift], axis, flip_pairs(count, shift))]
    all_gather x1, waiting for transfers between devices: 0.01 us -> 30 us  [local(): embed_full = lax.all_gather(embed_part, SLAB, axis=0, tiled=True)]
    ppermute x21, waiting for transfers between devices: 43.1 us -> 15.6 us  [flips(): lax.ppermute(value, axis, flip_pairs(count, shift))]
    reshape x6 -> x1, local copies, waits for them, and re-layouts: 26.3 us -> 0.19 us  [local(): slim_all = z_sum(slim_sum).reshape(slim_chunks, row_count, 6, DEC)]
    ppermute x21 -> x30, starting transfers between devices: 25.5 us -> 37.8 us  [flips_of(): lax.ppermute(pieces[shift], axis, flip_pairs(count, shift))]
    transpose x3 -> x1, local copies, waits for them, and re-layouts: 13 us -> 1.76 us  [local(): ff_sum[:up_size].reshape(up_rows, crops, per_class).transpose(1, 0, 2)]
    unnamed x6, waiting for transfers between devices: 0.1 us -> 10 us
    pallas_call x4 -> x6, Pallas kernels: 13.5 us -> 22.4 us  [moves(): pl.pallas_call(kernel, in_specs=[pl.BlockSpec(memory_space=pltpu.SMEM)] +...]
  transfers between devices with their start and end apart: 89 -> 96, of which waited for: 40 -> 35; matrix products, arithmetic and copies ran while one was open for 29% -> 27% of each run, Pallas kernels for 2% -> 3%
where the time goes in v3:
time: 800 us; the launch traced here: 791 us
  waiting for transfers between devices  210 us (26%)
  local copies, waits for them, and re-layouts  179 us (22%)
  starting transfers between devices  149 us (19%)
  matrix products  90.8 us (11%)
  other arithmetic  83.8 us (10%)
  blocking collectives  29.5 us (4%)
  between operations  26.4 us (3%)
  Pallas kernels  22.4 us (3%)
    ppermute x30, waiting for transfers between devices, flips_of(): lax.ppermute(pieces[shift], axis, flip_pairs(count, shift))  84.9 us
    unnamed x444, local copies, waits for them, and re-layouts  42.8 us
    ppermute x30, starting transfers between devices, flips_of(): lax.ppermute(pieces[shift], axis, flip_pairs(count, shift))  37.8 us
    dot_general x10, matrix products, matmul(): return jnp.dot(left, right, preferred_element_type=jnp.float32)  34.2 us
    ppermute x21, starting transfers between devices, flips(): lax.ppermute(value, axis, flip_pairs(count, shift))  33.2 us
    all_gather x1, waiting for transfers between devices, local(): embed_full = lax.all_gather(embed_part, SLAB, axis=0, tiled=True)  30 us
    dot_general x8, matrix products, matmul_left_t(): lax.dot_general(left, right, CONTRACT_ROWS, preferred_element_type=jnp.fl...  29.3 us
    all_to_all x2, waiting for transfers between devices, heads_back(): shaped = lax.all_to_all(block, SLAB, 1, 0, tiled=True)[:crop_count * HEADS]  25.4 us
  transfers between devices with their start and end apart: 96, of which 35 were waited for; matrix products, arithmetic and copies ran while one was open for 27% of the time, Pallas kernels for 3%

profile of v3, /device:TPU:0, one launch (start us, length us, event | category | flops | bytes accessed | tf_op | source)
XLA Modules:
  0.0 790.9 jit_solution(12747679519603988951)
XLA Ops:
  18.6 5.2 all-to-all-start
  23.8 10.8 %all-to-all-done = bf16[4,438,192]{1,2,0:T(8,128)(2,1)S(1)} async-done(((bf16[4,438,192]{1,2,0:T(8,128)(2,1)}), bf16[4,438,192]{1,2,0:T(8,128)(2,1)S(1)}, u32[]{:S(2)}, u32[]{:S(2)}) %all-to-all-start) | async-done | bytes 672800 | tf_op jit(solution)/shard_map/all_to_all | solution.py:81
  45.9 14.2 %all_to_all.81 = bf16[4,640,192]{1,2,0:T(8,128)(2,1)} all-to-all(bf16[4,640,192]{1,2,0:T(8,128)(2,1)S(1)} %copy.701), channel_id=1, replica_groups=mesh['crop'=4,'z'=4,'core'=2] {'crop'}, dimensions={0} | all-to-all | bytes 1966080 | tf_op jit(solution)/shard_map/all_to_all | solution.py:81
  69.9 22.5 %collective-permute-done.3 = bf16[128,4096]{1,0:T(8,128)(2,1)S(1)} collective-permute-done((bf16[128,4096]{1,0:T(8,128)(2,1)S(1)}, bf16[128,4096]{1,0:T(8,128)(2,1)S(1)}, u32[]{:S(2)}, u32[]{:S(2)}) %collective-permute-start.3) | collective-permute-done | bytes 1048608 | tf_op jit(solution)/shard_map/ppermute | solution.py:94
  92.5 18.6 %collective-permute-done.4 = bf16[128,4096]{1,0:T(8,128)(2,1)S(1)} collective-permute-done((bf16[128,4096]{1,0:T(8,128)(2,1)S(1)}, bf16[128,4096]{1,0:T(8,128)(2,1)S(1)}, u32[]{:S(2)}, u32[]{:S(2)}) %collective-permute-start.4) | collective-permute-done | bytes 1048608 | tf_op jit(solution)/shard_map/ppermute | solution.py:94
  119.5 30.0 %all-gather.5.cloned.1.call-done = bf16[5120,768]{0,1:T(8,128)(2,1)} async-done(((bf16[640,768]{0,1:T(8,128)(2,1)}), bf16[5120,768]{0,1:T(8,128)(2,1)}) %all-gather.5.cloned.1.call-update) | async-done | bytes 7864336 | tf_op jit(solution)/shard_map/all_gather | solution.py:572
  149.5 9.9 %fusion.34 = bf16[512,768]{1,0:T(8,128)(2,1)} fusion(bf16[5120,768]{0,1:T(8,128)(2,1)} %all-gather.5.cloned.1.call-done, bf16[512,4096]{1,0:T(8,128)(2,1)} %broadcast_select_fusion, bf16[512,1024]{1,0:T(8,128)(2,1)} %slice_select_fusion.1), kind=kOutput, calls=%fused_computation.154 | convolution fusion | flops 4037410816 | bytes 13893632 | tf_op jit(solution)/shard_map/dot_general | solution.py:52
  203.0 16.2 %all-to-all-done.2 = bf16[24,64,192]{2,1,0:T(8,128)(2,1)S(1)} async-done(((bf16[24,64,192]{2,1,0:T(8,128)(2,1)}), bf16[24,64,192]{2,1,0:T(8,128)(2,1)S(1)}, u32[]{:S(2)}, u32[]{:S(2)}) %all-to-all-start.2) | async-done | bytes 589856 | tf_op jit(solution)/shard_map/all_to_all | solution.py:345
  238.3 7.3 all-to-all-done.3
  268.1 6.2 fusion.20
  303.4 4.8 fusion.245
  394.3 6.0 fusion.4
  415.0 8.9 %fusion.1 = bf16[6912,128]{1,0:T(8,128)(2,1)S(1)} fusion(bf16[2,2,16,16,6912]{4,3,2,1,0:T(8,128)(2,1)} %copy-done.117, bf16[2,4,16,16,128]{4,3,2,1,0:T(8,128)(2,1)S(1)} %fusion.90), kind=kOutput, calls=%fused_computation.3 | convolution fusion | flops 1812824064 | bytes 16187392 | tf_op jit(solution)/shard_map/dot_general | solution.py:56
  464.6 15.3 %all_to_all.82 = bf16[8,2,6144]{2,1,0:T(2,128)(2,1)} all-to-all(bf16[8,2,6144]{2,1,0:T(2,128)(2,1)S(1)} %reshape.753), channel_id=1, replica_groups=mesh['crop'=4,'z'=4,'core'=2] {'z','core'}, dimensions={0} | all-to-all | bytes 393216 | tf_op jit(solution)/shard_map/all_to_all | solution.py:345
  504.8 18.1 %all-to-all-done.5 = bf16[3,512,192]{2,0,1:T(4,128)(2,1)S(1)} async-done(((bf16[3,512,192]{2,0,1:T(4,128)(2,1)}), bf16[3,512,192]{2,0,1:T(4,128)(2,1)S(1)}, u32[]{:S(2)}, u32[]{:S(2)}) %all-to-all-start.5) | async-done | bytes 589856 | tf_op jit(solution)/shard_map/all_to_all | solution.py:349
  549.5 6.8 convolution_convert_fusion
  556.3 9.9 %reduce-scatter.7.cloned.1.call-done = bf16[192,768]{1,0:T(8,128)(2,1)} async-done(((bf16[1536,768]{1,0:T(8,128)(2,1)}), bf16[192,768]{1,0:T(8,128)(2,1)}) %reduce-scatter.7.cloned.1.call-update) | async-done | bytes 294928
  604.0 7.9 fusion.285
  624.1 11.7 %collective-permute-done.65 = bf16[4,5,24,768]{3,2,1,0:T(8,128)(2,1)} collective-permute-done((bf16[4,5,24,768]{3,2,1,0:T(8,128)(2,1)}, bf16[4,5,24,768]{3,2,1,0:T(8,128)(2,1)}, u32[]{:S(2)}, u32[]{:S(2)}) %collective-permute-start.65) | collective-permute-done | bytes 737312 | tf_op jit(solution)/shard_map/ppermute | solution.py:94
  635.7 14.3 %collective-permute-done.66 = bf16[4,5,24,768]{3,2,1,0:T(8,128)(2,1)} collective-permute-done((bf16[4,5,24,768]{3,2,1,0:T(8,128)(2,1)S(1)}, bf16[4,5,24,768]{3,2,1,0:T(8,128)(2,1)}, u32[]{:S(2)}, u32[]{:S(2)}) %collective-permute-start.66) | collective-permute-done | bytes 737312 | tf_op jit(solution)/shard_map/ppermute | solution.py:94
  660.3 6.5 collective-permute-done.74
  712.7 5.8 shard_map.590
  718.5 6.1 collective-permute-start.80
  734.6 6.7 collective-permute-start.84
  (948 shorter events, 494.7 us)
Async XLA Ops:
  23.7 91.0 %all-gather.7.cloned.1.call-start = ((), (), s32[]{:S(2)}) async-start(), calls=%async_computation.10 | async-start | bytes 1658880 | tf_op jit(solution)/shard_map/all_gather | solution.py:569
  37.7 111.8 %all-gather.5.cloned.1.call-start = ((), (), s32[]{:S(2)}) async-start(), calls=%async_computation.9 | async-start | bytes 8847360 | tf_op jit(solution)/shard_map/all_gather | solution.py:572
  60.1 200.6 %all-gather.9.cloned.1.call-start = ((), (), s32[]{:S(2)}) async-start(), calls=%async_computation.12 | async-start | bytes 2654208 | tf_op jit(solution)/shard_map/all_gather | solution.py:575
  67.5 43.7 %collective-permute-start.4 = (bf16[128,4096]{1,0:T(8,128)(2,1)S(1)}, bf16[128,4096]{1,0:T(8,128)(2,1)S(1)}, u32[]{:S(2)}, u32[]{:S(2)}) collective-permute-start(bf16[128,4096]{1,0:T(8,128)(2,1)S(1)} %get-tuple-element.75), channel_id=1, source_target_pairs={{0,16},{8,24},{16,0},{24,8},{1,17},{9,25},{17,1},{25,9},{2,18},{10... | collective-permute-start | bytes 3145736 | tf_op jit(solution)/shard_map/ppermute | solution.py:94
  67.8 43.4 %collective-permute-start.5 = (bf16[128,4096]{1,0:T(8,128)(2,1)S(1)}, bf16[128,4096]{1,0:T(8,128)(2,1)S(1)}, u32[]{:S(2)}, u32[]{:S(2)}) collective-permute-start(bf16[128,4096]{1,0:T(8,128)(2,1)S(1)} %get-tuple-element.76), channel_id=1, source_target_pairs={{0,24},{8,16},{16,8},{24,0},{1,25},{9,17},{17,9},{25,1},{2,26},{10... | collective-permute-start | bytes 3145736 | tf_op jit(solution)/shard_map/ppermute | solution.py:94
  115.9 43.5 %collective-permute-start.10 = (bf16[4,5,24,768]{3,2,1,0:T(8,128)(2,1)S(1)}, bf16[4,5,24,768]{3,2,1,0:T(8,128)(2,1)S(1)}, u32[]{:S(2)}, u32[]{:S(2)}) collective-permute-start(bf16[4,5,24,768]{3,2,1,0:T(8,128)(2,1)S(1)} %slice.666.refs_0_), channel_id=1, source_target_pairs={{0,16},{8,24},{16,0},{24,8},{1,17},{9,25},{17,1},{25,9},{2,18},{10... | collective-permute-start | bytes 2211848 | tf_op jit(solution)/shard_map/ppermute | solution.py:87
  116.4 43.0 %collective-permute-start.11 = (bf16[4,5,24,768]{3,2,1,0:T(8,128)(2,1)S(1)}, bf16[4,5,24,768]{3,2,1,0:T(8,128)(2,1)S(1)}, u32[]{:S(2)}, u32[]{:S(2)}) collective-permute-start(bf16[4,5,24,768]{3,2,1,0:T(8,128)(2,1)S(1)} %slice.666.refs_0_), channel_id=1, source_target_pairs={{0,24},{8,16},{16,8},{24,0},{1,25},{9,17},{17,9},{25,1},{2,26},{10... | collective-permute-start | bytes 2211848 | tf_op jit(solution)/shard_map/ppermute | solution.py:87
  118.2 41.2 %collective-permute-start.9 = (bf16[4,5,24,768]{3,2,1,0:T(8,128)(2,1)S(1)}, bf16[4,5,24,768]{3,2,1,0:T(8,128)(2,1)S(1)}, u32[]{:S(2)}, u32[]{:S(2)}) collective-permute-start(bf16[4,5,24,768]{3,2,1,0:T(8,128)(2,1)S(1)} %slice.666.refs_0_), channel_id=1, source_target_pairs={{0,8},{8,0},{16,24},{24,16},{1,9},{9,1},{17,25},{25,17},{2,10},{10... | collective-permute-start | bytes 2211848 | tf_op jit(solution)/shard_map/ppermute | solution.py:87
  199.4 29.2 %collective-permute-start.16 = (bf16[4,4,24,768]{3,2,1,0:T(8,128)(2,1)S(1)}, bf16[4,4,24,768]{3,2,1,0:T(8,128)(2,1)S(1)}, u32[]{:S(2)}, u32[]{:S(2)}) collective-permute-start(bf16[4,4,24,768]{3,2,1,0:T(8,128)(2,1)S(1)} %slice.676.refs_0_), channel_id=1, source_target_pairs={{0,8},{8,0},{16,24},{24,16},{1,9},{9,1},{17,25},{25,17},{2,10},{10... | collective-permute-start | bytes 1769480 | tf_op jit(solution)/shard_map/ppermute | solution.py:87
  201.1 28.0 %collective-permute-start.17 = (bf16[4,4,24,768]{3,2,1,0:T(8,128)(2,1)S(1)}, bf16[4,4,24,768]{3,2,1,0:T(8,128)(2,1)S(1)}, u32[]{:S(2)}, u32[]{:S(2)}) collective-permute-start(bf16[4,4,24,768]{3,2,1,0:T(8,128)(2,1)S(1)} %slice.676.refs_0_), channel_id=1, source_target_pairs={{0,16},{8,24},{16,0},{24,8},{1,17},{9,25},{17,1},{25,9},{2,18},{10... | collective-permute-start | bytes 1769480 | tf_op jit(solution)/shard_map/ppermute | solution.py:87
  314.3 45.1 %collective-permute-start.41 = (bf16[2,1,16,16,128]{4,3,2,1,0:T(8,128)(2,1)}, bf16[2,1,16,16,128]{4,3,2,1,0:T(8,128)(2,1)}, u32[]{:S(2)}, u32[]{:S(2)}) collective-permute-start(bf16[2,1,16,16,128]{4,3,2,1,0:T(8,128)(2,1)} %get-tuple-element.567), channel_id=1, source_target_pairs={{0,1},{1,2},{2,3},{3,4},{4,5},{5,6},{6,7},{8,9},{9,10},{10,11},{11... | collective-permute-start | bytes 393224 | tf_op jit(solution)/shard_map/ppermute | solution.py:269
  316.8 42.6 %collective-permute-start.42 = (bf16[2,1,16,16,128]{4,3,2,1,0:T(8,128)(2,1)}, bf16[2,1,16,16,128]{4,3,2,1,0:T(8,128)(2,1)}, u32[]{:S(2)}, u32[]{:S(2)}) collective-permute-start(bf16[2,1,16,16,128]{4,3,2,1,0:T(8,128)(2,1)} %get-tuple-element.568), channel_id=1, source_target_pairs={{1,0},{2,1},{3,2},{4,3},{5,4},{6,5},{7,6},{9,8},{10,9},{11,10},{12... | collective-permute-start | bytes 393224 | tf_op jit(solution)/shard_map/ppermute | solution.py:270
  492.7 30.1 %all-to-all-start.5 = ((bf16[3,512,192]{2,0,1:T(4,128)(2,1)}), bf16[3,512,192]{2,0,1:T(4,128)(2,1)S(1)}, u32[]{:S(2)}, u32[]{:S(2)}) async-start(bf16[3,512,192]{2,0,1:T(4,128)(2,1)} %copy.742), calls=%async_computation.5 | async-start | bytes 2097152 | tf_op jit(solution)/shard_map/all_to_all | solution.py:349
  496.4 69.9 %reduce-scatter.7.cloned.1.call-start = ((), (), s32[]{:S(2)}) async-start(), calls=%async_computation.13 | async-start | bytes 2654208
  496.4 35.2 %collective-permute-start.58 = (bf16[4,4,24,768]{3,2,1,0:T(8,128)(2,1)}, bf16[4,4,24,768]{3,2,1,0:T(8,128)(2,1)}, u32[]{:S(2)}, u32[]{:S(2)}) collective-permute-start(bf16[4,4,24,768]{3,2,1,0:T(8,128)(2,1)} %get-tuple-element.526), channel_id=1, source_target_pairs={{0,8},{8,0},{16,24},{24,16},{1,9},{9,1},{17,25},{25,17},{2,10},{10... | collective-permute-start | bytes 1769480 | tf_op jit(solution)/shard_map/ppermute | solution.py:94
  497.3 34.4 %collective-permute-start.59 = (bf16[4,4,24,768]{3,2,1,0:T(8,128)(2,1)}, bf16[4,4,24,768]{3,2,1,0:T(8,128)(2,1)}, u32[]{:S(2)}, u32[]{:S(2)}) collective-permute-start(bf16[4,4,24,768]{3,2,1,0:T(8,128)(2,1)} %get-tuple-element.525), channel_id=1, source_target_pairs={{0,16},{8,24},{16,0},{24,8},{1,17},{9,25},{17,1},{25,9},{2,18},{10... | collective-permute-start | bytes 1769480 | tf_op jit(solution)/shard_map/ppermute | solution.py:94
  498.7 32.9 %collective-permute-start.60 = (bf16[4,4,24,768]{3,2,1,0:T(8,128)(2,1)}, bf16[4,4,24,768]{3,2,1,0:T(8,128)(2,1)}, u32[]{:S(2)}, u32[]{:S(2)}) collective-permute-start(bf16[4,4,24,768]{3,2,1,0:T(8,128)(2,1)} %get-tuple-element.524), channel_id=1, source_target_pairs={{0,24},{8,16},{16,8},{24,0},{1,25},{9,17},{17,9},{25,1},{2,26},{10... | collective-permute-start | bytes 1769480 | tf_op jit(solution)/shard_map/ppermute | solution.py:94
  531.6 159.0 %reduce-scatter.5.cloned.1.call-start = ((), (), s32[]{:S(2)}) async-start(), calls=%async_computation.11 | async-start | bytes 8847360 | tf_op jit(solution)/shard_map/reduce_scatter | solution.py:756
  617.5 32.6 %collective-permute-start.66 = (bf16[4,5,24,768]{3,2,1,0:T(8,128)(2,1)S(1)}, bf16[4,5,24,768]{3,2,1,0:T(8,128)(2,1)}, u32[]{:S(2)}, u32[]{:S(2)}) collective-permute-start(bf16[4,5,24,768]{3,2,1,0:T(8,128)(2,1)S(1)} %get-tuple-element.523), channel_id=1, source_target_pairs={{0,16},{8,24},{16,0},{24,8},{1,17},{9,25},{17,1},{25,9},{2,18},{10... | collective-permute-start | bytes 2211848 | tf_op jit(solution)/shard_map/ppermute | solution.py:94
  618.8 31.2 %collective-permute-start.67 = (bf16[4,5,24,768]{3,2,1,0:T(8,128)(2,1)S(1)}, bf16[4,5,24,768]{3,2,1,0:T(8,128)(2,1)}, u32[]{:S(2)}, u32[]{:S(2)}) collective-permute-start(bf16[4,5,24,768]{3,2,1,0:T(8,128)(2,1)S(1)} %get-tuple-element.522), channel_id=1, source_target_pairs={{0,24},{8,16},{16,8},{24,0},{1,25},{9,17},{17,9},{25,1},{2,26},{10... | collective-permute-start | bytes 2211848 | tf_op jit(solution)/shard_map/ppermute | solution.py:94
  658.3 54.4 %collective-permute-start.68 = (bf16[128,4096]{1,0:T(8,128)(2,1)}, bf16[128,4096]{1,0:T(8,128)(2,1)S(1)}, u32[]{:S(2)}, u32[]{:S(2)}) collective-permute-start(bf16[128,4096]{1,0:T(8,128)(2,1)} %get-tuple-element.102), channel_id=1, source_target_pairs={{0,8},{8,0},{16,24},{24,16},{1,9},{9,1},{17,25},{25,17},{2,10},{10... | collective-permute-start | bytes 3145736 | tf_op jit(solution)/shard_map/ppermute | solution.py:94
  659.6 53.1 %collective-permute-start.69 = (bf16[128,4096]{1,0:T(8,128)(2,1)}, bf16[128,4096]{1,0:T(8,128)(2,1)S(1)}, u32[]{:S(2)}, u32[]{:S(2)}) collective-permute-start(bf16[128,4096]{1,0:T(8,128)(2,1)} %get-tuple-element.103), channel_id=1, source_target_pairs={{0,16},{8,24},{16,0},{24,8},{1,17},{9,25},{17,1},{25,9},{2,18},{10... | collective-permute-start | bytes 3145736 | tf_op jit(solution)/shard_map/ppermute | solution.py:94
  666.8 46.0 %collective-permute-start.70 = (bf16[128,4096]{1,0:T(8,128)(2,1)}, bf16[128,4096]{1,0:T(8,128)(2,1)}, u32[]{:S(2)}, u32[]{:S(2)}) collective-permute-start(bf16[128,4096]{1,0:T(8,128)(2,1)} %get-tuple-element.104), channel_id=1, source_target_pairs={{0,24},{8,16},{16,8},{24,0},{1,25},{9,17},{17,9},{25,1},{2,26},{10... | collective-permute-start | bytes 3145736 | tf_op jit(solution)/shard_map/ppermute | solution.py:94
  703.5 46.2 %all-to-all-start.6 = ((bf16[4,1014,192]{1,2,0:T(8,128)(2,1)}), bf16[4,1014,192]{1,2,0:T(8,128)(2,1)}, u32[]{:S(2)}, u32[]{:S(2)}) async-start(bf16[4,1014,192]{1,2,0:T(8,128)(2,1)} %concatenate.130), calls=%async_computation.7 | async-start | bytes 3145728 | tf_op jit(solution)/shard_map/all_to_all | solution.py:81
  (236 other events, 2305.9 us)
Sparse Core Ops, SparseCore 0:
  37.8 33.2 all-gather.6
  72.7 76.6 all-gather.4
  164.8 30.1 all-gather.8
  531.8 34.4 reduce-scatter.6
  568.4 98.2 reduce-scatter.4

commit v4 on v3

--- a/solution.py
+++ b/solution.py
@@ -253,13 +253,16 @@
     return lax.optimization_barrier((value, earlier))[0]
 
 
-def z_sum(pack):
+def z_sum(pack, late=None):
     own = lax.axis_index("z")
     pieces = [
         lax.dynamic_index_in_dim(pack, own ^ shift, 0, keepdims=False)
         for shift in range(pack.shape[0])
     ]
-    return total_of(flips_of(pieces, "z")).astype(jnp.bfloat16)
+    got = flips_of(pieces, "z")
+    if late is not None:
+        got = after(got, late)
+    return total_of(got).astype(jnp.bfloat16)
 
 
 def neighbours(volume):
@@ -754,9 +757,6 @@
     weight_embed = matmul_left_t(pixel_rows, grad_rows).astype(jnp.bfloat16)
     slim_sum = total_of(after(slim_got, weight_embed)).astype(jnp.bfloat16)
     embed_sum = lax.psum_scatter(after(weight_embed, ff_sum), SLAB, scatter_dimension=0, tiled=True)
-    pixel_grad = matmul_right_t(after(grad_rows, weight_embed), embed_full)
-    ct_grad = jnp.pad(pixel_grad[:, :ct_size], ((0, 0), (0, (CHANS - 1) * ct_size)))
-    pixel_grad = jnp.where(is_mri, pixel_grad[:, ct_size:], ct_grad).astype(jnp.bfloat16)
     bias_ct = jnp.sum(jnp.where(own_mri, 0.0, grad_hidden), 0)
     bias_mri = jnp.sum(jnp.where(own_mri, grad_hidden, 0.0), 0)
     position_grad = jnp.sum(grad_hidden.reshape(crop_batch, local_tokens, D), 0)
@@ -800,11 +800,64 @@
         one_spots,
         5,
     ))
+    pixel_grad = matmul_right_t(after(grad_rows, one_parts), embed_full)
+    ct_grad = jnp.pad(pixel_grad[:, :ct_size], ((0, 0), (0, (CHANS - 1) * ct_size)))
+    pixel_grad = jnp.where(is_mri, pixel_grad[:, ct_size:], ct_grad).astype(jnp.bfloat16)
+    slim_all = z_sum(slim_sum, one_parts).reshape(slim_chunks, row_count, 6, DEC)
+    slim_all = slim_all.transpose(0, 2, 1, 3).reshape(-1, DEC)
+    first_start = 8 * row_count
+    second_start = first_start + first_chunks * row_count
+    lift_sum = slim_all[:first_start].reshape(8, row_count, DEC).transpose(1, 0, 2)
+    lift_sum = lift_sum.reshape(row_count, crops, -1).transpose(1, 0, 2)
+    narrow_sum = jnp.concatenate(
+        [
+            slim_all[first_start : first_start + first_count],
+            slim_all[second_start : second_start + second_count],
+        ],
+        0,
+    )
+    narrow_sum = narrow_sum.reshape(-1, crops, DEC // crops).transpose(1, 0, 2)
+    lift_units, narrow_units = to_units(lift_sum, unit), to_units(narrow_sum, unit)
+    up_units = ff_sum[:up_size].reshape(up_rows, crops, per_class).transpose(1, 0, 2)
+    up_units = to_units(up_units, unit)
     one_got = flips_of(one_parts, "crop")
+    one_got, lift_units, narrow_units, up_units, _ = lax.optimization_barrier(
+        (one_got, lift_units, narrow_units, up_units, position_grad)
+    )
     one_sum = total_of(one_got).astype(jnp.bfloat16)
     pixel_got = flips_of(
         after(list(pixel_grad.reshape(crops, rows_in, pieces * block)), one_got), "crop"
     )
+
+    def by_units(rows, chunks):
+        shaped = rows.reshape(chunks, -1, crops, unit).transpose(0, 2, 1, 3)
+        return shaped.reshape(crops, -1, unit)
+
+    def join_units(got, chunks):
+        return (
+            got.reshape(crops, chunks, -1, unit).transpose(0, 2, 1, 3).reshape(-1, chunks * unit)
+        )
+
+    sum_one = z_sum(one_sum).reshape(-1, D)
+
+    wide = jnp.concatenate(
+        [
+            up_units,
+            by_units(ff_sum[up_size:], 1),
+            by_units(sum_one[: 3 * row_count], 3),
+            by_units(sum_one[3 * row_count : 4 * row_count], 1),
+            lift_units,
+            narrow_units,
+            by_units(embed_sum, 1),
+        ],
+        1,
+    )
+    local_sum = jnp.float32(0.0)
+    for gradient in (embed_sum, ff_sum, lift_sum, narrow_sum, sum_one, position_grad):
+        wide_grad = gradient.astype(jnp.float32)
+        local_sum = local_sum + jnp.sum(wide_grad * wide_grad)
+    wide = crop_swap(after(wide, local_sum)).astype(jnp.float32)
+    norm_crop = total_of(flips(local_sum.reshape(1, 1), "crop"))
     if block % 128 == 0:
         (patch_grad,) = moves(
             column_plan(pieces, block, False), pixel_got, [(rows_in, crops * lanes)]
@@ -819,52 +872,6 @@
         )
         patch_grad = patch_grad.reshape(crops, rows_in, pieces, block).transpose(1, 2, 0, 3)
     patch_grad = patch_grad.reshape(patches.shape)
-
-    def by_units(rows, chunks):
-        shaped = rows.reshape(chunks, -1, crops, unit).transpose(0, 2, 1, 3)
-        return shaped.reshape(crops, -1, unit)
-
-    def join_units(got, chunks):
-        return (
-            got.reshape(crops, chunks, -1, unit).transpose(0, 2, 1, 3).reshape(-1, chunks * unit)
-        )
-
-    slim_all = z_sum(slim_sum).reshape(slim_chunks, row_count, 6, DEC)
-    sum_one = z_sum(one_sum).reshape(-1, D)
-
-    slim_all = slim_all.transpose(0, 2, 1, 3).reshape(-1, DEC)
-    first_start = 8 * row_count
-    second_start = first_start + first_chunks * row_count
-    lift_sum = slim_all[:first_start].reshape(8, row_count, DEC).transpose(1, 0, 2)
-    lift_sum = lift_sum.reshape(row_count, crops, -1).transpose(1, 0, 2)
-    narrow_sum = jnp.concatenate(
-        [
-            slim_all[first_start : first_start + first_count],
-            slim_all[second_start : second_start + second_count],
-        ],
-        0,
-    )
-    narrow_sum = narrow_sum.reshape(-1, crops, DEC // crops).transpose(1, 0, 2)
-    lift_units, narrow_units = to_units(lift_sum, unit), to_units(narrow_sum, unit)
-    up_units = ff_sum[:up_size].reshape(up_rows, crops, per_class).transpose(1, 0, 2)
-    up_units = to_units(up_units, unit)
-    wide = jnp.concatenate(
-        [
-            up_units,
-            by_units(ff_sum[up_size:], 1),
-            by_units(sum_one[: 3 * row_count], 3),
-            by_units(sum_one[3 * row_count : 4 * row_count], 1),
-            lift_units,
-            narrow_units,
-            by_units(embed_sum, 1),
-        ],
-        1,
-    )
-    local_sum = jnp.float32(0.0)
-    for gradient in (embed_sum, ff_sum, lift_sum, narrow_sum, sum_one, position_grad):
-        wide_grad = gradient.astype(jnp.float32)
-        local_sum = local_sum + jnp.sum(wide_grad * wide_grad)
-    wide = crop_swap(after(wide, local_sum)).astype(jnp.float32)
     embed_got = wide[:, -share:]
     embed_grad = (
         embed_got.astype(jnp.float32).reshape(crops, groups, block, unit).transpose(1, 0, 2, 3).reshape(-1, unit)
@@ -898,7 +905,7 @@
         position_grad,
         vector_final,
     )
-    grad_norm = jnp.sqrt(slab_sum(total_of(flips(local_sum.reshape(1, 1), "crop"))))[0, 0]
+    grad_norm = jnp.sqrt(slab_sum(norm_crop))[0, 0]
     factor = jnp.minimum(1.0, CLIP / grad_norm)
     news, means, squares = ([], [], [])
     for weight, gradient, mean_old, square_old, step_rate, step_decay in zip(

time: 800 us -> 786 us (0.983)
    unnamed x444 -> x450, local copies, waits for them, and re-layouts: 42.8 us -> 42.1 us
  transfers between devices with their start and end apart: 96 -> 96, of which waited for: 35 -> 40; matrix products, arithmetic and copies ran while one was open for 27% -> 27% of each run, Pallas kernels for 3% -> 3%
where the time goes in v4:
time: 786 us; the launch traced here: 777 us
  waiting for transfers between devices  208 us (26%)
  local copies, waits for them, and re-layouts  172 us (22%)
  starting transfers between devices  142 us (18%)
  matrix products  89.2 us (11%)
  other arithmetic  85.9 us (11%)
  blocking collectives  29.5 us (4%)
  between operations  26.2 us (3%)
  Pallas kernels  24 us (3%)
    ppermute x30, waiting for transfers between devices, flips_of(): lax.ppermute(pieces[shift], axis, flip_pairs(count, shift))  80.3 us
    unnamed x450, local copies, waits for them, and re-layouts  42.1 us
    ppermute x30, starting transfers between devices, flips_of(): lax.ppermute(pieces[shift], axis, flip_pairs(count, shift))  37 us
    dot_general x10, matrix products, matmul(): return jnp.dot(left, right, preferred_element_type=jnp.float32)  34.2 us
    ppermute x21, starting transfers between devices, flips(): lax.ppermute(value, axis, flip_pairs(count, shift))  31.5 us
    all_gather x1, waiting for transfers between devices, local(): embed_full = lax.all_gather(embed_part, SLAB, axis=0, tiled=True)  30.2 us
    dot_general x8, matrix products, matmul_left_t(): lax.dot_general(left, right, CONTRACT_ROWS, preferred_element_type=jnp.fl...  27.7 us
    all_to_all x2, waiting for transfers between devices, heads_back(): shaped = lax.all_to_all(block, SLAB, 1, 0, tiled=True)[:crop_count * HEADS]  25.4 us
  transfers between devices with their start and end apart: 96, of which 40 were waited for; matrix products, arithmetic and copies ran while one was open for 27% of the time, Pallas kernels for 3%

profile of v4, /device:TPU:0, one launch (start us, length us, event | category | flops | bytes accessed | tf_op | source)
XLA Modules:
  0.0 776.7 jit_solution(146815860686099006)
XLA Ops:
  18.6 5.2 all-to-all-start
  23.8 10.8 %all-to-all-done = bf16[4,438,192]{1,2,0:T(8,128)(2,1)S(1)} async-done(((bf16[4,438,192]{1,2,0:T(8,128)(2,1)}), bf16[4,438,192]{1,2,0:T(8,128)(2,1)S(1)}, u32[]{:S(2)}, u32[]{:S(2)}) %all-to-all-start) | async-done | bytes 672800 | tf_op jit(solution)/shard_map/all_to_all | solution.py:81
  45.9 14.2 %all_to_all.81 = bf16[4,640,192]{1,2,0:T(8,128)(2,1)} all-to-all(bf16[4,640,192]{1,2,0:T(8,128)(2,1)S(1)} %copy.701), channel_id=1, replica_groups=mesh['crop'=4,'z'=4,'core'=2] {'crop'}, dimensions={0} | all-to-all | bytes 1966080 | tf_op jit(solution)/shard_map/all_to_all | solution.py:81
  69.6 22.5 %collective-permute-done.3 = bf16[128,4096]{1,0:T(8,128)(2,1)S(1)} collective-permute-done((bf16[128,4096]{1,0:T(8,128)(2,1)S(1)}, bf16[128,4096]{1,0:T(8,128)(2,1)S(1)}, u32[]{:S(2)}, u32[]{:S(2)}) %collective-permute-start.3) | collective-permute-done | bytes 1048608 | tf_op jit(solution)/shard_map/ppermute | solution.py:94
  92.2 18.6 %collective-permute-done.4 = bf16[128,4096]{1,0:T(8,128)(2,1)S(1)} collective-permute-done((bf16[128,4096]{1,0:T(8,128)(2,1)S(1)}, bf16[128,4096]{1,0:T(8,128)(2,1)S(1)}, u32[]{:S(2)}, u32[]{:S(2)}) %collective-permute-start.4) | collective-permute-done | bytes 1048608 | tf_op jit(solution)/shard_map/ppermute | solution.py:94
  119.2 30.2 %all-gather.5.cloned.1.call-done = bf16[5120,768]{0,1:T(8,128)(2,1)} async-done(((bf16[640,768]{0,1:T(8,128)(2,1)}), bf16[5120,768]{0,1:T(8,128)(2,1)}) %all-gather.5.cloned.1.call-update) | async-done | bytes 7864336 | tf_op jit(solution)/shard_map/all_gather | solution.py:575
  149.5 10.0 %fusion.34 = bf16[512,768]{1,0:T(8,128)(2,1)} fusion(bf16[5120,768]{0,1:T(8,128)(2,1)} %all-gather.5.cloned.1.call-done, bf16[512,4096]{1,0:T(8,128)(2,1)} %broadcast_select_fusion, bf16[512,1024]{1,0:T(8,128)(2,1)} %slice_select_fusion.1), kind=kOutput, calls=%fused_computation.154 | convolution fusion | flops 4037410816 | bytes 13893632 | tf_op jit(solution)/shard_map/dot_general | solution.py:52
  203.3 16.2 %all-to-all-done.2 = bf16[24,64,192]{2,1,0:T(8,128)(2,1)S(1)} async-done(((bf16[24,64,192]{2,1,0:T(8,128)(2,1)}), bf16[24,64,192]{2,1,0:T(8,128)(2,1)S(1)}, u32[]{:S(2)}, u32[]{:S(2)}) %all-to-all-start.2) | async-done | bytes 589856 | tf_op jit(solution)/shard_map/all_to_all | solution.py:348
  232.8 4.8 all-to-all-start.3
  238.6 7.3 all-to-all-done.3
  268.4 6.2 fusion.20
  303.6 4.8 fusion.242
  309.1 4.8 collective-permute-start.33
  394.6 6.0 fusion.4
  415.3 8.9 %fusion.1 = bf16[6912,128]{1,0:T(8,128)(2,1)S(1)} fusion(bf16[2,2,16,16,6912]{4,3,2,1,0:T(8,128)(2,1)} %copy-done.120, bf16[2,4,16,16,128]{4,3,2,1,0:T(8,128)(2,1)S(1)} %fusion.90), kind=kOutput, calls=%fused_computation.3 | convolution fusion | flops 1812824064 | bytes 16187392 | tf_op jit(solution)/shard_map/dot_general | solution.py:56
  464.9 15.3 %all_to_all.82 = bf16[8,2,6144]{2,1,0:T(2,128)(2,1)} all-to-all(bf16[8,2,6144]{2,1,0:T(2,128)(2,1)S(1)} %reshape.750), channel_id=1, replica_groups=mesh['crop'=4,'z'=4,'core'=2] {'z','core'}, dimensions={0} | all-to-all | bytes 393216 | tf_op jit(solution)/shard_map/all_to_all | solution.py:348
  505.0 18.1 %all-to-all-done.5 = bf16[3,512,192]{2,0,1:T(4,128)(2,1)S(1)} async-done(((bf16[3,512,192]{2,0,1:T(4,128)(2,1)}), bf16[3,512,192]{2,0,1:T(4,128)(2,1)S(1)}, u32[]{:S(2)}, u32[]{:S(2)}) %all-to-all-start.5) | async-done | bytes 589856 | tf_op jit(solution)/shard_map/all_to_all | solution.py:352
  549.8 6.8 convolution_convert_fusion
  556.6 9.8 %reduce-scatter.7.cloned.1.call-done = bf16[192,768]{1,0:T(8,128)(2,1)} async-done(((bf16[1536,768]{1,0:T(8,128)(2,1)}), bf16[192,768]{1,0:T(8,128)(2,1)}) %reduce-scatter.7.cloned.1.call-update) | async-done | bytes 294928
  608.4 7.9 %fusion.281 = bf16[512,5120]{1,0:T(8,128)(2,1)S(1)} fusion(bf16[512,768]{1,0:T(8,128)(2,1)S(1)} %pad_maximum_fusion.8, bf16[5120,768]{0,1:T(8,128)(2,1)} %all-gather.5.cloned.1.call-done), kind=kOutput, calls=%fused_computation.589 | convolution fusion | flops 4026531840 | bytes 13893632 | tf_op jit(solution)/shard_map/dot_general | solution.py:60
  627.0 13.4 %collective-permute-done.66 = bf16[4,5,24,768]{3,2,1,0:T(8,128)(2,1)} collective-permute-done((bf16[4,5,24,768]{3,2,1,0:T(8,128)(2,1)}, bf16[4,5,24,768]{3,2,1,0:T(8,128)(2,1)}, u32[]{:S(2)}, u32[]{:S(2)}) %collective-permute-start.66) | collective-permute-done | bytes 737312 | tf_op jit(solution)/shard_map/ppermute | solution.py:94
  658.8 6.5 collective-permute-done.78
  702.2 5.8 shard_map.590
  722.4 4.8 collective-permute-start.84
  (954 shorter events, 491.5 us)
Async XLA Ops:
  23.7 90.8 %all-gather.7.cloned.1.call-start = ((), (), s32[]{:S(2)}) async-start(), calls=%async_computation.10 | async-start | bytes 1658880 | tf_op jit(solution)/shard_map/all_gather | solution.py:572
  37.7 111.8 %all-gather.5.cloned.1.call-start = ((), (), s32[]{:S(2)}) async-start(), calls=%async_computation.9 | async-start | bytes 8847360 | tf_op jit(solution)/shard_map/all_gather | solution.py:575
  60.1 200.9 %all-gather.9.cloned.1.call-start = ((), (), s32[]{:S(2)}) async-start(), calls=%async_computation.12 | async-start | bytes 2654208 | tf_op jit(solution)/shard_map/all_gather | solution.py:578
  67.2 43.7 %collective-permute-start.4 = (bf16[128,4096]{1,0:T(8,128)(2,1)S(1)}, bf16[128,4096]{1,0:T(8,128)(2,1)S(1)}, u32[]{:S(2)}, u32[]{:S(2)}) collective-permute-start(bf16[128,4096]{1,0:T(8,128)(2,1)S(1)} %get-tuple-element.86), channel_id=1, source_target_pairs={{0,16},{8,24},{16,0},{24,8},{1,17},{9,25},{17,1},{25,9},{2,18},{10... | collective-permute-start | bytes 3145736 | tf_op jit(solution)/shard_map/ppermute | solution.py:94
  67.5 43.4 %collective-permute-start.5 = (bf16[128,4096]{1,0:T(8,128)(2,1)S(1)}, bf16[128,4096]{1,0:T(8,128)(2,1)S(1)}, u32[]{:S(2)}, u32[]{:S(2)}) collective-permute-start(bf16[128,4096]{1,0:T(8,128)(2,1)S(1)} %get-tuple-element.87), channel_id=1, source_target_pairs={{0,24},{8,16},{16,8},{24,0},{1,25},{9,17},{17,9},{25,1},{2,26},{10... | collective-permute-start | bytes 3145736 | tf_op jit(solution)/shard_map/ppermute | solution.py:94
  115.7 43.7 %collective-permute-start.10 = (bf16[4,5,24,768]{3,2,1,0:T(8,128)(2,1)S(1)}, bf16[4,5,24,768]{3,2,1,0:T(8,128)(2,1)S(1)}, u32[]{:S(2)}, u32[]{:S(2)}) collective-permute-start(bf16[4,5,24,768]{3,2,1,0:T(8,128)(2,1)S(1)} %slice.666.refs_0_), channel_id=1, source_target_pairs={{0,16},{8,24},{16,0},{24,8},{1,17},{9,25},{17,1},{25,9},{2,18},{10... | collective-permute-start | bytes 2211848 | tf_op jit(solution)/shard_map/ppermute | solution.py:87
  116.0 43.4 %collective-permute-start.11 = (bf16[4,5,24,768]{3,2,1,0:T(8,128)(2,1)S(1)}, bf16[4,5,24,768]{3,2,1,0:T(8,128)(2,1)S(1)}, u32[]{:S(2)}, u32[]{:S(2)}) collective-permute-start(bf16[4,5,24,768]{3,2,1,0:T(8,128)(2,1)S(1)} %slice.666.refs_0_), channel_id=1, source_target_pairs={{0,24},{8,16},{16,8},{24,0},{1,25},{9,17},{17,9},{25,1},{2,26},{10... | collective-permute-start | bytes 2211848 | tf_op jit(solution)/shard_map/ppermute | solution.py:87
  117.9 41.6 %collective-permute-start.9 = (bf16[4,5,24,768]{3,2,1,0:T(8,128)(2,1)S(1)}, bf16[4,5,24,768]{3,2,1,0:T(8,128)(2,1)S(1)}, u32[]{:S(2)}, u32[]{:S(2)}) collective-permute-start(bf16[4,5,24,768]{3,2,1,0:T(8,128)(2,1)S(1)} %slice.666.refs_0_), channel_id=1, source_target_pairs={{0,8},{8,0},{16,24},{24,16},{1,9},{9,1},{17,25},{25,17},{2,10},{10... | collective-permute-start | bytes 2211848 | tf_op jit(solution)/shard_map/ppermute | solution.py:87
  199.7 29.2 %collective-permute-start.16 = (bf16[4,4,24,768]{3,2,1,0:T(8,128)(2,1)S(1)}, bf16[4,4,24,768]{3,2,1,0:T(8,128)(2,1)S(1)}, u32[]{:S(2)}, u32[]{:S(2)}) collective-permute-start(bf16[4,4,24,768]{3,2,1,0:T(8,128)(2,1)S(1)} %slice.676.refs_0_), channel_id=1, source_target_pairs={{0,8},{8,0},{16,24},{24,16},{1,9},{9,1},{17,25},{25,17},{2,10},{10... | collective-permute-start | bytes 1769480 | tf_op jit(solution)/shard_map/ppermute | solution.py:87
  201.4 28.0 %collective-permute-start.17 = (bf16[4,4,24,768]{3,2,1,0:T(8,128)(2,1)S(1)}, bf16[4,4,24,768]{3,2,1,0:T(8,128)(2,1)S(1)}, u32[]{:S(2)}, u32[]{:S(2)}) collective-permute-start(bf16[4,4,24,768]{3,2,1,0:T(8,128)(2,1)S(1)} %slice.676.refs_0_), channel_id=1, source_target_pairs={{0,16},{8,24},{16,0},{24,8},{1,17},{9,25},{17,1},{25,9},{2,18},{10... | collective-permute-start | bytes 1769480 | tf_op jit(solution)/shard_map/ppermute | solution.py:87
  202.9 26.6 %collective-permute-start.18 = (bf16[4,4,24,768]{3,2,1,0:T(8,128)(2,1)S(1)}, bf16[4,4,24,768]{3,2,1,0:T(8,128)(2,1)}, u32[]{:S(2)}, u32[]{:S(2)}) collective-permute-start(bf16[4,4,24,768]{3,2,1,0:T(8,128)(2,1)S(1)} %slice.676.refs_0_), channel_id=1, source_target_pairs={{0,24},{8,16},{16,8},{24,0},{1,25},{9,17},{17,9},{25,1},{2,26},{10... | collective-permute-start | bytes 1769480 | tf_op jit(solution)/shard_map/ppermute | solution.py:87
  314.6 45.1 %collective-permute-start.41 = (bf16[2,1,16,16,128]{4,3,2,1,0:T(8,128)(2,1)}, bf16[2,1,16,16,128]{4,3,2,1,0:T(8,128)(2,1)}, u32[]{:S(2)}, u32[]{:S(2)}) collective-permute-start(bf16[2,1,16,16,128]{4,3,2,1,0:T(8,128)(2,1)} %get-tuple-element.589), channel_id=1, source_target_pairs={{0,1},{1,2},{2,3},{3,4},{4,5},{5,6},{6,7},{8,9},{9,10},{10,11},{11... | collective-permute-start | bytes 393224 | tf_op jit(solution)/shard_map/ppermute | solution.py:272
  317.1 42.6 %collective-permute-start.42 = (bf16[2,1,16,16,128]{4,3,2,1,0:T(8,128)(2,1)}, bf16[2,1,16,16,128]{4,3,2,1,0:T(8,128)(2,1)}, u32[]{:S(2)}, u32[]{:S(2)}) collective-permute-start(bf16[2,1,16,16,128]{4,3,2,1,0:T(8,128)(2,1)} %get-tuple-element.590), channel_id=1, source_target_pairs={{1,0},{2,1},{3,2},{4,3},{5,4},{6,5},{7,6},{9,8},{10,9},{11,10},{12... | collective-permute-start | bytes 393224 | tf_op jit(solution)/shard_map/ppermute | solution.py:273
  493.0 30.1 %all-to-all-start.5 = ((bf16[3,512,192]{2,0,1:T(4,128)(2,1)}), bf16[3,512,192]{2,0,1:T(4,128)(2,1)S(1)}, u32[]{:S(2)}, u32[]{:S(2)}) async-start(bf16[3,512,192]{2,0,1:T(4,128)(2,1)} %copy.742), calls=%async_computation.5 | async-start | bytes 2097152 | tf_op jit(solution)/shard_map/all_to_all | solution.py:352
  496.6 69.8 %reduce-scatter.7.cloned.1.call-start = ((), (), s32[]{:S(2)}) async-start(), calls=%async_computation.13 | async-start | bytes 2654208
  496.7 35.2 %collective-permute-start.58 = (bf16[4,4,24,768]{3,2,1,0:T(8,128)(2,1)}, bf16[4,4,24,768]{3,2,1,0:T(8,128)(2,1)}, u32[]{:S(2)}, u32[]{:S(2)}) collective-permute-start(bf16[4,4,24,768]{3,2,1,0:T(8,128)(2,1)} %get-tuple-element.547), channel_id=1, source_target_pairs={{0,8},{8,0},{16,24},{24,16},{1,9},{9,1},{17,25},{25,17},{2,10},{10... | collective-permute-start | bytes 1769480 | tf_op jit(solution)/shard_map/ppermute | solution.py:94
  497.5 34.4 %collective-permute-start.59 = (bf16[4,4,24,768]{3,2,1,0:T(8,128)(2,1)}, bf16[4,4,24,768]{3,2,1,0:T(8,128)(2,1)}, u32[]{:S(2)}, u32[]{:S(2)}) collective-permute-start(bf16[4,4,24,768]{3,2,1,0:T(8,128)(2,1)} %get-tuple-element.546), channel_id=1, source_target_pairs={{0,16},{8,24},{16,0},{24,8},{1,17},{9,25},{17,1},{25,9},{2,18},{10... | collective-permute-start | bytes 1769480 | tf_op jit(solution)/shard_map/ppermute | solution.py:94
  499.0 32.9 %collective-permute-start.60 = (bf16[4,4,24,768]{3,2,1,0:T(8,128)(2,1)}, bf16[4,4,24,768]{3,2,1,0:T(8,128)(2,1)}, u32[]{:S(2)}, u32[]{:S(2)}) collective-permute-start(bf16[4,4,24,768]{3,2,1,0:T(8,128)(2,1)} %get-tuple-element.545), channel_id=1, source_target_pairs={{0,24},{8,16},{16,8},{24,0},{1,25},{9,17},{17,9},{25,1},{2,26},{10... | collective-permute-start | bytes 1769480 | tf_op jit(solution)/shard_map/ppermute | solution.py:94
  531.9 146.2 %reduce-scatter.5.cloned.1.call-start = ((), (), s32[]{:S(2)}) async-start(), calls=%async_computation.11 | async-start | bytes 8847360 | tf_op jit(solution)/shard_map/reduce_scatter | solution.py:759
  608.0 32.4 %collective-permute-start.66 = (bf16[4,5,24,768]{3,2,1,0:T(8,128)(2,1)}, bf16[4,5,24,768]{3,2,1,0:T(8,128)(2,1)}, u32[]{:S(2)}, u32[]{:S(2)}) collective-permute-start(bf16[4,5,24,768]{3,2,1,0:T(8,128)(2,1)} %get-tuple-element.542), channel_id=1, source_target_pairs={{0,16},{8,24},{16,0},{24,8},{1,17},{9,25},{17,1},{25,9},{2,18},{10... | collective-permute-start | bytes 2211848 | tf_op jit(solution)/shard_map/ppermute | solution.py:94
  653.7 46.3 %collective-permute-start.74 = (bf16[128,4096]{1,0:T(8,128)(2,1)}, bf16[128,4096]{1,0:T(8,128)(2,1)S(1)}, u32[]{:S(2)}, u32[]{:S(2)}) collective-permute-start(bf16[128,4096]{1,0:T(8,128)(2,1)} %get-tuple-element.126), channel_id=1, source_target_pairs={{0,8},{8,0},{16,24},{24,16},{1,9},{9,1},{17,25},{25,17},{2,10},{10... | collective-permute-start | bytes 3145736 | tf_op jit(solution)/shard_map/ppermute | solution.py:94
  655.0 46.7 %collective-permute-start.75 = (bf16[128,4096]{1,0:T(8,128)(2,1)}, bf16[128,4096]{1,0:T(8,128)(2,1)S(1)}, u32[]{:S(2)}, u32[]{:S(2)}) collective-permute-start(bf16[128,4096]{1,0:T(8,128)(2,1)} %get-tuple-element.127), channel_id=1, source_target_pairs={{0,16},{8,24},{16,0},{24,8},{1,17},{9,25},{17,1},{25,9},{2,18},{10... | collective-permute-start | bytes 3145736 | tf_op jit(solution)/shard_map/ppermute | solution.py:94
  657.4 44.8 %collective-permute-start.76 = (bf16[128,4096]{1,0:T(8,128)(2,1)}, bf16[128,4096]{1,0:T(8,128)(2,1)}, u32[]{:S(2)}, u32[]{:S(2)}) collective-permute-start(bf16[128,4096]{1,0:T(8,128)(2,1)} %get-tuple-element.128), channel_id=1, source_target_pairs={{0,24},{8,16},{16,8},{24,0},{1,25},{9,17},{17,9},{25,1},{2,26},{10... | collective-permute-start | bytes 3145736 | tf_op jit(solution)/shard_map/ppermute | solution.py:94
  690.9 44.6 %all-to-all-start.6 = ((bf16[4,1014,192]{1,2,0:T(8,128)(2,1)}), bf16[4,1014,192]{1,2,0:T(8,128)(2,1)}, u32[]{:S(2)}, u32[]{:S(2)}) async-start(bf16[4,1014,192]{1,2,0:T(8,128)(2,1)} %concatenate.130), calls=%async_computation.7 | async-start | bytes 3145728 | tf_op jit(solution)/shard_map/all_to_all | solution.py:81
  (239 other events, 2306.9 us)
Sparse Core Ops, SparseCore 0:
  37.8 33.2 all-gather.6
  72.7 76.6 all-gather.4
  164.8 30.1 all-gather.8
  532.0 34.3 reduce-scatter.6
  568.6 105.0 reduce-scatter.4

commit v5 on v4

--- a/solution.py
+++ b/solution.py
@@ -754,9 +754,10 @@
     grad_low = grad_hidden.astype(jnp.bfloat16)
 
     grad_rows = jnp.concatenate(flips(grad_low, "crop"), 0)
+    slim_sum = total_of(after(slim_got, grad_triple)).astype(jnp.bfloat16)
+    grad_rows = after(grad_rows, (ff_grads, slim_sum))
     weight_embed = matmul_left_t(pixel_rows, grad_rows).astype(jnp.bfloat16)
-    slim_sum = total_of(after(slim_got, weight_embed)).astype(jnp.bfloat16)
-    embed_sum = lax.psum_scatter(after(weight_embed, ff_sum), SLAB, scatter_dimension=0, tiled=True)
+    embed_sum = lax.psum_scatter(weight_embed, SLAB, scatter_dimension=0, tiled=True)
     bias_ct = jnp.sum(jnp.where(own_mri, 0.0, grad_hidden), 0)
     bias_mri = jnp.sum(jnp.where(own_mri, grad_hidden, 0.0), 0)
     position_grad = jnp.sum(grad_hidden.reshape(crop_batch, local_tokens, D), 0)

time: 786 us -> 781 us (level)
    reduce_scatter x1, waiting for transfers between devices: 0.01 us -> 15.8 us  [local(): lax.psum_scatter(weight_embed, SLAB, scatter_dimension=0, tiled=True)]
    unnamed x6, waiting for transfers between devices: 9.91 us -> 0.09 us
    unnamed x450 -> x442, local copies, waits for them, and re-layouts: 42.1 us -> 41.3 us
  transfers between devices with their start and end apart: 96 -> 96, of which waited for: 40 -> 34; matrix products, arithmetic and copies ran while one was open for 27% -> 26% of each run, Pallas kernels for 3% -> 3%
where the time goes in v5:
time: 781 us; the launch traced here: 771 us
  waiting for transfers between devices  203 us (26%)
  local copies, waits for them, and re-layouts  168 us (22%)
  starting transfers between devices  148 us (19%)
  matrix products  88.7 us (11%)
  other arithmetic  85.8 us (11%)
  blocking collectives  27.5 us (4%)
  between operations  26.5 us (3%)
  Pallas kernels  24 us (3%)
    ppermute x30, waiting for transfers between devices, flips_of(): lax.ppermute(pieces[shift], axis, flip_pairs(count, shift))  76 us
    unnamed x442, local copies, waits for them, and re-layouts  41.3 us
    ppermute x30, starting transfers between devices, flips_of(): lax.ppermute(pieces[shift], axis, flip_pairs(count, shift))  37.4 us
    ppermute x21, starting transfers between devices, flips(): lax.ppermute(value, axis, flip_pairs(count, shift))  35.1 us
    dot_general x10, matrix products, matmul(): return jnp.dot(left, right, preferred_element_type=jnp.float32)  34.2 us
    all_gather x1, waiting for transfers between devices, local(): embed_full = lax.all_gather(embed_part, SLAB, axis=0, tiled=True)  30.3 us
    dot_general x8, matrix products, matmul_left_t(): lax.dot_general(left, right, CONTRACT_ROWS, preferred_element_type=jnp.fl...  27.1 us
    all_to_all x2, waiting for transfers between devices, heads_back(): shaped = lax.all_to_all(block, SLAB, 1, 0, tiled=True)[:crop_count * HEADS]  25.5 us
  transfers between devices with their start and end apart: 96, of which 34 were waited for; matrix products, arithmetic and copies ran while one was open for 26% of the time, Pallas kernels for 3%

profile of v5, /device:TPU:0, one launch (start us, length us, event | category | flops | bytes accessed | tf_op | source)
XLA Modules:
  0.0 771.5 jit_solution(9338067048006004991)
XLA Ops:
  19.5 5.2 all-to-all-start
  24.7 10.8 %all-to-all-done = bf16[4,438,192]{1,2,0:T(8,128)(2,1)S(1)} async-done(((bf16[4,438,192]{1,2,0:T(8,128)(2,1)}), bf16[4,438,192]{1,2,0:T(8,128)(2,1)S(1)}, u32[]{:S(2)}, u32[]{:S(2)}) %all-to-all-start) | async-done | bytes 672800 | tf_op jit(solution)/shard_map/all_to_all | solution.py:81
  46.8 14.2 %all_to_all.81 = bf16[4,640,192]{1,2,0:T(8,128)(2,1)} all-to-all(bf16[4,640,192]{1,2,0:T(8,128)(2,1)S(1)} %copy.701), channel_id=1, replica_groups=mesh['crop'=4,'z'=4,'core'=2] {'crop'}, dimensions={0} | all-to-all | bytes 1966080 | tf_op jit(solution)/shard_map/all_to_all | solution.py:81
  70.6 22.5 %collective-permute-done.3 = bf16[128,4096]{1,0:T(8,128)(2,1)S(1)} collective-permute-done((bf16[128,4096]{1,0:T(8,128)(2,1)S(1)}, bf16[128,4096]{1,0:T(8,128)(2,1)S(1)}, u32[]{:S(2)}, u32[]{:S(2)}) %collective-permute-start.3) | collective-permute-done | bytes 1048608 | tf_op jit(solution)/shard_map/ppermute | solution.py:94
  93.2 18.6 %collective-permute-done.4 = bf16[128,4096]{1,0:T(8,128)(2,1)S(1)} collective-permute-done((bf16[128,4096]{1,0:T(8,128)(2,1)S(1)}, bf16[128,4096]{1,0:T(8,128)(2,1)S(1)}, u32[]{:S(2)}, u32[]{:S(2)}) %collective-permute-start.4) | collective-permute-done | bytes 1048608 | tf_op jit(solution)/shard_map/ppermute | solution.py:94
  120.1 30.3 %all-gather.5.cloned.1.call-done = bf16[5120,768]{0,1:T(8,128)(2,1)} async-done(((bf16[640,768]{0,1:T(8,128)(2,1)}), bf16[5120,768]{0,1:T(8,128)(2,1)}) %all-gather.5.cloned.1.call-update) | async-done | bytes 7864336 | tf_op jit(solution)/shard_map/all_gather | solution.py:575
  150.4 9.9 %fusion.34 = bf16[512,768]{1,0:T(8,128)(2,1)} fusion(bf16[5120,768]{0,1:T(8,128)(2,1)} %all-gather.5.cloned.1.call-done, bf16[512,4096]{1,0:T(8,128)(2,1)} %broadcast_select_fusion, bf16[512,1024]{1,0:T(8,128)(2,1)} %slice_select_fusion.1), kind=kOutput, calls=%fused_computation.154 | convolution fusion | flops 4037410816 | bytes 13893632 | tf_op jit(solution)/shard_map/dot_general | solution.py:52
  206.2 16.2 %all-to-all-done.2 = bf16[24,64,192]{2,1,0:T(8,128)(2,1)S(1)} async-done(((bf16[24,64,192]{2,1,0:T(8,128)(2,1)}), bf16[24,64,192]{2,1,0:T(8,128)(2,1)S(1)}, u32[]{:S(2)}, u32[]{:S(2)}) %all-to-all-start.2) | async-done | bytes 589856 | tf_op jit(solution)/shard_map/all_to_all | solution.py:348
  241.5 7.3 all-to-all-done.3
  271.4 6.2 fusion.20
  306.6 4.8 fusion.242
  397.4 6.0 fusion.4
  418.6 8.9 %fusion.1 = bf16[6912,128]{1,0:T(8,128)(2,1)S(1)} fusion(bf16[2,2,16,16,6912]{4,3,2,1,0:T(8,128)(2,1)} %copy-done.114, bf16[2,4,16,16,128]{4,3,2,1,0:T(8,128)(2,1)S(1)} %fusion.90), kind=kOutput, calls=%fused_computation.3 | convolution fusion | flops 1812824064 | bytes 16187392 | tf_op jit(solution)/shard_map/dot_general | solution.py:56
  454.5 6.8 collective-permute-done.55
  470.1 13.2 %all_to_all.82 = bf16[8,2,6144]{2,1,0:T(2,128)(2,1)} all-to-all(bf16[8,2,6144]{2,1,0:T(2,128)(2,1)S(1)} %reshape.750), channel_id=1, replica_groups=mesh['crop'=4,'z'=4,'core'=2] {'z','core'}, dimensions={0} | all-to-all | bytes 393216 | tf_op jit(solution)/shard_map/all_to_all | solution.py:348
  508.3 18.2 %all-to-all-done.5 = bf16[3,512,192]{2,0,1:T(4,128)(2,1)S(1)} async-done(((bf16[3,512,192]{2,0,1:T(4,128)(2,1)}), bf16[3,512,192]{2,0,1:T(4,128)(2,1)S(1)}, u32[]{:S(2)}, u32[]{:S(2)}) %all-to-all-start.5) | async-done | bytes 589856 | tf_op jit(solution)/shard_map/all_to_all | solution.py:352
  552.5 6.8 convolution_convert_fusion
  585.1 8.0 %fusion.281 = bf16[512,5120]{1,0:T(8,128)(2,1)S(1)} fusion(bf16[512,768]{1,0:T(8,128)(2,1)S(1)} %copy-done.76, bf16[5120,768]{0,1:T(8,128)(2,1)} %all-gather.5.cloned.1.call-done), kind=kOutput, calls=%fused_computation.589 | convolution fusion | flops 4026531840 | bytes 13893632 | tf_op jit(solution)/shard_map/dot_general | solution.py:60
  602.8 14.2 %collective-permute-done.66 = bf16[4,5,24,768]{3,2,1,0:T(8,128)(2,1)} collective-permute-done((bf16[4,5,24,768]{3,2,1,0:T(8,128)(2,1)}, bf16[4,5,24,768]{3,2,1,0:T(8,128)(2,1)}, u32[]{:S(2)}, u32[]{:S(2)}) %collective-permute-start.66) | collective-permute-done | bytes 737312 | tf_op jit(solution)/shard_map/ppermute | solution.py:94
  640.4 5.5 collective-permute-done.79
  656.0 15.8 %reduce-scatter.5.cloned.1.call-done = bf16[640,768]{1,0:T(8,128)(2,1)} async-done(((bf16[5120,768]{1,0:T(8,128)(2,1)}), bf16[640,768]{1,0:T(8,128)(2,1)}) %reduce-scatter.5.cloned.1.call-update) | async-done | bytes 983056 | tf_op jit(solution)/shard_map/reduce_scatter | solution.py:760
  693.7 5.8 shard_map.590
  699.5 7.5 collective-permute-start.80
  722.2 5.1 collective-permute-start.85
  (946 shorter events, 477.0 us)
Async XLA Ops:
  24.7 90.7 %all-gather.7.cloned.1.call-start = ((), (), s32[]{:S(2)}) async-start(), calls=%async_computation.10 | async-start | bytes 1658880 | tf_op jit(solution)/shard_map/all_gather | solution.py:572
  38.6 111.8 %all-gather.5.cloned.1.call-start = ((), (), s32[]{:S(2)}) async-start(), calls=%async_computation.9 | async-start | bytes 8847360 | tf_op jit(solution)/shard_map/all_gather | solution.py:575
  61.0 203.0 %all-gather.9.cloned.1.call-start = ((), (), s32[]{:S(2)}) async-start(), calls=%async_computation.12 | async-start | bytes 2654208 | tf_op jit(solution)/shard_map/all_gather | solution.py:578
  68.1 43.7 %collective-permute-start.4 = (bf16[128,4096]{1,0:T(8,128)(2,1)S(1)}, bf16[128,4096]{1,0:T(8,128)(2,1)S(1)}, u32[]{:S(2)}, u32[]{:S(2)}) collective-permute-start(bf16[128,4096]{1,0:T(8,128)(2,1)S(1)} %get-tuple-element.86), channel_id=1, source_target_pairs={{0,16},{8,24},{16,0},{24,8},{1,17},{9,25},{17,1},{25,9},{2,18},{10... | collective-permute-start | bytes 3145736 | tf_op jit(solution)/shard_map/ppermute | solution.py:94
  68.5 43.4 %collective-permute-start.5 = (bf16[128,4096]{1,0:T(8,128)(2,1)S(1)}, bf16[128,4096]{1,0:T(8,128)(2,1)S(1)}, u32[]{:S(2)}, u32[]{:S(2)}) collective-permute-start(bf16[128,4096]{1,0:T(8,128)(2,1)S(1)} %get-tuple-element.87), channel_id=1, source_target_pairs={{0,24},{8,16},{16,8},{24,0},{1,25},{9,17},{17,9},{25,1},{2,26},{10... | collective-permute-start | bytes 3145736 | tf_op jit(solution)/shard_map/ppermute | solution.py:94
  116.6 43.8 %collective-permute-start.10 = (bf16[4,5,24,768]{3,2,1,0:T(8,128)(2,1)S(1)}, bf16[4,5,24,768]{3,2,1,0:T(8,128)(2,1)S(1)}, u32[]{:S(2)}, u32[]{:S(2)}) collective-permute-start(bf16[4,5,24,768]{3,2,1,0:T(8,128)(2,1)S(1)} %slice.666.refs_0_), channel_id=1, source_target_pairs={{0,16},{8,24},{16,0},{24,8},{1,17},{9,25},{17,1},{25,9},{2,18},{10... | collective-permute-start | bytes 2211848 | tf_op jit(solution)/shard_map/ppermute | solution.py:87
  117.0 43.4 %collective-permute-start.11 = (bf16[4,5,24,768]{3,2,1,0:T(8,128)(2,1)S(1)}, bf16[4,5,24,768]{3,2,1,0:T(8,128)(2,1)S(1)}, u32[]{:S(2)}, u32[]{:S(2)}) collective-permute-start(bf16[4,5,24,768]{3,2,1,0:T(8,128)(2,1)S(1)} %slice.666.refs_0_), channel_id=1, source_target_pairs={{0,24},{8,16},{16,8},{24,0},{1,25},{9,17},{17,9},{25,1},{2,26},{10... | collective-permute-start | bytes 2211848 | tf_op jit(solution)/shard_map/ppermute | solution.py:87
  118.8 41.5 %collective-permute-start.9 = (bf16[4,5,24,768]{3,2,1,0:T(8,128)(2,1)S(1)}, bf16[4,5,24,768]{3,2,1,0:T(8,128)(2,1)S(1)}, u32[]{:S(2)}, u32[]{:S(2)}) collective-permute-start(bf16[4,5,24,768]{3,2,1,0:T(8,128)(2,1)S(1)} %slice.666.refs_0_), channel_id=1, source_target_pairs={{0,8},{8,0},{16,24},{24,16},{1,9},{9,1},{17,25},{25,17},{2,10},{10... | collective-permute-start | bytes 2211848 | tf_op jit(solution)/shard_map/ppermute | solution.py:87
  202.7 30.8 %collective-permute-start.16 = (bf16[4,4,24,768]{3,2,1,0:T(8,128)(2,1)S(1)}, bf16[4,4,24,768]{3,2,1,0:T(8,128)(2,1)S(1)}, u32[]{:S(2)}, u32[]{:S(2)}) collective-permute-start(bf16[4,4,24,768]{3,2,1,0:T(8,128)(2,1)S(1)} %slice.676.refs_0_), channel_id=1, source_target_pairs={{0,8},{8,0},{16,24},{24,16},{1,9},{9,1},{17,25},{25,17},{2,10},{10... | collective-permute-start | bytes 1769480 | tf_op jit(solution)/shard_map/ppermute | solution.py:87
  204.4 29.1 %collective-permute-start.17 = (bf16[4,4,24,768]{3,2,1,0:T(8,128)(2,1)S(1)}, bf16[4,4,24,768]{3,2,1,0:T(8,128)(2,1)S(1)}, u32[]{:S(2)}, u32[]{:S(2)}) collective-permute-start(bf16[4,4,24,768]{3,2,1,0:T(8,128)(2,1)S(1)} %slice.676.refs_0_), channel_id=1, source_target_pairs={{0,16},{8,24},{16,0},{24,8},{1,17},{9,25},{17,1},{25,9},{2,18},{10... | collective-permute-start | bytes 1769480 | tf_op jit(solution)/shard_map/ppermute | solution.py:87
  205.8 27.6 %collective-permute-start.18 = (bf16[4,4,24,768]{3,2,1,0:T(8,128)(2,1)S(1)}, bf16[4,4,24,768]{3,2,1,0:T(8,128)(2,1)}, u32[]{:S(2)}, u32[]{:S(2)}) collective-permute-start(bf16[4,4,24,768]{3,2,1,0:T(8,128)(2,1)S(1)} %slice.676.refs_0_), channel_id=1, source_target_pairs={{0,24},{8,16},{16,8},{24,0},{1,25},{9,17},{17,9},{25,1},{2,26},{10... | collective-permute-start | bytes 1769480 | tf_op jit(solution)/shard_map/ppermute | solution.py:87
  317.6 45.0 %collective-permute-start.41 = (bf16[2,1,16,16,128]{4,3,2,1,0:T(8,128)(2,1)}, bf16[2,1,16,16,128]{4,3,2,1,0:T(8,128)(2,1)}, u32[]{:S(2)}, u32[]{:S(2)}) collective-permute-start(bf16[2,1,16,16,128]{4,3,2,1,0:T(8,128)(2,1)} %get-tuple-element.589), channel_id=1, source_target_pairs={{0,1},{1,2},{2,3},{3,4},{4,5},{5,6},{6,7},{8,9},{9,10},{10,11},{11... | collective-permute-start | bytes 393224 | tf_op jit(solution)/shard_map/ppermute | solution.py:272
  320.1 42.5 %collective-permute-start.42 = (bf16[2,1,16,16,128]{4,3,2,1,0:T(8,128)(2,1)}, bf16[2,1,16,16,128]{4,3,2,1,0:T(8,128)(2,1)}, u32[]{:S(2)}, u32[]{:S(2)}) collective-permute-start(bf16[2,1,16,16,128]{4,3,2,1,0:T(8,128)(2,1)} %get-tuple-element.590), channel_id=1, source_target_pairs={{1,0},{2,1},{3,2},{4,3},{5,4},{6,5},{7,6},{9,8},{10,9},{11,10},{12... | collective-permute-start | bytes 393224 | tf_op jit(solution)/shard_map/ppermute | solution.py:273
  496.2 30.2 %all-to-all-start.5 = ((bf16[3,512,192]{2,0,1:T(4,128)(2,1)}), bf16[3,512,192]{2,0,1:T(4,128)(2,1)S(1)}, u32[]{:S(2)}, u32[]{:S(2)}) async-start(bf16[3,512,192]{2,0,1:T(4,128)(2,1)} %copy.742), calls=%async_computation.5 | async-start | bytes 2097152 | tf_op jit(solution)/shard_map/all_to_all | solution.py:352
  499.9 101.5 %reduce-scatter.7.cloned.1.call-start = ((), (), s32[]{:S(2)}) async-start(), calls=%async_computation.13 | async-start | bytes 2654208
  500.0 35.3 %collective-permute-start.58 = (bf16[4,4,24,768]{3,2,1,0:T(8,128)(2,1)}, bf16[4,4,24,768]{3,2,1,0:T(8,128)(2,1)}, u32[]{:S(2)}, u32[]{:S(2)}) collective-permute-start(bf16[4,4,24,768]{3,2,1,0:T(8,128)(2,1)} %get-tuple-element.547), channel_id=1, source_target_pairs={{0,8},{8,0},{16,24},{24,16},{1,9},{9,1},{17,25},{25,17},{2,10},{10... | collective-permute-start | bytes 1769480 | tf_op jit(solution)/shard_map/ppermute | solution.py:94
  501.2 34.1 %collective-permute-start.59 = (bf16[4,4,24,768]{3,2,1,0:T(8,128)(2,1)}, bf16[4,4,24,768]{3,2,1,0:T(8,128)(2,1)}, u32[]{:S(2)}, u32[]{:S(2)}) collective-permute-start(bf16[4,4,24,768]{3,2,1,0:T(8,128)(2,1)} %get-tuple-element.546), channel_id=1, source_target_pairs={{0,16},{8,24},{16,0},{24,8},{1,17},{9,25},{17,1},{25,9},{2,18},{10... | collective-permute-start | bytes 1769480 | tf_op jit(solution)/shard_map/ppermute | solution.py:94
  502.3 33.0 %collective-permute-start.60 = (bf16[4,4,24,768]{3,2,1,0:T(8,128)(2,1)}, bf16[4,4,24,768]{3,2,1,0:T(8,128)(2,1)}, u32[]{:S(2)}, u32[]{:S(2)}) collective-permute-start(bf16[4,4,24,768]{3,2,1,0:T(8,128)(2,1)} %get-tuple-element.545), channel_id=1, source_target_pairs={{0,24},{8,16},{16,8},{24,0},{1,25},{9,17},{17,9},{25,1},{2,26},{10... | collective-permute-start | bytes 1769480 | tf_op jit(solution)/shard_map/ppermute | solution.py:94
  535.3 136.5 %reduce-scatter.5.cloned.1.call-start = ((), (), s32[]{:S(2)}) async-start(), calls=%async_computation.11 | async-start | bytes 8847360 | tf_op jit(solution)/shard_map/reduce_scatter | solution.py:760
  583.7 33.4 %collective-permute-start.66 = (bf16[4,5,24,768]{3,2,1,0:T(8,128)(2,1)}, bf16[4,5,24,768]{3,2,1,0:T(8,128)(2,1)}, u32[]{:S(2)}, u32[]{:S(2)}) collective-permute-start(bf16[4,5,24,768]{3,2,1,0:T(8,128)(2,1)} %get-tuple-element.542), channel_id=1, source_target_pairs={{0,16},{8,24},{16,0},{24,8},{1,17},{9,25},{17,1},{25,9},{2,18},{10... | collective-permute-start | bytes 2211848 | tf_op jit(solution)/shard_map/ppermute | solution.py:94
  630.4 63.3 %collective-permute-start.74 = (bf16[128,4096]{1,0:T(8,128)(2,1)}, bf16[128,4096]{1,0:T(8,128)(2,1)S(1)}, u32[]{:S(2)}, u32[]{:S(2)}) collective-permute-start(bf16[128,4096]{1,0:T(8,128)(2,1)} %get-tuple-element.127), channel_id=1, source_target_pairs={{0,8},{8,0},{16,24},{24,16},{1,9},{9,1},{17,25},{25,17},{2,10},{10... | collective-permute-start | bytes 3145736 | tf_op jit(solution)/shard_map/ppermute | solution.py:94
  631.5 62.1 %collective-permute-start.75 = (bf16[128,4096]{1,0:T(8,128)(2,1)}, bf16[128,4096]{1,0:T(8,128)(2,1)S(1)}, u32[]{:S(2)}, u32[]{:S(2)}) collective-permute-start(bf16[128,4096]{1,0:T(8,128)(2,1)} %get-tuple-element.128), channel_id=1, source_target_pairs={{0,16},{8,24},{16,0},{24,8},{1,17},{9,25},{17,1},{25,9},{2,18},{10... | collective-permute-start | bytes 3145736 | tf_op jit(solution)/shard_map/ppermute | solution.py:94
  634.8 58.9 %collective-permute-start.76 = (bf16[128,4096]{1,0:T(8,128)(2,1)}, bf16[128,4096]{1,0:T(8,128)(2,1)}, u32[]{:S(2)}, u32[]{:S(2)}) collective-permute-start(bf16[128,4096]{1,0:T(8,128)(2,1)} %get-tuple-element.129), channel_id=1, source_target_pairs={{0,24},{8,16},{16,8},{24,0},{1,25},{9,17},{17,9},{25,1},{2,26},{10... | collective-permute-start | bytes 3145736 | tf_op jit(solution)/shard_map/ppermute | solution.py:94
  684.6 45.7 %all-to-all-start.6 = ((bf16[4,1014,192]{1,2,0:T(8,128)(2,1)}), bf16[4,1014,192]{1,2,0:T(8,128)(2,1)}, u32[]{:S(2)}, u32[]{:S(2)}) async-start(bf16[4,1014,192]{1,2,0:T(8,128)(2,1)} %concatenate.130), calls=%async_computation.7 | async-start | bytes 3145728 | tf_op jit(solution)/shard_map/all_to_all | solution.py:81
  (235 other events, 2328.1 us)
Sparse Core Ops, SparseCore 0:
  38.7 33.2 all-gather.6
  73.7 76.6 all-gather.4
  165.7 30.1 all-gather.8
  535.4 34.3 reduce-scatter.6
  571.9 99.8 reduce-scatter.4
